TPU v7x, 32 devices: a whole 2x2x4 slice. The times are simulated.
32 devices in a mesh: shard: 2 (over x), ctx: 4 (over z), tp: 4 (over y, core).
Axes of the slice: x: 2, y: 2, z: 4, core: 2. Of those that a mesh axis runs over, the one named last changes fastest.
Arguments:
- tokens: bfloat16 [1536, 1536], P(('shard', 'ctx')), may hold values from -6 to 6
- cotangent: bfloat16 [1536, 1536], P(('shard', 'ctx')), may hold values from -6 to 6
- valid_mask: int32 [1536], P(('shard', 'ctx')), may hold values 0 or 1
- lengths: int32 [2, 3], P('shard'), may hold values from 1 to 576, 768 in all within a row
- deal: int32 [2, 8], P('shard'), may hold values from 0 to 7, as said below
- attn_gain: bfloat16 [1536], replicated, may hold values from 0.5 to 1.5
- w_query: bfloat16 [1536, 1536], P(('shard', 'ctx'), 'tp'), may hold values from -0.15625 to 0.15625
- w_key: bfloat16 [1536, 1536], P(('shard', 'ctx'), 'tp'), may hold values from -0.15625 to 0.15625
- w_value: bfloat16 [1536, 1536], P(('shard', 'ctx'), 'tp'), may hold values from -0.15625 to 0.15625
- w_house: bfloat16 [1536, 1536], P(('shard', 'ctx'), 'tp'), may hold values from -0.15625 to 0.15625
- w_beta: bfloat16 [1536, 12], P(('shard', 'ctx'), 'tp'), may hold values from -0.15625 to 0.15625
- conv_taps: bfloat16 [4, 1536], P(None, 'tp'), may hold values from -3 to 3
- w_out: bfloat16 [1536, 1536], P('tp', ('shard', 'ctx')), may hold values from -0.625 to 0.625
- mlp_gain: bfloat16 [1536], replicated, may hold values from 0.5 to 1.5
- w_gate: bfloat16 [1536, 4096], P(('shard', 'ctx'), 'tp'), may hold values from -0.15625 to 0.15625
- w_up: bfloat16 [1536, 4096], P(('shard', 'ctx'), 'tp'), may hold values from -0.15625 to 0.15625
- w_down: bfloat16 [4096, 1536], P('tp', ('shard', 'ctx')), may hold values from -0.09375 to 0.09375
Outputs:
- output: bfloat16 [1536, 1536], P(('shard', 'ctx'))
- d_tokens: bfloat16 [1536, 1536], P(('shard', 'ctx'))
- d_attn_gain: float32 [1536], replicated
- d_query: float32 [1536, 1536], P(('shard', 'ctx'), 'tp')
- d_key: float32 [1536, 1536], P(('shard', 'ctx'), 'tp')
- d_value: float32 [1536, 1536], P(('shard', 'ctx'), 'tp')
- d_house: float32 [1536, 1536], P(('shard', 'ctx'), 'tp')
- d_beta: float32 [1536, 12], P(('shard', 'ctx'), 'tp')
- d_taps: float32 [4, 1536], P(None, 'tp')
- d_out: float32 [1536, 1536], P('tp', ('shard', 'ctx'))
- d_mlp_gain: float32 [1536], replicated
- d_gate: float32 [1536, 4096], P(('shard', 'ctx'), 'tp')
- d_up: float32 [1536, 4096], P(('shard', 'ctx'), 'tp')
- d_down: float32 [4096, 1536], P('tp', ('shard', 'ctx'))
- rms_stats: float32 [4], replicated
Inputs may be any that keep to these rules, and one draw needn't show every extreme that they name: `deal`: each row is a permutation of 0 .. 7; for every p, of the causal pieces p and 7 - p exactly one holds a given piece under 8 // 2. `lengths`: each row sums to 768.
All inputs are finite; a program needn't handle non-finite values. No bound on the sum of `valid_mask` on one device may be relied on, other than what follows from the above.
Results may differ from a plain program's by a relative error of at most 0.015.
Values may be sent and summed in bfloat16 or wider, within the bound.
No kernel may reach another device: no remote copies, remote signals or barrier semaphores. Data moves between devices by JAX's collectives and lax.ppermute only.
A program may use at most 256 MiB of HBM per device.

v0:
```python
import jax
import jax.numpy as jnp
from jax import lax
from jax.sharding import PartitionSpec as P

EPS = 1e-06
NEG = -1e30


def padded(cells, sides, width):
    for axis, dim in sides:
        count = lax.axis_size(axis)
        ends = count - 1
        head = lax.slice_in_dim(cells, 0, width, axis=dim)
        tail = lax.slice_in_dim(cells, cells.shape[dim] - width, cells.shape[dim], axis=dim)
        cells = jnp.concatenate(
            [
                lax.ppermute(tail, axis, [(i, (i + 1) % count) for i in range(ends)]),
                cells,
                lax.ppermute(head, axis, [((i + 1) % count, i) for i in range(ends)]),
            ],
            axis=dim,
        )
    return cells


def matmul(left, right):
    return jnp.dot(left, right, precision=lax.Precision.HIGHEST)


def bmatmul(left, right):
    return jnp.matmul(left, right, precision=lax.Precision.HIGHEST)


def rounded(value):
    return value + lax.stop_gradient(value.astype(jnp.bfloat16).astype(jnp.float32) - value)


def unit_lower_inverse(system):
    length = system.shape[-1]
    padded_len = 1 << max(length - 1, 0).bit_length()
    extra = padded_len - length
    system = jnp.pad(system, ((0, extra), (0, extra)))
    system = system + jnp.pad(jnp.eye(extra, dtype=system.dtype), ((length, 0), (length, 0)))
    blocks = jnp.ones((padded_len, 1, 1), system.dtype)
    size = 1
    while size < padded_len:
        count = padded_len // (2 * size)
        tiled = system.reshape(count, 2 * size, count, 2 * size)
        picker = jnp.eye(count, dtype=system.dtype)[:, None, :, None]
        diag_blocks = jnp.sum(tiled * picker, axis=2)
        lower_left = diag_blocks[:, size:, :size]
        upper_inv = blocks[0::2]
        lower_inv = blocks[1::2]
        corner = -bmatmul(bmatmul(lower_inv, lower_left), upper_inv)
        top = jnp.concatenate([upper_inv, jnp.zeros_like(upper_inv)], axis=2)
        bottom = jnp.concatenate([corner, lower_inv], axis=2)
        blocks = jnp.concatenate([top, bottom], axis=1)
        size = 2 * size
    return blocks[0][:length, :length]


def piece_parts(queries, key_rows, house_rows, beta_rows):
    length = queries.shape[0]
    row_ids = lax.broadcasted_iota(jnp.int32, (length, length), 0)
    col_ids = lax.broadcasted_iota(jnp.int32, (length, length), 1)
    identity = jnp.eye(length, dtype=queries.dtype)
    gram_rows = beta_rows[:, None] * matmul(house_rows, house_rows.T)
    lower_sys = identity + jnp.where(row_ids > col_ids, gram_rows, 0.0)
    upper_sys = identity + jnp.where(row_ids < col_ids, gram_rows, 0.0)
    lower_inv = unit_lower_inverse(lower_sys)
    upper_inv = jnp.flip(unit_lower_inverse(jnp.flip(upper_sys, (0, 1))), (0, 1))
    key_coef = matmul(
        lower_inv,
        beta_rows[:, None] * jnp.where(row_ids > col_ids, matmul(house_rows, key_rows.T), 0.0),
    )
    query_house = matmul(queries, house_rows.T)
    inner_scores = matmul(queries, key_rows.T) - matmul(
        jnp.where(row_ids >= col_ids, query_house, 0.0), key_coef
    )
    moved_keys = key_rows - matmul(key_coef.T, house_rows)
    query_coef = matmul(
        upper_inv, beta_rows[:, None] * jnp.where(row_ids <= col_ids, query_house.T, 0.0)
    )
    moved_queries = queries - matmul(query_coef.T, house_rows)
    through = matmul(lower_inv, beta_rows[:, None] * house_rows)
    transfer = jnp.eye(house_rows.shape[1], dtype=queries.dtype) - matmul(house_rows.T, through)
    return (inner_scores, moved_queries, moved_keys, transfer)


def finish(inner_scores, values, seg_own, cross_raw, usable, all_values, all_segs):
    length, width = values.shape
    piece_count = cross_raw.shape[0]
    score_scale = width ** (-0.5)
    row_ids = lax.broadcasted_iota(jnp.int32, (length, length), 0)
    col_ids = lax.broadcasted_iota(jnp.int32, (length, length), 1)
    own_logits = jnp.where(
        (row_ids >= col_ids) & (seg_own[:, None] == seg_own[None, :]),
        inner_scores * score_scale,
        NEG,
    )
    same_seq = seg_own[None, :, None] == all_segs[:, None, :]
    cross = jnp.where(usable[:, None, None] & same_seq, cross_raw, NEG)
    cross = cross.transpose(1, 0, 2).reshape(length, piece_count * length)
    row_max = jnp.maximum(jnp.max(own_logits, axis=1), jnp.max(cross, axis=1))
    own_exp = jnp.exp(own_logits - row_max[:, None])
    cross_exp = jnp.exp(cross - row_max[:, None])
    row_total = jnp.sum(own_exp, axis=1) + jnp.sum(cross_exp, axis=1)
    own_prob = rounded(own_exp / row_total[:, None])
    cross_prob = rounded(cross_exp / row_total[:, None])
    return matmul(own_prob, values) + matmul(
        cross_prob, all_values.reshape(piece_count * length, width)
    )


def norm_back(value, inverse, gain, grad):
    scaled = grad * gain
    return inverse * scaled - value * inverse**3 * jnp.mean(scaled * value, axis=1, keepdims=True)


def local(
    tokens,
    cotangent,
    valid_mask,
    lengths,
    deal,
    attn_gain,
    w_query,
    w_key,
    w_value,
    w_house,
    w_beta,
    conv_taps,
    w_out,
    mlp_gain,
    w_gate,
    w_up,
    w_down,
):
    ctx_size = lax.axis_size("ctx")
    ctx_index = lax.axis_index("ctx")
    span, width = tokens.shape
    piece = span // 2
    pieces = 2 * ctx_size
    heads = w_beta.shape[1]
    columns = w_query.shape[1]
    head_width = columns // heads
    taps_count = conv_taps.shape[0]
    margin = taps_count - 1
    deal_row = deal[0]
    labels = jnp.arange(pieces, dtype=jnp.int32)
    placed_at = jnp.sum(jnp.where(deal_row[:, None] == labels[None, :], labels[:, None], 0), axis=0)
    own_ids = jnp.stack([ctx_index, pieces - 1 - ctx_index])
    is_last = ctx_index == ctx_size - 1
    ident = placed_at[2 * ctx_index + jnp.arange(2, dtype=jnp.int32)]
    targets = jnp.minimum(ident, pieces - 1 - ident)
    sources = deal_row[own_ids] // 2
    devices = jnp.arange(ctx_size, dtype=jnp.int32)

    def spread(data, where_to):
        picked = where_to[None, :] == devices[:, None]
        picked = picked.reshape(picked.shape + (1,) * (data.ndim - 1))
        return jnp.sum(jnp.where(picked, data[None], jnp.zeros((), data.dtype)), axis=1)

    outgoing = (
        spread(tokens.reshape(2, piece, width), targets),
        spread(cotangent.reshape(2, piece, width), targets),
        spread(valid_mask.reshape(2, piece).astype(jnp.bfloat16), targets),
    )
    got_tokens, got_grads, got_mask = (
        lax.all_to_all(outgoing[0], "ctx", split_axis=0, concat_axis=0, tiled=True),
        lax.all_to_all(outgoing[1], "ctx", split_axis=0, concat_axis=0, tiled=True),
        lax.all_to_all(outgoing[2], "ctx", split_axis=0, concat_axis=0, tiled=True),
    )
    x_rows = jnp.take(got_tokens, sources, axis=0).reshape(span, width).astype(jnp.float32)
    grad_rows = jnp.take(got_grads, sources, axis=0).reshape(span, width)
    mask_rows = jnp.take(got_mask, sources, axis=0).reshape(span).astype(jnp.float32)
    seq_ends = jnp.cumsum(lengths[0])[:-1]

    def segment_of(positions):
        return jnp.sum((positions[..., None] >= seq_ends).astype(jnp.int32), axis=-1)

    offsets = jnp.arange(piece, dtype=jnp.int32)
    own_seg = segment_of(own_ids[:, None] * piece + offsets[None, :])
    all_seg = segment_of(labels[:, None] * piece + offsets[None, :])
    prior = own_ids[:, None] * piece - margin + jnp.arange(margin, dtype=jnp.int32)[None, :]
    prior_seg = jnp.where(prior >= 0, segment_of(prior), -1)
    shared = (w_query, w_key, w_value, w_house, w_beta, w_out, w_gate, w_up, w_down)
    wq_full, wk_full, wv_full, wh_full, wb_full, wo_full, wg_full, wu_full, wd_full = (
        lax.all_gather(shared[0], ("shard", "ctx"), axis=0, tiled=True),
        lax.all_gather(shared[1], ("shard", "ctx"), axis=0, tiled=True),
        lax.all_gather(shared[2], ("shard", "ctx"), axis=0, tiled=True),
        lax.all_gather(shared[3], ("shard", "ctx"), axis=0, tiled=True),
        lax.all_gather(shared[4], ("shard", "ctx"), axis=0, tiled=True),
        lax.all_gather(shared[5], ("shard", "ctx"), axis=1, tiled=True),
        lax.all_gather(shared[6], ("shard", "ctx"), axis=0, tiled=True),
        lax.all_gather(shared[7], ("shard", "ctx"), axis=0, tiled=True),
        lax.all_gather(shared[8], ("shard", "ctx"), axis=1, tiled=True),
    )
    gain_one = attn_gain.astype(jnp.float32)
    inv_one = lax.rsqrt(jnp.mean(x_rows * x_rows, axis=1, keepdims=True) + EPS)
    normed_one = (x_rows * inv_one * gain_one).astype(jnp.bfloat16)

    def project(weight):
        return jnp.dot(normed_one, weight, preferred_element_type=jnp.float32)

    queries = project(wq_full).astype(jnp.bfloat16)
    key_rows = project(wk_full).astype(jnp.bfloat16)
    value_rows = project(wv_full).astype(jnp.bfloat16)
    raw_house = project(wh_full)
    beta_gate = jax.nn.sigmoid(project(wb_full))
    beta_rows = 2.0 * beta_gate
    raw_pieces = raw_house.reshape(2, piece, columns)
    own_tails = raw_pieces[:, piece - margin :]
    beside_all = padded(jnp.stack([own_tails[1], own_tails[0]]), (("ctx", 0),), 1)
    prev_tails = jnp.stack([beside_all[0], jnp.where(is_last, own_tails[0], beside_all[3])])
    tap_values = conv_taps.astype(jnp.float32)

    def house_of(raw_in, tails_in, taps_in):
        extended = jnp.concatenate([tails_in, raw_in], axis=1)
        ext_seg = jnp.concatenate([prior_seg, own_seg], axis=1)
        mixed = taps_in[0] * raw_in
        for offset in range(1, taps_count):
            begin_at = margin - offset
            earlier = extended[:, begin_at : begin_at + piece]
            same_seq = ext_seg[:, begin_at : begin_at + piece] == own_seg
            mixed = mixed + taps_in[offset] * jnp.where(same_seq[..., None], earlier, 0.0)
        mixed = mixed.reshape(2, piece, heads, head_width)
        return mixed * lax.rsqrt(jnp.sum(mixed * mixed, axis=-1, keepdims=True) + EPS)

    unit_rows, house_back = jax.vjp(house_of, raw_pieces, prev_tails, tap_values)
    house_rows = lax.optimization_barrier(unit_rows.astype(jnp.bfloat16)).astype(jnp.float32)

    def heads_of(value):
        return value.reshape(2, piece, heads, head_width).transpose(0, 2, 1, 3)

    def rows_of(value):
        return value.transpose(0, 2, 1, 3).reshape(span, columns)

    q_heads = heads_of(queries.astype(jnp.float32))
    k_heads = heads_of(key_rows.astype(jnp.float32))
    v_heads = heads_of(value_rows.astype(jnp.float32))
    w_heads = house_rows.transpose(0, 2, 1, 3)
    b_heads = beta_rows.reshape(2, piece, heads).transpose(0, 2, 1)

    def parts_of(q_in, k_in, w_in, b_in):
        return jax.vmap(jax.vmap(piece_parts))(q_in, k_in, w_in, b_in)

    (inner_scores, moved_q, moved_k, transfer), parts_back = jax.vjp(
        parts_of, q_heads, k_heads, w_heads, b_heads
    )
    far_keys, far_values, far_transfer = (
        lax.all_gather(moved_k, "ctx", axis=0, tiled=True),
        lax.all_gather(v_heads, "ctx", axis=0, tiled=True),
        lax.all_gather(transfer, "ctx", axis=0, tiled=True),
    )

    def to_causal(value):
        paired = value.reshape((ctx_size, 2) + value.shape[1:])
        return jnp.concatenate([paired[:, 0], jnp.flip(paired[:, 1], 0)], axis=0).swapaxes(0, 1)

    def to_slots(value):
        value = value.swapaxes(0, 1)
        return jnp.stack([value[:ctx_size], jnp.flip(value[ctx_size:], 0)], axis=1).reshape(
            (pieces,) + value.shape[1:]
        )

    first_id = own_ids[0]
    second_id = own_ids[1]
    step_count = pieces - 1

    def pair_head(head_item):
        inner_two, moved_two, values_two, keys_causal, values_causal, transfer_causal = head_item
        score_scale = head_width ** (-0.5)

        def advance(carry, step):
            current_a, current_b = carry
            on_first = step < first_id
            key_piece = jnp.where(on_first, first_id - 1 - step, pieces - 2 - step)
            current = jnp.where(on_first, current_a, current_b)
            scores = matmul(current, keys_causal[key_piece].T) * score_scale
            moved = matmul(current, transfer_causal[key_piece])
            return (
                (jnp.where(on_first, moved, current_a), jnp.where(on_first, current_b, moved)),
                scores,
            )

        step_ids = jnp.arange(step_count, dtype=jnp.int32)
        unused, step_scores = lax.scan(advance, (moved_two[0], moved_two[1]), step_ids)
        cross_first = jnp.take(
            step_scores, jnp.clip(first_id - 1 - labels, 0, step_count - 1), axis=0
        )
        cross_second = jnp.take(
            step_scores, jnp.clip(pieces - 2 - labels, 0, step_count - 1), axis=0
        )
        out_first = finish(
            inner_two[0],
            values_two[0],
            own_seg[0],
            cross_first,
            labels < first_id,
            values_causal,
            all_seg,
        )
        out_second = finish(
            inner_two[1],
            values_two[1],
            own_seg[1],
            cross_second,
            labels < second_id,
            values_causal,
            all_seg,
        )
        return jnp.stack([out_first, out_second])

    def attend_all(inner_in, moved_in, values_in, keys_far, values_far, transfer_far):

        def flip_lead(value):
            return value.swapaxes(0, 1)

        result = lax.map(
            jax.checkpoint(pair_head),
            (
                flip_lead(inner_in),
                flip_lead(moved_in),
                flip_lead(values_in),
                keys_far,
                values_far,
                transfer_far,
            ),
        )
        return flip_lead(result)

    attended, attend_back = jax.vjp(
        attend_all,
        inner_scores,
        moved_q,
        v_heads,
        to_causal(far_keys),
        to_causal(far_values),
        to_causal(far_transfer),
    )
    attended_b = rows_of(attended).astype(jnp.bfloat16)
    attn_rows = lax.psum(jnp.dot(attended_b, wo_full, preferred_element_type=jnp.float32), "tp")
    middle = x_rows + attn_rows
    gain_two = mlp_gain.astype(jnp.float32)
    inv_two = lax.rsqrt(jnp.mean(middle * middle, axis=1, keepdims=True) + EPS)
    normed_two = (middle * inv_two * gain_two).astype(jnp.bfloat16)
    gate_rows = jnp.dot(normed_two, wg_full, preferred_element_type=jnp.float32)
    up_rows = jnp.dot(normed_two, wu_full, preferred_element_type=jnp.float32)
    gate_sig = jax.nn.sigmoid(gate_rows)
    swish = gate_rows * gate_sig
    act_rows = (swish * up_rows).astype(jnp.bfloat16)
    mlp_rows = lax.psum(jnp.dot(act_rows, wd_full, preferred_element_type=jnp.float32), "tp")
    result_rows = middle + mlp_rows
    totals = jnp.stack(
        [
            jnp.sum(mask_rows * jnp.sum(branch * branch, axis=1))
            for branch in (x_rows, attn_rows, mlp_rows, result_rows)
        ]
        + [jnp.sum(mask_rows)]
    )
    wq_full, wk_full, wv_full, wh_full, wb_full, wo_full, wg_full, wu_full, wd_full = (
        lax.all_gather(shared[0], ("shard", "ctx"), axis=0, tiled=True),
        lax.all_gather(shared[1], ("shard", "ctx"), axis=0, tiled=True),
        lax.all_gather(shared[2], ("shard", "ctx"), axis=0, tiled=True),
        lax.all_gather(shared[3], ("shard", "ctx"), axis=0, tiled=True),
        lax.all_gather(shared[4], ("shard", "ctx"), axis=0, tiled=True),
        lax.all_gather(shared[5], ("shard", "ctx"), axis=1, tiled=True),
        lax.all_gather(shared[6], ("shard", "ctx"), axis=0, tiled=True),
        lax.all_gather(shared[7], ("shard", "ctx"), axis=0, tiled=True),
        lax.all_gather(shared[8], ("shard", "ctx"), axis=1, tiled=True),
    )
    d_wdown = jnp.dot(act_rows.T, grad_rows, preferred_element_type=jnp.float32)
    d_act = jnp.dot(grad_rows, wd_full.T, preferred_element_type=jnp.float32)
    d_gate_b = (d_act * up_rows * gate_sig * (1.0 + gate_rows * (1.0 - gate_sig))).astype(
        jnp.bfloat16
    )
    d_up_b = (d_act * swish).astype(jnp.bfloat16)
    d_wgate = jnp.dot(normed_two.T, d_gate_b, preferred_element_type=jnp.float32)
    d_wup = jnp.dot(normed_two.T, d_up_b, preferred_element_type=jnp.float32)
    d_two = lax.psum(
        jnp.dot(d_gate_b, wg_full.T, preferred_element_type=jnp.float32)
        + jnp.dot(d_up_b, wu_full.T, preferred_element_type=jnp.float32),
        "tp",
    )
    d_gain_two = jnp.sum(d_two * middle * inv_two, axis=0)
    d_middle = grad_rows.astype(jnp.float32) + norm_back(middle, inv_two, gain_two, d_two)
    d_attn_b = d_middle.astype(jnp.bfloat16)
    d_wout = jnp.dot(attended_b.T, d_attn_b, preferred_element_type=jnp.float32)
    d_attended = heads_of(
        jnp.dot(d_attn_b, wo_full.T, preferred_element_type=jnp.float32)
        .astype(jnp.bfloat16)
        .astype(jnp.float32)
    )
    d_inner, d_moved, d_vown, d_far_keys, d_far_values, d_far_transfer = attend_back(d_attended)
    back_keys, back_values, back_transfer = (
        lax.psum_scatter(to_slots(d_far_keys), "ctx", scatter_dimension=0, tiled=True),
        lax.psum_scatter(to_slots(d_far_values), "ctx", scatter_dimension=0, tiled=True),
        lax.psum_scatter(to_slots(d_far_transfer), "ctx", scatter_dimension=0, tiled=True),
    )
    d_qh, d_kh, d_wh, d_bh = parts_back((d_inner, d_moved, back_keys, back_transfer))
    d_queries = rows_of(d_qh).astype(jnp.bfloat16)
    d_keys = rows_of(d_kh).astype(jnp.bfloat16)
    d_values = rows_of(d_vown + back_values).astype(jnp.bfloat16)
    d_logit = (
        d_bh.transpose(0, 2, 1).reshape(span, heads) * 2.0 * beta_gate * (1.0 - beta_gate)
    ).astype(jnp.bfloat16)
    d_raw, d_tails, d_taps = house_back(d_wh.transpose(0, 2, 1, 3))
    around_back = padded(d_tails, (("ctx", 0),), 1)
    tail_back = jnp.stack([around_back[3] + jnp.where(is_last, d_tails[1], 0.0), around_back[0]])
    d_raw = d_raw.at[:, piece - margin :].add(tail_back)
    d_raw_b = d_raw.reshape(span, columns).astype(jnp.bfloat16)

    def weight_grad(grad):
        return jnp.dot(normed_one.T, grad, preferred_element_type=jnp.float32)

    d_wq = weight_grad(d_queries)
    d_wk = weight_grad(d_keys)
    d_wv = weight_grad(d_values)
    d_wh = weight_grad(d_raw_b)
    d_wb = weight_grad(d_logit)
    d_one = lax.psum(
        jnp.dot(d_queries, wq_full.T, preferred_element_type=jnp.float32)
        + jnp.dot(d_keys, wk_full.T, preferred_element_type=jnp.float32)
        + jnp.dot(d_values, wv_full.T, preferred_element_type=jnp.float32)
        + jnp.dot(d_raw_b, wh_full.T, preferred_element_type=jnp.float32)
        + jnp.dot(d_logit, wb_full.T, preferred_element_type=jnp.float32),
        "tp",
    )
    d_gain_one = jnp.sum(d_one * x_rows * inv_one, axis=0)
    d_input = d_middle + norm_back(x_rows, inv_one, gain_one, d_one)
    returning = (
        spread(result_rows.astype(jnp.bfloat16).reshape(2, piece, width), sources),
        spread(d_input.astype(jnp.bfloat16).reshape(2, piece, width), sources),
    )
    got_output, got_dinput = (
        lax.all_to_all(returning[0], "ctx", split_axis=0, concat_axis=0, tiled=True),
        lax.all_to_all(returning[1], "ctx", split_axis=0, concat_axis=0, tiled=True),
    )
    output_given = jnp.take(got_output, targets, axis=0).reshape(span, width)
    dinput_given = jnp.take(got_dinput, targets, axis=0).reshape(span, width)
    gathered_grads = (
        lax.psum_scatter(d_wq, ("shard", "ctx"), scatter_dimension=0, tiled=True),
        lax.psum_scatter(d_wk, ("shard", "ctx"), scatter_dimension=0, tiled=True),
        lax.psum_scatter(d_wv, ("shard", "ctx"), scatter_dimension=0, tiled=True),
        lax.psum_scatter(d_wh, ("shard", "ctx"), scatter_dimension=0, tiled=True),
        lax.psum_scatter(d_wb, ("shard", "ctx"), scatter_dimension=0, tiled=True),
        lax.psum_scatter(d_wout, ("shard", "ctx"), scatter_dimension=1, tiled=True),
        lax.psum_scatter(d_wgate, ("shard", "ctx"), scatter_dimension=0, tiled=True),
        lax.psum_scatter(d_wup, ("shard", "ctx"), scatter_dimension=0, tiled=True),
        lax.psum_scatter(d_wdown, ("shard", "ctx"), scatter_dimension=1, tiled=True),
    )
    small = lax.psum((d_gain_one, d_gain_two, d_taps, totals), ("shard", "ctx"))
    sums_all = small[3]
    rms_stats = jnp.sqrt(sums_all[:4] / (jnp.maximum(sums_all[4], 1.0) * width))
    return (
        output_given,
        dinput_given,
        small[0],
        gathered_grads[0],
        gathered_grads[1],
        gathered_grads[2],
        gathered_grads[3],
        gathered_grads[4],
        small[2],
        gathered_grads[5],
        small[1],
        gathered_grads[6],
        gathered_grads[7],
        gathered_grads[8],
        rms_stats,
    )


def solution(mesh):
    placed = (
        P(("shard", "ctx"), None),
        P(("shard", "ctx"), None),
        P(("shard", "ctx")),
        P("shard", None),
        P("shard", None),
        P(),
        P(("shard", "ctx"), "tp"),
        P(("shard", "ctx"), "tp"),
        P(("shard", "ctx"), "tp"),
        P(("shard", "ctx"), "tp"),
        P(("shard", "ctx"), "tp"),
        P(None, "tp"),
        P("tp", ("shard", "ctx")),
        P(),
        P(("shard", "ctx"), "tp"),
        P(("shard", "ctx"), "tp"),
        P("tp", ("shard", "ctx")),
    )
    return jax.shard_map(
        local,
        mesh=mesh,
        in_specs=placed,
        out_specs=(
            P(("shard", "ctx"), None),
            P(("shard", "ctx"), None),
            P(),
            P(("shard", "ctx"), "tp"),
            P(("shard", "ctx"), "tp"),
            P(("shard", "ctx"), "tp"),
            P(("shard", "ctx"), "tp"),
            P(("shard", "ctx"), "tp"),
            P(None, "tp"),
            P("tp", ("shard", "ctx")),
            P(),
            P(("shard", "ctx"), "tp"),
            P(("shard", "ctx"), "tp"),
            P("tp", ("shard", "ctx")),
            P(),
        ),
        check_vma=False,
    )
```

profile of v0, /device:TPU:0, one launch (start us, length us, event | category | flops | bytes accessed | tf_op | source)
XLA Modules:
  0.0 3068.5 jit_solution(5489049846067693130)
XLA Ops:
  29.6 37.1 %all-to-all-done = bf16[4,96,1536]{2,1,0:T(8,128)(2,1)S(1)} async-done(((bf16[4,96,1536]{2,1,0:T(8,128)(2,1)}), bf16[4,96,1536]{2,1,0:T(8,128)(2,1)S(1)}, u32[]{:S(2)}, u32[]{:S(2)}) %all-to-all-start) | async-done | bytes 1179680 | tf_op jit(solution)/shard_map/all_to_all | solution.py:171
  72.5 50.6 %all-gather = bf16[8,192,3]{1,2,0:T(4,128)(2,1)S(1)} all-gather(bf16[1,192,3]{1,2,0:T(4,128)(2,1)S(1)} %bitcast.1249), channel_id=1, replica_groups=mesh['shard'=2,'ctx'=4,'tp'=4] {'shard','ctx'}, dimensions={0}, use_global_device_ids=true | all-gather | bytes 10368 | tf_op jit(solution)/shard_map/all_gather | solution.py:194
  144.9 17.2 all-gather.15.cloned.1.call-done
  170.8 26.5 reshape.1534
  197.3 14.3 reshape.1535
  211.8 26.5 reshape.1528
  238.3 14.3 reshape.1529
  274.3 18.5 multiply_reduce_fusion.4
  347.8 36.0 %while.190 = (s32[]{:T(128)}, pred[7]{0:T(512)(128)(4,1)}, s32[7]{0:T(128)}, s32[7]{0:T(128)S(1)}, s32[]{:T(128)}, /*index=5*/s32[]{:T(128)}, s32[]{:T(128)}, s32[]{:T(128)}, s32[]{:T(128)}, s32[]{:T(128)}) while((s32[]{:T(128)}, pred[7]{0:T(512)(128)(4,1)}, s32[7]{0:T(128)}, s32[7]{0:T(128)S(1)}, s32[]{:T(128)}, /*index=5*/s32[]{:T(128)}, ...), condition=%wide.region_20.22_spmd, body=%wide.region_19.21_spmd.sunk | while | flops 9 | bytes 219 | solution.py:289
  421.8 153.8 %while.195 = (s32[]{:T(128)}, bf16[3,2,96,128]{3,2,1,0:T(8,128)(2,1)}, f32[3,2,96,96]{3,2,0,1:T(8,128)}, f32[3,2,96,128]{3,2,1,0:T(8,128)}, f32[3,8,96,128]{3,2,...) while((s32[]{:T(128)}, ...), condition=%wide.region_33.35_spmd.clone.clone.clone, body=%wide.region_22.34_spmd.clone.clone.clone.sunk | while | flops 291562304 | bytes 11778353 | solution.py:321
  425.9 38.7 %while.198 = (s32[]{:T(128)}, f32[96,128]{1,0:T(8,128)S(1)}, f32[96,128]{1,0:T(8,128)S(1)}, f32[7,96,96]{2,1,0:T(8,128)S(1)}, pred[7]{0:T(512)(128)(4,1)}, /*ind...) while((s32[]{:T(128)}, f32[96,128]{1,0:T(8,128)S(1)}, ...), condition=%wide.region_25.26_spmd, body=%wide.region_24.25_spmd.sunk | while | flops 33088512 | bytes 755328 | solution.py:289
  477.1 38.7 %while.198 = (s32[]{:T(128)}, f32[96,128]{1,0:T(8,128)S(1)}, f32[96,128]{1,0:T(8,128)S(1)}, f32[7,96,96]{2,1,0:T(8,128)S(1)}, pred[7]{0:T(512)(128)(4,1)}, /*ind...) while((s32[]{:T(128)}, f32[96,128]{1,0:T(8,128)S(1)}, ...), condition=%wide.region_25.26_spmd, body=%wide.region_24.25_spmd.sunk | while | flops 33088512 | bytes 755328 | solution.py:289
  528.4 38.7 %while.198 = (s32[]{:T(128)}, f32[96,128]{1,0:T(8,128)S(1)}, f32[96,128]{1,0:T(8,128)S(1)}, f32[7,96,96]{2,1,0:T(8,128)S(1)}, pred[7]{0:T(512)(128)(4,1)}, /*ind...) while((s32[]{:T(128)}, f32[96,128]{1,0:T(8,128)S(1)}, ...), condition=%wide.region_25.26_spmd, body=%wide.region_24.25_spmd.sunk | while | flops 33088512 | bytes 755328 | solution.py:289
  581.8 34.2 %all-reduce.76.cloned.1.call-done = f32[192,1536]{1,0:T(8,128)} async-done(((f32[192,1536]{1,0:T(8,128)}), f32[192,1536]{1,0:T(8,128)}) %all-reduce.76.cloned.1.call-update) | async-done | bytes 1179664 | tf_op jit(solution)/shard_map/psum | solution.py:344
  618.3 60.2 %all-gather.29.cloned.1.call-done = bf16[1536,1024]{1,0:T(8,128)(2,1)} async-done(((bf16[192,1024]{1,0:T(8,128)(2,1)}), bf16[1536,1024]{1,0:T(8,128)(2,1)}) %all-gather.29.cloned.1.call-update) | async-done | bytes 3145744 | tf_op jit(solution)/shard_map/all_gather | solution.py:196
  682.1 57.7 %all-gather.33.cloned.1.call-done = bf16[1024,1536]{0,1:T(8,128)(2,1)} async-done(((bf16[1024,192]{0,1:T(8,128)(2,1)}), bf16[1024,1536]{0,1:T(8,128)(2,1)}) %all-gather.33.cloned.1.call-update) | async-done | bytes 3145744 | tf_op jit(solution)/shard_map/all_gather | solution.py:198
  743.3 57.5 %all-gather.31.cloned.1.call-done = bf16[1536,1024]{1,0:T(8,128)(2,1)} async-done(((bf16[192,1024]{1,0:T(8,128)(2,1)}), bf16[1536,1024]{1,0:T(8,128)(2,1)}) %all-gather.31.cloned.1.call-update) | async-done | bytes 3145744 | tf_op jit(solution)/shard_map/all_gather | solution.py:197
  831.0 34.8 %all-reduce.80.cloned.1.call-done = (f32[192,1536]{1,0:T(8,128)}, f32[192,1536]{1,0:T(8,128)}) async-done(((f32[192,1536]{1,0:T(8,128)}, f32[192,1536]{1,0:T(8,128)}), (f32[192,1536]{1,0:T(8,128)}, f32[192,1536]{1,0:T(8,128)})) %all-reduce.80.cloned.1.call-update) | async-done | bytes 2359312 | tf_op jit(solution)/shard_map/psum | solution.py:382
  878.1 356.5 %while.193 = (s32[]{:T(128)}, f32[3,2,96,96]{2,3,1,0:T(8,128)}, f32[3,2,96,128]{3,2,1,0:T(8,128)}, f32[3,2,96,128]{3,2,0,1:T(8,128)}, f32[3,8,96,128]{3,2,1,0:T(...) while((s32[]{:T(128)}, f32[3,2,96,96]{2,3,1,0:T(8,128)}, ...), condition=%wide.region_68.71_spmd.clone, body=%wide.region_41.70_spmd.clone.sunk | while | flops 615480704 | bytes 31726716 | solution.py:321
  885.0 34.3 %while.196 = (s32[]{:T(128)}, f32[96,128]{1,0:T(8,128)S(1)}, f32[96,128]{1,0:T(8,128)S(1)}, f32[7,96,96]{2,1,0:T(8,128)S(1)}, pred[7]{0:T(512)(128)(4,1)S(1)}, /...) while((s32[]{:T(128)}, f32[96,128]{1,0:T(8,128)S(1)}, ...), condition=%wide.region_44.45_spmd, body=%wide.region_43.44_spmd.sunk | while | flops 33076232 | bytes 919348 | solution.py:289
  929.4 62.3 %while.197 = (s32[]{:T(128)}, f32[8,96,128]{2,1,0:T(8,128)S(1)}, f32[8,128,128]{2,1,0:T(8,128)S(1)}, f32[96,128]{1,0:T(8,128)S(1)}, f32[96,128]{1,0:T(8,128)S(1)...) while((s32[]{:T(128)}, f32[8,96,128]{2,1,0:T(8,128)S(1)}, ...), condition=%wide.region_67.69_spmd.clone, body=%wide.region_66.68_spmd.clone.sunk | while | flops 66340868 | bytes 1053886 | solution.py:289
  1003.8 34.3 %while.196 = (s32[]{:T(128)}, f32[96,128]{1,0:T(8,128)S(1)}, f32[96,128]{1,0:T(8,128)S(1)}, f32[7,96,96]{2,1,0:T(8,128)S(1)}, pred[7]{0:T(512)(128)(4,1)S(1)}, /...) while((s32[]{:T(128)}, f32[96,128]{1,0:T(8,128)S(1)}, ...), condition=%wide.region_44.45_spmd, body=%wide.region_43.44_spmd.sunk | while | flops 33076232 | bytes 919348 | solution.py:289
  1048.1 62.3 %while.197 = (s32[]{:T(128)}, f32[8,96,128]{2,1,0:T(8,128)S(1)}, f32[8,128,128]{2,1,0:T(8,128)S(1)}, f32[96,128]{1,0:T(8,128)S(1)}, f32[96,128]{1,0:T(8,128)S(1)...) while((s32[]{:T(128)}, f32[8,96,128]{2,1,0:T(8,128)S(1)}, ...), condition=%wide.region_67.69_spmd.clone, body=%wide.region_66.68_spmd.clone.sunk | while | flops 66340868 | bytes 1053886 | solution.py:289
  1122.5 34.3 %while.196 = (s32[]{:T(128)}, f32[96,128]{1,0:T(8,128)S(1)}, f32[96,128]{1,0:T(8,128)S(1)}, f32[7,96,96]{2,1,0:T(8,128)S(1)}, pred[7]{0:T(512)(128)(4,1)S(1)}, /...) while((s32[]{:T(128)}, f32[96,128]{1,0:T(8,128)S(1)}, ...), condition=%wide.region_44.45_spmd, body=%wide.region_43.44_spmd.sunk | while | flops 33076232 | bytes 919348 | solution.py:289
  1166.8 62.3 %while.197 = (s32[]{:T(128)}, f32[8,96,128]{2,1,0:T(8,128)S(1)}, f32[8,128,128]{2,1,0:T(8,128)S(1)}, f32[96,128]{1,0:T(8,128)S(1)}, f32[96,128]{1,0:T(8,128)S(1)...) while((s32[]{:T(128)}, f32[8,96,128]{2,1,0:T(8,128)S(1)}, ...), condition=%wide.region_67.69_spmd.clone, body=%wide.region_66.68_spmd.clone.sunk | while | flops 66340868 | bytes 1053886 | solution.py:289
  1321.4 91.2 %pad.251 = f32[2,3,4,32,32]{2,4,3,1,0:T(8,128)} pad(f32[2,3,2,32,32]{2,4,3,1,0:T(8,128)} %get-tuple-element.2061, f32[]{:T(128)} %constant.504.clone.1), padding=0_0_0x0_0_0x0_1_1x0_0_0x0_0_0 | pad | bytes 147460 | tf_op jit(solution)/shard_map/transpose(jvp(vmap(vmap())))/pad | solution.py:53
  1412.6 91.3 %pad.250 = f32[2,3,4,32,32]{2,4,3,1,0:T(8,128)} pad(f32[2,3,2,32,32]{2,4,3,1,0:T(8,128)} %get-tuple-element.2060, f32[]{:T(128)} %constant.504.clone.1), padding=0_0_0x0_0_0x1_0_1x0_0_0x0_0_0 | pad | bytes 147460 | tf_op jit(solution)/shard_map/transpose(jvp(vmap(vmap())))/pad | solution.py:54
  1514.2 37.0 %pad.254 = f32[2,3,8,16,16]{2,4,3,1,0:T(8,128)S(1)} pad(f32[2,3,4,16,16]{2,4,3,1,0:T(8,128)} %add_add_fusion.5, f32[]{:T(128)} %constant.504.clone.1), padding=0_0_0x0_0_0x0_1_1x0_0_0x0_0_0 | pad | bytes 73732 | tf_op jit(solution)/shard_map/transpose(jvp(vmap(vmap())))/pad | solution.py:53
  1551.3 33.3 %pad.253 = f32[2,3,8,16,16]{2,4,3,1,0:T(8,128)} pad(f32[2,3,4,16,16]{2,4,3,1,0:T(8,128)S(1)} %get-tuple-element.2064, f32[]{:T(128)} %constant.504.clone.1), padding=0_0_0x0_0_0x1_0_1x0_0_0x0_0_0 | pad | bytes 73732 | tf_op jit(solution)/shard_map/transpose(jvp(vmap(vmap())))/pad | solution.py:54
  1651.5 18.5 broadcast_in_dim.798
  1760.4 14.4 add_any.481
  1802.6 91.2 %pad.272 = f32[2,3,4,32,32]{2,4,3,1,0:T(8,128)} pad(f32[2,3,2,32,32]{2,4,3,1,0:T(8,128)} %get-tuple-element.2063, f32[]{:T(128)} %constant.504.clone.1), padding=0_0_0x0_0_0x0_1_1x0_0_0x0_0_0 | pad | bytes 147460 | tf_op jit(solution)/shard_map/transpose(jvp(vmap(vmap())))/pad | solution.py:53
  1893.7 91.3 %pad.271 = f32[2,3,4,32,32]{2,4,3,1,0:T(8,128)} pad(f32[2,3,2,32,32]{2,4,3,1,0:T(8,128)} %get-tuple-element.2062, f32[]{:T(128)} %constant.504.clone.1), padding=0_0_0x0_0_0x1_0_1x0_0_0x0_0_0 | pad | bytes 147460 | tf_op jit(solution)/shard_map/transpose(jvp(vmap(vmap())))/pad | solution.py:54
  1993.4 33.1 %pad.275 = f32[2,3,8,16,16]{2,4,3,1,0:T(8,128)} pad(f32[2,3,4,16,16]{2,4,3,1,0:T(8,128)S(1)} %add_add_fusion.4, f32[]{:T(128)} %constant.504.clone.1), padding=0_0_0x0_0_0x0_1_1x0_0_0x0_0_0 | pad | bytes 73732 | tf_op jit(solution)/shard_map/transpose(jvp(vmap(vmap())))/pad | solution.py:53
  2026.4 33.2 %pad.274 = f32[2,3,8,16,16]{2,4,3,1,0:T(8,128)} pad(f32[2,3,4,16,16]{2,4,3,1,0:T(8,128)S(1)} %get-tuple-element.2067, f32[]{:T(128)} %constant.504.clone.1), padding=0_0_0x0_0_0x1_0_1x0_0_0x0_0_0 | pad | bytes 73732 | tf_op jit(solution)/shard_map/transpose(jvp(vmap(vmap())))/pad | solution.py:54
  2073.0 16.8 pad.277
  2135.6 18.3 broadcast_in_dim.815
  2259.9 39.0 %all_to_all.32 = bf16[4,96,1536]{2,1,0:T(8,128)(2,1)S(1)} all-to-all(bf16[4,96,1536]{2,1,0:T(8,128)(2,1)S(1)} %get-tuple-element.1830), channel_id=1, replica_groups=mesh['shard'=2,'ctx'=4,'tp'=4] {'ctx'}, dimensions={0} | all-to-all | bytes 2359296 | tf_op jit(solution)/shard_map/all_to_all | solution.py:439
  2306.6 24.9 reduce-scatter.37.cloned.1.call-done
  2333.1 40.2 %all-reduce.70 = (f32[1536]{0:T(1024)}, f32[4,384]{1,0:T(4,128)}, f32[1536]{0:T(1024)}, f32[5]{0:T(128)S(1)}) all-reduce(f32[1536]{0:T(1024)S(1)} %get-tuple-element.1803, f32[4,384]{1,0:T(4,128)S(1)} %pad_add_fusion.7, f32[1536]{0:T(1024)S(1)} %copy-done.272, ...), channel_id=1, replica_groups=mesh['shard'=2,'ctx'=4,'tp'=4] {'shard','ctx'}, use_global_device_ids=true, to_apply=%region_81.84 | all-reduce | flops 4613 | bytes 36904 | tf_op jit(solution)/shard_map/psum | solution.py:454
  2377.5 29.7 reduce-scatter.21.cloned.1.call-done
  2407.1 72.3 %reduce-scatter.29.cloned.1.call-done = f32[384,192]{0,1:T(8,128)} async-done(((f32[384,1536]{0,1:T(8,128)}), f32[384,192]{0,1:T(8,128)}) %reduce-scatter.29.cloned.1.call-update) | async-done | bytes 294928 | tf_op jit(solution)/shard_map/reduce_scatter | solution.py:449
  2479.5 72.6 %reduce-scatter.23.cloned.1.call-done = f32[192,384]{1,0:T(8,128)} async-done(((f32[1536,384]{1,0:T(8,128)}), f32[192,384]{1,0:T(8,128)}) %reduce-scatter.23.cloned.1.call-update) | async-done | bytes 294928 | tf_op jit(solution)/shard_map/reduce_scatter | solution.py:445
  2552.1 72.5 %reduce-scatter.25.cloned.1.call-done = f32[192,384]{1,0:T(8,128)} async-done(((f32[1536,384]{1,0:T(8,128)}), f32[192,384]{1,0:T(8,128)}) %reduce-scatter.25.cloned.1.call-update) | async-done | bytes 294928 | tf_op jit(solution)/shard_map/reduce_scatter | solution.py:446
  2624.5 72.6 %reduce-scatter.27.cloned.1.call-done = f32[192,384]{1,0:T(8,128)} async-done(((f32[1536,384]{1,0:T(8,128)}), f32[192,384]{1,0:T(8,128)}) %reduce-scatter.27.cloned.1.call-update) | async-done | bytes 294928 | tf_op jit(solution)/shard_map/reduce_scatter | solution.py:447
  2697.1 121.5 %reduce-scatter.31.cloned.1.call-done = f32[192,1024]{1,0:T(8,128)} async-done(((f32[1536,1024]{1,0:T(8,128)}), f32[192,1024]{1,0:T(8,128)}) %reduce-scatter.31.cloned.1.call-update) | async-done | bytes 786448 | tf_op jit(solution)/shard_map/reduce_scatter | solution.py:450
  2818.6 121.7 %reduce-scatter.33.cloned.1.call-done = f32[192,1024]{1,0:T(8,128)} async-done(((f32[1536,1024]{1,0:T(8,128)}), f32[192,1024]{1,0:T(8,128)}) %reduce-scatter.33.cloned.1.call-update) | async-done | bytes 786448 | tf_op jit(solution)/shard_map/reduce_scatter | solution.py:451
  2940.2 121.6 %reduce-scatter.35.cloned.1.call-done = f32[1024,192]{0,1:T(8,128)} async-done(((f32[1024,1536]{0,1:T(8,128)}), f32[1024,192]{0,1:T(8,128)}) %reduce-scatter.35.cloned.1.call-update) | async-done | bytes 786448 | tf_op jit(solution)/shard_map/reduce_scatter | solution.py:452
  (2037 shorter events, 1186.3 us)
Async XLA Ops:
  7.2 128.1 %all-gather.17.cloned.1.call-start = ((), (), s32[]{:S(2)}) async-start(), calls=%async_computation.19 | async-start | bytes 1327104 | tf_op jit(solution)/shard_map/all_gather | solution.py:193
  7.9 130.7 %all-gather.23.cloned.1.call-start = ((), (), s32[]{:S(2)}) async-start(), calls=%async_computation.22 | async-start | bytes 1327104 | tf_op jit(solution)/shard_map/all_gather | solution.py:192
  8.7 153.5 %all-gather.15.cloned.1.call-start = ((), (), s32[]{:S(2)}) async-start(), calls=%async_computation.18 | async-start | bytes 1327104 | tf_op jit(solution)/shard_map/all_gather | solution.py:191
  12.3 11.8 all-to-all-start.4
  18.7 365.3 %all-gather.13.cloned.1.call-start = ((), (), s32[]{:S(2)}) async-start(), calls=%async_computation.17 | async-start | bytes 1327104 | tf_op jit(solution)/shard_map/all_gather | solution.py:190
  24.1 42.6 %all-to-all-start = ((bf16[4,96,1536]{2,1,0:T(8,128)(2,1)}), bf16[4,96,1536]{2,1,0:T(8,128)(2,1)S(1)}, u32[]{:S(2)}, u32[]{:S(2)}) async-start(bf16[4,96,1536]{2,1,0:T(8,128)(2,1)} %get-tuple-element.1833), calls=%async_computation | async-start | bytes 2359296 | tf_op jit(solution)/shard_map/all_to_all | solution.py:171
  29.2 37.5 %copy-start.303 = (s32[2]{0:T(128)}, s32[2]{0:T(128)S(1)}, u32[]{:S(2)}) copy-start(s32[2]{0:T(128)S(1)} %slice_bitcast_fusion.17) | copy-start | bytes 28
  29.4 98.2 %copy-start.262 = (s32[2,96]{1,0:T(2,128)}, s32[2,96]{1,0:T(2,128)S(1)}, u32[]{:S(2)}) copy-start(s32[2,96]{1,0:T(2,128)S(1)} %fusion.376) | copy-start | bytes 2308
  29.5 94.9 %copy-start.319 = (s32[2]{0:T(128)}, s32[2]{0:T(128)S(1)}, u32[]{:S(2)}) copy-start(s32[2]{0:T(128)S(1)} %get-tuple-element.2018) | copy-start | bytes 28
  29.5 100.3 %copy-start.294 = (pred[2]{0:T(512)(128)(4,1)}, pred[2]{0:T(512)(128)(4,1)S(1)}, u32[]{:S(2)}) copy-start(pred[2]{0:T(512)(128)(4,1)S(1)} %get-tuple-element.2017) | copy-start | bytes 10
  66.7 63.5 %all-to-all-start.2 = ((bf16[4,96,1536]{2,1,0:T(8,128)(2,1)}), bf16[4,96,1536]{2,1,0:T(8,128)(2,1)S(1)}, u32[]{:S(2)}, u32[]{:S(2)}) async-start(bf16[4,96,1536]{2,1,0:T(8,128)(2,1)} %get-tuple-element.1832), calls=%async_computation.2 | async-start | bytes 2359296 | tf_op jit(solution)/shard_map/all_to_all | solution.py:172
  70.4 341.3 %all-gather.25.cloned.1.call-start = ((), (), s32[]{:S(2)}) async-start(), calls=%async_computation.23 | async-start | bytes 1474560 | tf_op jit(solution)/shard_map/all_gather | solution.py:254
  131.9 484.1 %copy-start.5 = (f32[2,96,1536]{2,1,0:T(8,128)}, f32[2,96,1536]{2,1,0:T(8,128)S(1)}, u32[]{:S(2)}) copy-start(f32[2,96,1536]{2,1,0:T(8,128)S(1)} %get-tuple-element.2163) | copy-start | bytes 3538948
  133.5 250.5 %copy-start.7 = (bf16[192,1536]{1,0:T(8,128)(2,1)}, bf16[192,1536]{1,0:T(8,128)(2,1)S(1)}, u32[]{:S(2)}) copy-start(bf16[192,1536]{1,0:T(8,128)(2,1)S(1)} %multiply_convert_fusion.2) | copy-start | bytes 1769476
  137.3 5.5 collective-permute-start.1
  142.8 22.9 collective-permute-start
  165.7 248.6 %all-gather.19.cloned.1.call-start = ((), (), s32[]{:S(2)}) async-start(), calls=%async_computation.20 | async-start | bytes 1474560 | tf_op jit(solution)/shard_map/all_gather | solution.py:253
  342.0 68.4 %copy-start.26 = (f32[2,3,96,96]{3,2,1,0:T(8,128)}, f32[2,3,96,96]{3,2,1,0:T(8,128)S(1)}, u32[]{:S(2)}) copy-start(f32[2,3,96,96]{3,2,1,0:T(8,128)S(1)} %fusion.251) | copy-start | bytes 663556
  343.1 73.8 %all-gather.21.cloned.1.call-start = ((), (), s32[]{:S(2)}) async-start(), calls=%async_computation.21 | async-start | bytes 1966080 | tf_op jit(solution)/shard_map/all_gather | solution.py:255
  343.2 40.6 %copy-start.304 = (s32[2]{0:T(128)S(1)}, s32[2]{0:T(128)}, u32[]{:S(2)}) copy-start(s32[2]{0:T(128)} %copy-done.303) | copy-start | bytes 28
  344.4 39.3 %copy-start.95 = (f32[2,3,96,128]{3,2,1,0:T(8,128)}, f32[2,3,96,128]{3,2,1,0:T(8,128)S(1)}, u32[]{:S(2)}) copy-start(f32[2,3,96,128]{3,2,1,0:T(8,128)S(1)} %fusion.208) | copy-start | bytes 884740
  345.6 231.1 %all-gather.27.cloned.1.call-start = ((), (), s32[]{:S(2)}) async-start(), calls=%async_computation.24 | async-start | bytes 1327104 | tf_op jit(solution)/shard_map/all_gather | solution.py:195
  346.3 269.6 %all-reduce.76.cloned.1.call-start = ((), (), s32[]{:S(2)}) async-start(), calls=%async_computation.25 | async-start | bytes 2359296 | tf_op jit(solution)/shard_map/psum | solution.py:344
  347.1 63.2 %copy-start.241 = (pred[96,96]{0,1:T(8,128)(4,1)}, pred[96,96]{0,1:T(8,128)(4,1)S(1)}, u32[]{:S(2)}) copy-start(pred[96,96]{0,1:T(8,128)(4,1)S(1)} %iota_compare_fusion.16) | copy-start | bytes 27652
  579.7 98.8 %all-gather.29.cloned.1.call-start = ((), (), s32[]{:S(2)}) async-start(), calls=%async_computation.26 | async-start | bytes 3538944 | tf_op jit(solution)/shard_map/all_gather | solution.py:196
  580.3 159.5 %all-gather.33.cloned.1.call-start = ((), (), s32[]{:S(2)}) async-start(), calls=%async_computation.28 | async-start | bytes 3538944 | tf_op jit(solution)/shard_map/all_gather | solution.py:198
  581.0 219.8 %all-gather.31.cloned.1.call-start = ((), (), s32[]{:S(2)}) async-start(), calls=%async_computation.27 | async-start | bytes 3538944 | tf_op jit(solution)/shard_map/all_gather | solution.py:197
  581.6 284.2 %all-reduce.80.cloned.1.call-start = ((), (), s32[]{:S(2)}) async-start(), calls=%async_computation.42 | async-start | bytes 4718592 | tf_op jit(solution)/shard_map/psum | solution.py:382
  618.3 182.5 %copy-start.13 = (bf16[192,1536]{1,0:T(8,128)(2,1)}, bf16[192,1536]{1,0:T(8,128)(2,1)S(1)}, u32[]{:S(2)}) copy-start(bf16[192,1536]{1,0:T(8,128)(2,1)S(1)} %multiply_convert_fusion) | copy-start | bytes 1769476
  618.3 121.4 %copy-start.22 = (bf16[2,96,1536]{2,1,0:T(8,128)(2,1)S(1)}, bf16[2,96,1536]{2,1,0:T(8,128)(2,1)}, u32[]{:S(2)}) copy-start(bf16[2,96,1536]{2,1,0:T(8,128)(2,1)} %get-tuple-element.2162) | copy-start | bytes 1769476
  811.2 893.4 %reduce-scatter.15.cloned.1.call-start = ((), (), s32[]{:S(2)}) async-start(), calls=%async_computation.29 | async-start | bytes 1474560 | tf_op jit(solution)/shard_map/reduce_scatter | solution.py:398
  878.1 358.0 %copy-start.244 = (pred[96,96]{0,1:T(8,128)(4,1)S(1)}, pred[96,96]{0,1:T(8,128)(4,1)}, u32[]{:S(2)}) copy-start(pred[96,96]{0,1:T(8,128)(4,1)} %iota_compare_fusion.12) | copy-start | bytes 27652
  1551.3 34.5 %copy-start.51 = (f32[2,3,16,8,8]{4,3,2,1,0:T(8,128)S(1)}, f32[2,3,16,8,8]{4,3,2,1,0:T(8,128)}, u32[]{:S(2)}) copy-start(f32[2,3,16,8,8]{4,3,2,1,0:T(8,128)} %copy-done.50) | copy-start | bytes 73732
  1589.8 121.3 %reduce-scatter.17.cloned.1.call-start = ((), (), s32[]{:S(2)}) async-start(), calls=%async_computation.30 | async-start | bytes 1474560 | tf_op jit(solution)/shard_map/reduce_scatter | solution.py:399
  1619.9 96.0 %reduce-scatter.19.cloned.1.call-start = ((), (), s32[]{:S(2)}) async-start(), calls=%async_computation.31 | async-start | bytes 1966080 | tf_op jit(solution)/shard_map/reduce_scatter | solution.py:400
  1630.6 624.0 %all-reduce.78.cloned.1.call-start = ((), (), s32[]{:S(2)}) async-start(), calls=%async_computation.32 | async-start | bytes 2359296 | tf_op jit(solution)/shard_map/psum | solution.py:423
  2201.8 5.5 collective-permute-start.2
  2207.3 4.8 collective-permute-start.3
  2217.3 114.3 %reduce-scatter.37.cloned.1.call-start = ((), (), s32[]{:S(2)}) async-start(), calls=%async_computation.41 | async-start | bytes 884736
  2219.7 187.5 %reduce-scatter.21.cloned.1.call-start = ((), (), s32[]{:S(2)}) async-start(), calls=%async_computation.33 | async-start | bytes 2654208 | tf_op jit(solution)/shard_map/reduce_scatter | solution.py:444
  2221.8 257.7 %reduce-scatter.29.cloned.1.call-start = ((), (), s32[]{:S(2)}) async-start(), calls=%async_computation.37 | async-start | bytes 2654208 | tf_op jit(solution)/shard_map/reduce_scatter | solution.py:449
  2225.4 326.7 %reduce-scatter.23.cloned.1.call-start = ((), (), s32[]{:S(2)}) async-start(), calls=%async_computation.34 | async-start | bytes 2654208 | tf_op jit(solution)/shard_map/reduce_scatter | solution.py:445
  2228.3 396.2 %reduce-scatter.25.cloned.1.call-start = ((), (), s32[]{:S(2)}) async-start(), calls=%async_computation.35 | async-start | bytes 2654208 | tf_op jit(solution)/shard_map/reduce_scatter | solution.py:446
  2231.3 465.8 %reduce-scatter.27.cloned.1.call-start = ((), (), s32[]{:S(2)}) async-start(), calls=%async_computation.36 | async-start | bytes 2654208 | tf_op jit(solution)/shard_map/reduce_scatter | solution.py:447
  2233.3 585.2 %reduce-scatter.31.cloned.1.call-start = ((), (), s32[]{:S(2)}) async-start(), calls=%async_computation.38 | async-start | bytes 7077888 | tf_op jit(solution)/shard_map/reduce_scatter | solution.py:450
  2238.2 702.1 %reduce-scatter.33.cloned.1.call-start = ((), (), s32[]{:S(2)}) async-start(), calls=%async_computation.39 | async-start | bytes 7077888 | tf_op jit(solution)/shard_map/reduce_scatter | solution.py:451
  2242.8 819.0 %reduce-scatter.35.cloned.1.call-start = ((), (), s32[]{:S(2)}) async-start(), calls=%async_computation.40 | async-start | bytes 7077888 | tf_op jit(solution)/shard_map/reduce_scatter | solution.py:452
  2299.0 76.7 %all-to-all-start.1 = ((bf16[4,96,1536]{2,1,0:T(8,128)(2,1)}), bf16[4,96,1536]{2,1,0:T(8,128)(2,1)S(1)}, u32[]{:S(2)}, u32[]{:S(2)}) async-start(bf16[4,96,1536]{2,1,0:T(8,128)(2,1)} %get-tuple-element.1831), calls=%async_computation.1 | async-start | bytes 2359296 | tf_op jit(solution)/shard_map/all_to_all | solution.py:438
  (319 other events, 1282.4 us)
Sparse Core Ops, SparseCore 0:
  10.1 55.9 all-gather.16
  68.2 51.9 all-gather.22
  122.4 39.7 all-gather.14
  164.1 39.8 all-gather.12
  205.4 29.2 all-gather.24
  343.2 29.1 all-gather.18
  374.6 36.2 all-gather.20
  413.0 40.0 all-gather.26
  579.8 36.1 all-reduce.75
  617.9 60.5 all-gather.28
  680.6 59.0 all-gather.32
  741.7 59.0 all-gather.30
  811.3 54.4 all-reduce.79
  1589.9 29.3 reduce-scatter.14
  1621.5 27.8 reduce-scatter.16
  1651.6 33.9 reduce-scatter.18
  2217.4 37.1 all-reduce.77
  2257.8 73.7 reduce-scatter.36
  2336.0 71.0 reduce-scatter.20
  2411.5 67.9 reduce-scatter.28
  2483.9 68.0 reduce-scatter.22
  2556.5 67.9 reduce-scatter.24
  2629.0 68.0 reduce-scatter.26
  2701.5 116.9 reduce-scatter.30
  2823.1 117.0 reduce-scatter.32
  2944.7 117.0 reduce-scatter.34
where the time goes:
time: 3120 us; the launch traced here: 3070 us
  local copies, waits for them, and re-layouts  1170 us (38%)
  waiting for transfers between devices  1030 us (33%)
  matrix products  407 us (13%)
  other arithmetic  231 us (7%)
  blocking collectives  130 us (4%)
  loops' own time  54.6 us (2%)
    dot_general x237, matrix products, matmul(): return jnp.dot(left, right, precision=lax.Precision.HIGHEST)  289 us
    pad x8, local copies, waits for them, and re-layouts, unit_lower_inverse(): lower_inv = blocks[1::2]  275 us
    pad x8, local copies, waits for them, and re-layouts, unit_lower_inverse(): upper_inv = blocks[0::2]  264 us
    broadcast_in_dim x24, local copies, waits for them, and re-layouts, unit_lower_inverse(): diag_blocks = jnp.sum(tiled * picker, axis=2)  122 us
    reduce_scatter x1, waiting for transfers between devices, local(): lax.psum_scatter(d_wup, ('shard', 'ctx'), scatter_dimension=0, tiled=True)  122 us
    reduce_scatter x1, waiting for transfers between devices, local(): lax.psum_scatter(d_wdown, ('shard', 'ctx'), scatter_dimension=1, tiled=True)  122 us
    reduce_scatter x1, waiting for transfers between devices, local(): lax.psum_scatter(d_wgate, ('shard', 'ctx'), scatter_dimension=0, tiled=True)  121 us
    reshape x12, local copies, waits for them, and re-layouts, unit_lower_inverse(): tiled = system.reshape(count, 2 * size, count, 2 * size)  103 us
  transfers between devices with their start and end apart: 34, of which 21 were waited for; matrix products, arithmetic and copies ran while one was open for 20% of the time, Pallas kernels for 0%

commit v1 on v0

v1 whole, which is shorter than its diff:
```python
import functools

import jax
import jax.numpy as jnp
from jax import lax
from jax.experimental import pallas as pl
from jax.experimental.pallas import tpu as pltpu
from jax.sharding import PartitionSpec as P

EPS = 1e-06
NEG = -1e30
BF = jnp.bfloat16
F32 = jnp.float32
CHUNK = 128


def dg(left, right, cl, cr):
    return lax.dot_general(left, right, (((cl,), (cr,)), ((), ())), preferred_element_type=F32)


def halves(value):
    high = value.astype(BF)
    return high, (value - high.astype(F32)).astype(BF)


def joined(pairs, cl=1, cr=0):
    lefts, rights = [], []
    for left, right in pairs:
        if left.dtype == BF and right.dtype == BF:
            lefts += [left]
            rights += [right]
        elif left.dtype == BF:
            lefts += [left, left]
            rights += halves(right)
        elif right.dtype == BF:
            lefts += halves(left)
            rights += [right, right]
        else:
            lh, ll = halves(left)
            rh, rl = halves(right)
            lefts += [lh, lh, ll]
            rights += [rh, rl, rh]
    return dg(jnp.concatenate(lefts, axis=cl), jnp.concatenate(rights, axis=cr), cl, cr)


def mm(left, right, cl=1, cr=0):
    return joined([(left, right)], cl, cr)


def ml(left, right, cl=1, cr=0):
    return dg(left.astype(BF), right.astype(BF), cl, cr)


def seg_at(position, ends):
    seg = (position >= ends[0]).astype(jnp.int32)
    for end in ends[1:]:
        seg = seg + (position >= end).astype(jnp.int32)
    return seg


def seq_ends(len_ref):
    ends = [len_ref[0, 0]]
    for index in range(1, len_ref.shape[1] - 1):
        ends.append(ends[-1] + len_ref[0, index])
    return ends


def shifted_mask(rows, width, shift, ends):
    here = lax.broadcasted_iota(jnp.int32, (rows, width), 0)
    back = here - shift
    return (back >= 0) & (seg_at(here, ends) == seg_at(back, ends))


def tile_iota():
    row = lax.broadcasted_iota(jnp.int32, (CHUNK, CHUNK), 0)
    col = lax.broadcasted_iota(jnp.int32, (CHUNK, CHUNK), 1)
    return row, col


def forward_kernel(
    deal_ref, found_ref, len_ref, x_ref, gain_ref, w_ref, wb_ref, taps_ref,
    o_ref, h1_ref, q_ref, k_ref, v_ref, house_ref, raw_ref, logit_ref, prob_ref,
    u_ref, kt_ref, tr_ref, tinv_ref, xq_ref, yk_ref, z_ref,
    proj_ref, score_ref,
):
    rows = x_ref.shape[0]
    pieces = deal_ref.shape[1]
    piece = rows // pieces
    chunks = rows // CHUNK
    width = o_ref.shape[1]
    scale = width ** (-0.5)
    ends = seq_ends(len_ref)
    gain = gain_ref[...].astype(F32)

    def project(step, carry):
        base = pl.multiple_of(step * piece, piece)
        here = pl.multiple_of(found_ref[0, step] * piece, piece)
        x = x_ref[pl.ds(here, piece), :].astype(F32)
        inv = lax.rsqrt(jnp.mean(x * x, axis=1, keepdims=True) + EPS)
        h1 = (x * inv * gain).astype(BF)
        h1_ref[pl.ds(base, piece), :] = h1
        proj_ref[pl.ds(base, piece), :] = dg(h1, w_ref[...], 1, 0)
        logit_ref[pl.ds(base, piece), :] = dg(h1, wb_ref[...], 1, 0)
        return carry

    lax.fori_loop(0, pieces, project, 0)
    q_ref[...] = proj_ref[:, :width].astype(BF)
    k_ref[...] = proj_ref[:, width:2 * width].astype(BF)
    v_ref[...] = proj_ref[:, 2 * width:3 * width].astype(BF)
    raw = proj_ref[:, 3 * width:4 * width]
    raw_ref[...] = raw
    taps = taps_ref[...].astype(F32)
    mixed = taps[0:1, :] * raw
    for shift in range(1, taps.shape[0]):
        moved = pltpu.roll(raw, shift, 0)
        mixed = mixed + taps[shift:shift + 1, :] * jnp.where(
            shifted_mask(rows, width, shift, ends), moved, 0.0
        )
    unit = mixed * lax.rsqrt(jnp.sum(mixed * mixed, axis=1, keepdims=True) + EPS)
    house_ref[...] = unit.astype(BF)

    row, col = tile_iota()
    strict = row > col
    eye = jnp.where(row == col, 1.0, 0.0)
    spans = [slice(n * CHUNK, (n + 1) * CHUNK) for n in range(chunks)]
    strength = [2.0 * jax.nn.sigmoid(logit_ref[s, 0:1]) for s in spans]
    system = []
    for n, s in enumerate(spans):
        house = house_ref[s, :]
        system.append(jnp.where(strict, strength[n] * dg(house, house, 1, 1), 0.0))
    inverse = [eye - jnp.where((row ^ col) == 1, a, 0.0) for a in system]
    level = 1
    while (1 << level) < CHUNK:
        block = ((row ^ col) >> level) == 1
        inner = [mm(jnp.where(block, a, 0.0), t) for a, t in zip(system, inverse)]
        inverse = [t - mm(t, i) for t, i in zip(inverse, inner)]
        level += 1
    for n, s in enumerate(spans):
        query, key, house = q_ref[s, :], k_ref[s, :], house_ref[s, :]
        tinv = inverse[n]
        tinv_ref[s, :] = tinv
        across = jnp.transpose(jnp.broadcast_to(strength[n], (CHUNK, CHUNK)))
        merged = tinv * across
        a_qw = jnp.where(row >= col, dg(query, house, 1, 1), 0.0)
        a_wk = jnp.where(strict, dg(house, key, 1, 1), 0.0)
        xq = mm(a_qw, merged)
        yk = mm(merged, a_wk)
        zz = mm(merged, house)
        xq_ref[s, :] = xq
        yk_ref[s, :] = yk
        z_ref[s, :] = zz
        score_ref[s, s] = (dg(query, key, 1, 1) - mm(xq, a_wk)) * scale
        proj_ref[s, :width] = query.astype(F32) - mm(xq, house)
        kt_ref[s, :] = key.astype(F32) - mm(yk, house, 0, 0)
        tr_ref[s, :] = eye - mm(house, zz, 0, 0)
    offset = 0
    for n in range(chunks - 2, -1, -1):
        later = slice((n + 1) * CHUNK, rows)
        count = rows - (n + 1) * CHUNK
        carried = proj_ref[later, :width]
        u_ref[offset:offset + count, :] = carried
        offset += count
        score_ref[later, spans[n]] = mm(carried, kt_ref[spans[n], :], 1, 1) * scale
        if n > 0:
            proj_ref[later, :width] = mm(carried, tr_ref[spans[n], :])
    for m, s in enumerate(spans):
        reach = (m + 1) * CHUNK
        at_row = lax.broadcasted_iota(jnp.int32, (CHUNK, reach), 0) + m * CHUNK
        at_col = lax.broadcasted_iota(jnp.int32, (CHUNK, reach), 1)
        keep = (at_row >= at_col) & (seg_at(at_row, ends) == seg_at(at_col, ends))
        logits = jnp.where(keep, score_ref[s, :reach], NEG)
        top = jnp.max(logits, axis=1, keepdims=True)
        grown = jnp.exp(logits - top)
        prob = grown / jnp.sum(grown, axis=1, keepdims=True)
        prob_ref[s, :reach] = prob
        proj_ref[s, :width] = dg(prob.astype(BF), v_ref[:reach, :], 1, 0)

    def give(step, carry):
        base = pl.multiple_of(step * piece, piece)
        given = pl.multiple_of(deal_ref[0, step] * piece, piece)
        o_ref[pl.ds(given, piece), :] = proj_ref[pl.ds(base, piece), :width].astype(BF)
        return carry

    lax.fori_loop(0, pieces, give, 0)


def backward_kernel(
    deal_ref, place_ref, len_ref, live_ref, do_ref, h1_ref, w_ref, wb_ref, taps_ref,
    q_ref, k_ref, v_ref, house_ref, raw_ref, logit_ref, prob_ref,
    u_ref, kt_ref, tr_ref, tinv_ref, xq_ref, yk_ref, z_ref,
    dh1_ref, dw_ref, db_ref, dtaps_ref,
    ds_ref, dout_ref, du_ref, dkt_ref, dtr_ref, dhouse_ref, dproj_ref,
):
    rows = do_ref.shape[0]
    pieces = deal_ref.shape[1]
    piece = rows // pieces
    small = rows // place_ref.shape[1]
    chunks = rows // CHUNK
    width = do_ref.shape[1]
    scale = width ** (-0.5)
    ends = seq_ends(len_ref)
    spans = [slice(n * CHUNK, (n + 1) * CHUNK) for n in range(chunks)]
    row, col = tile_iota()
    strict = row > col

    def take(step, carry):
        base = pl.multiple_of(step * piece, piece)
        given = pl.multiple_of(deal_ref[0, step] * piece, piece)
        dout_ref[pl.ds(base, piece), :] = do_ref[pl.ds(given, piece), :]
        return carry

    lax.fori_loop(0, pieces, take, 0)
    for m, s in enumerate(spans):
        reach = (m + 1) * CHUNK
        prob = prob_ref[s, :reach]
        dprob = dg(dout_ref[s, :], v_ref[:reach, :], 1, 1)
        dot = jnp.sum(prob * dprob, axis=1, keepdims=True)
        ds_ref[s, :reach] = prob * (dprob - dot) * scale
    for n, s in enumerate(spans):
        dproj_ref[s, 2 * width:3 * width] = dg(
            prob_ref[n * CHUNK:, s].astype(BF), dout_ref[n * CHUNK:, :], 0, 0
        ).astype(BF)
    starts = {}
    offset = 0
    for n in range(chunks - 2, -1, -1):
        starts[n] = offset
        offset += rows - (n + 1) * CHUNK
    for n in range(chunks - 1):
        later = slice((n + 1) * CHUNK, rows)
        count = rows - (n + 1) * CHUNK
        grad = ds_ref[later, spans[n]]
        carried = u_ref[starts[n]:starts[n] + count, :]
        dkt_ref[spans[n], :] = mm(grad, carried, 0, 0)
        fresh = mm(grad, kt_ref[spans[n], :])
        if n > 0:
            before = du_ref[later, :]
            dtr_ref[spans[n], :] = mm(carried, before, 0, 0)
            fresh = fresh + mm(before, tr_ref[spans[n], :], 1, 1)
        du_ref[later, :] = fresh
    for n, s in enumerate(spans):
        query, key, house = q_ref[s, :], k_ref[s, :], house_ref[s, :]
        strength = 2.0 * jax.nn.sigmoid(logit_ref[s, 0:1])
        tinv = tinv_ref[s, :]
        merged = tinv * jnp.transpose(jnp.broadcast_to(strength, (CHUNK, CHUNK)))
        a_qw = jnp.where(row >= col, dg(query, house, 1, 1), 0.0)
        a_wk = jnp.where(strict, dg(house, key, 1, 1), 0.0)
        gram = jnp.where(strict, dg(house, house, 1, 1), 0.0)
        xq, yk, zz = xq_ref[s, :], yk_ref[s, :], z_ref[s, :]
        di = ds_ref[s, s]
        first, final = n == 0, n == chunks - 1
        if first:
            dxq = mm(di, a_wk, 1, 1)
            da_qw = mm(di, yk, 1, 1)
        else:
            dqt = du_ref[s, :]
            dxq = joined([(di, a_wk), (dqt, house)], 1, 1)
            da_qw = joined([(di, yk), (dqt, zz)], 1, 1)
        da_qw = jnp.where(row >= col, da_qw, 0.0)
        dm = mm(a_qw, dxq, 0, 0)
        cross = [(xq, di)]
        if not final:
            dkt = dkt_ref[s, :]
            dyk = mm(house, dkt, 1, 1)
            cross.append((merged, dyk))
            outer = [(dyk, a_wk)]
            if not first:
                dtr = dtr_ref[s, :]
                wd = mm(house, dtr)
                outer.append((wd, house))
            dm = dm + joined(outer, 1, 1)
        da_wk = jnp.where(strict, joined(cross, 0, 0), 0.0)
        ee = mm(tinv, dm, 0, 0)
        rest = jnp.where(row == col, 1.0, 0.0) - mm(gram, merged)
        dstrength = -jnp.sum(ee * rest, axis=1, keepdims=True)
        dgram = jnp.where(strict, mm(strength * ee, merged, 1, 1), 0.0)
        dq = joined([(di, key), (-da_qw, house)])
        dk = joined([(di, query), (-da_wk, house)], 0, 0)
        tall = [(da_qw, query), (-dgram, house)]
        wide = [(da_wk, key), (-dgram, house)]
        if not first:
            dq = dq + dqt
            tall.append((xq, dqt))
        if not final:
            dk = dk + dkt
            wide.append((yk, dkt))
            if not first:
                tall.append((merged, wd))
        dw = joined(tall, 0, 0) + joined(wide)
        if not first and not final:
            dw = dw + mm(zz, dtr, 1, 1)
        dw = -dw
        dproj_ref[s, :width] = dq.astype(BF)
        dproj_ref[s, width:2 * width] = dk.astype(BF)
        dhouse_ref[s, :] = dw
        gate = 0.5 * strength
        dlogit = dstrength * 2.0 * gate * (1.0 - gate)
        lane = lax.broadcasted_iota(jnp.int32, (CHUNK, width), 1)
        dproj_ref[s, 4 * width:] = jnp.where(lane == 0, dlogit, 0.0).astype(BF)
    raw = raw_ref[...]
    taps = taps_ref[...].astype(F32)
    count = taps.shape[0]
    mixed = taps[0:1, :] * raw
    earlier = [raw]
    masks = [None]
    for shift in range(1, count):
        masks.append(shifted_mask(rows, width, shift, ends))
        earlier.append(jnp.where(masks[shift], pltpu.roll(raw, shift, 0), 0.0))
        mixed = mixed + taps[shift:shift + 1, :] * earlier[shift]
    inv = lax.rsqrt(jnp.sum(mixed * mixed, axis=1, keepdims=True) + EPS)
    dunit = dhouse_ref[...]
    dmixed = inv * dunit - mixed * (
        inv * inv * inv * jnp.sum(dunit * mixed, axis=1, keepdims=True)
    )
    live = live_ref[0, 0].astype(F32)
    draw = taps[0:1, :] * dmixed
    dtaps_ref[0:1, :] = jnp.sum(dmixed * raw, axis=0, keepdims=True) * live
    for shift in range(1, count):
        dtaps_ref[shift:shift + 1, :] = (
            jnp.sum(dmixed * earlier[shift], axis=0, keepdims=True) * live
        )
        later = jnp.where(masks[shift], dmixed, 0.0)
        draw = draw + taps[shift:shift + 1, :] * pltpu.roll(later, rows - shift, 0)
    dproj_ref[:, 3 * width:4 * width] = draw.astype(BF)

    def send(step, carry):
        base = pl.multiple_of(step * piece, piece)
        grads = dproj_ref[pl.ds(base, piece), :]
        dh1 = dg(grads[:, :4 * width], w_ref[...], 1, 1) + dg(grads[:, 4 * width:], wb_ref[...], 1, 1)
        dh1 = (dh1 * live).astype(dh1_ref.dtype)
        for part in range(piece // small):
            there = place_ref[0, deal_ref[0, step] * (piece // small) + part]
            dh1_ref[pl.ds(pl.multiple_of(there * small, small), small), :] = dh1[
                part * small:(part + 1) * small
            ]
        return carry

    lax.fori_loop(0, pieces, send, 0)
    depth = h1_ref.shape[1]
    block = 256

    def weigh(step, carry):
        base = pl.multiple_of(step * block, block)
        got = dg(h1_ref[:, pl.ds(base, block)], dproj_ref[...], 0, 0) * live
        dw_ref[pl.ds(base, block), :] = got[:, :4 * width].astype(dw_ref.dtype)
        db_ref[pl.ds(base, block), :] = got[:, 4 * width:]
        return carry

    lax.fori_loop(0, depth // block, weigh, 0)


def saved_shapes(rows, depth, width):
    chunks = rows // CHUNK
    carried = CHUNK * chunks * (chunks - 1) // 2

    def of(shape, dtype):
        return jax.ShapeDtypeStruct(shape, dtype)

    tall = of((rows, width), F32)
    slim = of((rows, width), BF)
    return (
        of((rows, depth), BF), slim, slim, slim, slim, tall, tall, of((rows, rows), F32),
        of((carried, width), F32), tall, tall, tall, tall, tall, tall,
    )


VMEM = pl.BlockSpec(memory_space=pltpu.VMEM)
SMEM = pl.BlockSpec(memory_space=pltpu.SMEM)


def attend_forward(deal, found, lengths, x_all, gain, w_all, wb_all, taps):
    rows, depth = x_all.shape
    width = w_all.shape[1] // 4
    saved = saved_shapes(rows, depth, width)
    return pl.pallas_call(
        forward_kernel,
        out_shape=(jax.ShapeDtypeStruct((rows, width), BF),) + saved,
        in_specs=[SMEM, SMEM, SMEM] + [VMEM] * 5,
        out_specs=tuple([VMEM] * (1 + len(saved))),
        scratch_shapes=[pltpu.VMEM((rows, 4 * width), F32), pltpu.VMEM((rows, rows), F32)],
        compiler_params=pltpu.CompilerParams(vmem_limit_bytes=48 * 1024 * 1024),
        name="attend_forward",
    )(deal, found, lengths, x_all, gain, w_all, wb_all, taps)


def attend_backward(deal, place, lengths, live, d_out, h1, w_all, wb_all, taps, saved):
    rows, width = d_out.shape
    depth = h1.shape[1]
    return pl.pallas_call(
        backward_kernel,
        out_shape=(
            jax.ShapeDtypeStruct((rows, depth), BF),
            jax.ShapeDtypeStruct((depth, 4 * width), BF),
            jax.ShapeDtypeStruct((depth, width), F32),
            jax.ShapeDtypeStruct((taps.shape[0], width), F32),
        ),
        in_specs=[SMEM, SMEM, SMEM, SMEM] + [VMEM] * (5 + len(saved)),
        out_specs=(VMEM, VMEM, VMEM, VMEM),
        scratch_shapes=[
            pltpu.VMEM((rows, rows), F32),
            pltpu.VMEM((rows, width), BF),
            pltpu.VMEM((rows, width), F32),
            pltpu.VMEM((rows, width), F32),
            pltpu.VMEM((rows, width), F32),
            pltpu.VMEM((rows, width), F32),
            pltpu.VMEM((rows, 5 * width), BF),
        ],
        compiler_params=pltpu.CompilerParams(vmem_limit_bytes=56 * 1024 * 1024),
        name="attend_backward",
    )(deal, place, lengths, live, d_out, h1, w_all, wb_all, taps, *saved)


def steps_of(axis, descending):
    size = lax.axis_size(axis)
    bits = []
    bit = 1
    while bit < size:
        bits.append((axis, bit))
        bit *= 2
    return bits[::-1] if descending else bits


def swap(value, axis, bit):
    size = lax.axis_size(axis)
    return lax.ppermute(value, axis, [(i, i ^ bit) for i in range(size)])


def spread_rows(value, steps):
    for axis, bit in steps:
        value = jnp.concatenate([value, swap(value, axis, bit)], axis=0)
    return value


def gather_rows(value, steps):
    for axis, bit in steps[::-1]:
        half = value.shape[0] // 2
        value = value[:half] + swap(value[half:].astype(BF), axis, bit).astype(F32)
    return value


def over_shard(value):
    size = lax.axis_size("shard")
    if size == 2:
        other = swap(value, "shard", 1)
        mine = lax.axis_index("shard") == 0
        return jnp.stack([jnp.where(mine, value, other), jnp.where(mine, other, value)])
    return lax.all_gather(value, "shard", axis=0, tiled=False)


def deal_out(value, axis):
    return lax.all_to_all(value, axis, split_axis=0, concat_axis=0, tiled=True)


def norm_back(value, inverse, gain, grad):
    scaled = grad * gain
    return inverse * scaled - value * inverse**3 * jnp.mean(scaled * value, axis=1, keepdims=True)


def local(
    tokens, cotangent, valid_mask, lengths, deal, attn_gain,
    w_query, w_key, w_value, w_house, w_beta, conv_taps, w_out,
    mlp_gain, w_gate, w_up, w_down,
):
    shards, ranks, lanes = (lax.axis_size(a) for a in ("shard", "ctx", "tp"))
    shard, rank, lane = (lax.axis_index(a) for a in ("shard", "ctx", "tp"))
    span, depth = tokens.shape
    share, columns = w_query.shape
    heads = w_beta.shape[1]
    width = columns // heads
    piece = span // 2
    group = ranks * span
    small = span // lanes
    part = w_gate.shape[1] // shards
    spare = ranks - heads
    tp_steps = steps_of("tp", True)
    plane_steps = steps_of("shard", False) + tp_steps
    live = (rank < heads).astype(jnp.int32).reshape(1, 1)
    head_at = jnp.minimum(rank, heads - 1)

    half = lane % 2
    own = lax.dynamic_slice_in_dim(tokens, half * piece, piece, axis=0)
    near = [own] + [
        lax.ppermute(own, "ctx", [(i, (i + k) % ranks) for i in range(ranks)])
        for k in range(1, ranks)
    ]
    near = jnp.concatenate(near, axis=0)
    x_all = jnp.concatenate([near, swap(near, "tp", 1)], axis=0)
    owner = deal // 2
    found = jnp.where(deal % 2 == half, 0, ranks) + (rank - owner) % ranks

    blocks = jnp.stack([w_query, w_key, w_value, w_house]).reshape(4, share, heads, width)
    blocks = blocks.transpose(2, 1, 0, 3).reshape(heads, share, 4 * width)
    beta_rows = jnp.pad(w_beta.T.reshape(heads, 1, share), ((0, 0), (0, 15), (0, 4 * width - share)))
    blocks = jnp.pad(jnp.concatenate([blocks, beta_rows], axis=1), ((0, spare), (0, 0), (0, 0)))
    blocks = over_shard(deal_out(blocks, "ctx"))
    w_all = blocks[:, :, :share].reshape(depth, 4 * width)
    wb_all = jnp.pad(blocks[:, :, share, :share].reshape(depth, 1), ((0, 0), (0, width - 1)))
    taps = lax.dynamic_slice_in_dim(conv_taps, head_at * width, width, axis=1)

    def fetch(weight):
        parts = weight.reshape(share, shards, part).transpose(1, 0, 2)
        rows = deal_out(parts, "shard").reshape(shards * share, part)
        return lax.all_gather(rows, "ctx", axis=0, tiled=True)

    wo_t = lax.all_gather(w_out.T, ("shard", "ctx"), axis=0, tiled=True)
    wg_all = fetch(w_gate)
    wu_all = fetch(w_up)
    wd_all = fetch(w_down.T)

    def to_plane(value):
        value = value.reshape(-1, shards, ranks, share).transpose(0, 2, 1, 3)
        return value.reshape(-1, depth)

    def from_plane(value):
        value = value.reshape(-1, ranks, shards, share).transpose(0, 2, 1, 3)
        return value.reshape(-1, depth)

    def my_rows(value):
        return lax.dynamic_slice_in_dim(value, lane * small, small, axis=0)

    grad_own = my_rows(cotangent)
    grad_plane = spread_rows(to_plane(grad_own), plane_steps)

    fwd = attend_forward(deal, found, lengths, x_all, attn_gain[None], w_all, wb_all, taps)
    head_out, h1, saved = fwd[0], fwd[1], fwd[2:]
    slots = jnp.arange(lanes, dtype=jnp.int32)
    order = jnp.full_like(slots, lane)
    for index, (_, bit) in enumerate(tp_steps):
        order = order ^ jnp.where((slots >> index) % 2 == 1, bit, 0)
    o_rows = deal_out(head_out.reshape(ranks, span, width), "ctx")[:heads]
    o_rows = o_rows.reshape(heads, lanes, small, width).transpose(1, 2, 0, 3)
    o_rows = jnp.take(o_rows, order, axis=0).reshape(span, columns)
    attn = gather_rows(dg(o_rows, wo_t, 1, 1), tp_steps)
    x_own = my_rows(tokens).astype(F32)
    middle = x_own + attn
    gain_two = mlp_gain.astype(F32)
    inv_two = lax.rsqrt(jnp.mean(middle * middle, axis=1, keepdims=True) + EPS)
    normed = (middle * inv_two * gain_two).astype(BF)
    h2 = spread_rows(to_plane(normed), plane_steps)

    gate = dg(h2, wg_all, 1, 0)
    up = dg(h2, wu_all, 1, 0)
    sig = jax.nn.sigmoid(gate)
    swish = gate * sig
    act = (swish * up).astype(BF)
    d_act = dg(grad_plane, wd_all, 1, 0)
    d_gate = (d_act * up * sig * (1.0 + gate * (1.0 - sig))).astype(BF)
    d_up = (d_act * swish).astype(BF)
    d_two = gather_rows(dg(d_gate, wg_all, 1, 1) + dg(d_up, wu_all, 1, 1), plane_steps)
    d_two = from_plane(d_two)
    mlp = from_plane(gather_rows(dg(act, wd_all, 1, 1), plane_steps))
    result = middle + mlp

    def give_back(left, right):
        grad = dg(left, right, 0, 0).astype(BF)
        grad = lax.psum_scatter(grad, "ctx", scatter_dimension=0, tiled=True)
        grad = deal_out(grad.reshape(shards, share, part), "shard")
        return grad.transpose(1, 0, 2).reshape(share, shards * part).astype(F32)

    d_wgate = give_back(h2, d_gate)
    d_wup = give_back(h2, d_up)
    d_wdown = give_back(grad_plane, act).T

    d_gain_two = jnp.sum(d_two * middle * inv_two, axis=0)
    d_middle = grad_own.astype(F32) + norm_back(middle, inv_two, gain_two, d_two)
    d_attn = spread_rows(d_middle.astype(BF), tp_steps)
    d_heads = dg(d_attn, wo_t, 1, 0).astype(BF).reshape(lanes, small, heads, width)
    natural = jnp.zeros_like(slots)
    for index, (_, bit) in enumerate(tp_steps):
        natural = natural + jnp.where(((slots ^ lane) & bit) != 0, 1 << index, 0)
    d_heads = jnp.take(d_heads, natural, axis=0).transpose(2, 0, 1, 3).reshape(heads, span, width)
    d_heads = deal_out(jnp.pad(d_heads, ((0, spare), (0, 0), (0, 0))), "ctx")
    d_wout = dg(d_attn, o_rows, 0, 0).astype(BF)
    d_wout = lax.psum_scatter(d_wout, ("shard", "ctx"), scatter_dimension=0, tiled=True)
    d_wout = d_wout.astype(F32).T

    given = jnp.arange(group // small, dtype=jnp.int32)
    apart = (given % lanes) ^ lane
    turned = jnp.zeros_like(apart)
    for index, (_, bit) in enumerate(tp_steps):
        turned = turned + jnp.where((apart & bit) != 0, 1 << index, 0)
    place = (turned * ranks + given // lanes)[None]
    d_one, d_w, d_b, d_taps = attend_backward(
        deal, place, lengths, live, d_heads.reshape(group, width), h1, w_all, wb_all, taps, saved
    )
    d_one = gather_rows(d_one, tp_steps)
    d_one = deal_out(d_one.astype(BF).reshape(ranks, small, depth), "ctx")
    d_one = jnp.sum(d_one.astype(F32), axis=0)
    gain_one = attn_gain.astype(F32)
    inv_one = lax.rsqrt(jnp.mean(x_own * x_own, axis=1, keepdims=True) + EPS)
    d_gain_one = jnp.sum(d_one * x_own * inv_one, axis=0)
    d_input = d_middle + norm_back(x_own, inv_one, gain_one, d_one)
    d_tokens = lax.all_gather(d_input.astype(BF), "tp", axis=0, tiled=True)
    output = lax.all_gather(result.astype(BF), "tp", axis=0, tiled=True)

    d_w = deal_out(d_w.reshape(shards, ranks * share, 4 * width), "shard")
    d_w = jnp.sum(d_w.astype(F32), axis=0).astype(BF)
    d_w = deal_out(d_w.reshape(ranks, share, 4 * width), "ctx")[:heads].astype(F32)
    d_w = d_w.reshape(heads, share, 4, width).transpose(2, 1, 0, 3).reshape(4, share, columns)

    mask = my_rows(valid_mask).astype(F32)
    totals = jnp.stack(
        [jnp.sum(mask * jnp.sum(b * b, axis=1)) for b in (x_own, attn, mlp, result)]
        + [jnp.sum(mask)]
    )
    mine = (jnp.arange(heads) == rank).astype(F32)
    beta_part = mine[:, None] * d_b[:, 0][None]
    taps_part = mine[:, None, None] * d_taps[None]
    beta_sum, taps_sum, one_sum, two_sum, totals = lax.psum(
        (beta_part, taps_part, d_gain_one, d_gain_two, totals), ("shard", "ctx")
    )
    one_sum, two_sum, totals = lax.psum((one_sum, two_sum, totals), "tp")
    d_beta = lax.dynamic_slice_in_dim(beta_sum, (shard * ranks + rank) * share, share, axis=1).T
    d_conv = taps_sum.transpose(1, 0, 2).reshape(conv_taps.shape)
    rms_stats = jnp.sqrt(totals[:4] / (jnp.maximum(totals[4], 1.0) * depth))
    return (
        output, d_tokens, one_sum, d_w[0], d_w[1], d_w[2], d_w[3], d_beta, d_conv,
        d_wout, two_sum, d_wgate, d_wup, d_wdown, rms_stats,
    )


def solution(mesh):
    rows = P(("shard", "ctx"), None)
    tiled = P(("shard", "ctx"), "tp")
    turned = P("tp", ("shard", "ctx"))
    placed = (
        rows, rows, P(("shard", "ctx")), P("shard", None), P("shard", None), P(),
        tiled, tiled, tiled, tiled, tiled, P(None, "tp"), turned, P(), tiled, tiled, turned,
    )
    return jax.shard_map(
        local,
        mesh=mesh,
        in_specs=placed,
        out_specs=(
            rows, rows, P(), tiled, tiled, tiled, tiled, tiled, P(None, "tp"),
            turned, P(), tiled, tiled, turned, P(),
        ),
        check_vma=False,
    )
```

time: 3120 us -> 511 us (0.16); the launches traced: 3070 us -> 505 us
  local copies, waits for them, and re-layouts: 1170 us -> 71.8 us
  waiting for transfers between devices: 1030 us -> 189 us
  matrix products: 407 us -> 25.4 us
  other arithmetic: 231 us -> 27.9 us
  blocking collectives: 130 us -> 63.5 us
  loops' own time: 54.6 us -> 0 us
  starting transfers between devices: 26.7 us -> 70.3 us
  Pallas kernels: 0 us -> 40.6 us
    reduce_scatter x11 -> x4, waiting for transfers between devices: 684 us -> 9.82 us  [the longest x1 9.79 us: local(): lax.psum_scatter(d_wout, ('shard', 'ctx'), scatter_dimension=0, tiled=True)]
    pad x40 -> x3, local copies, waits for them, and re-layouts: 544 us -> 1.75 us  [the longest x1 0.98 us: local(): jnp.pad(jnp.concatenate([blocks, beta_rows], axis=1), ((0, spare), (0, 0)...]
    dot_general x335 -> x12, matrix products: 405 us -> 25.4 us  [dg(): lax.dot_general(left, right, (((cl,), (cr,)), ((), ())), preferred_elemen...]
    all_gather x11 -> x4, waiting for transfers between devices: 193 us -> 24.4 us  [the longest x3 24.4 us: fetch(): return lax.all_gather(rows, 'ctx', axis=0, tiled=True)]
    broadcast_in_dim x39 -> x1, local copies, waits for them, and re-layouts: 153 us -> 0.01 us  [local(): attn_gain[None]]
    dynamic_slice x133 -> x2, local copies, waits for them, and re-layouts: 110 us -> 0.93 us  [the longest x1 0.93 us: my_rows(): return lax.dynamic_slice_in_dim(value, lane * small, small, axis=0)]
    reshape x30 -> x19, local copies, waits for them, and re-layouts: 107 us -> 9.87 us  [the longest x3 5.4 us: fetch(): parts = weight.reshape(share, shards, part).transpose(1, 0, 2)]
    ppermute x4 -> x23, waiting for transfers between devices: 7.84 us -> 104 us  [the longest x20 52.9 us: swap(): return lax.ppermute(value, axis, [(i, i ^ bit) for i in range(size)])]
  transfers between devices with their start and end apart: 34 -> 43, of which waited for: 21 -> 22; matrix products, arithmetic and copies ran while one was open for 20% -> 19% of each run, Pallas kernels for 0% -> 8%
where the time goes in v1:
time: 511 us; the launch traced here: 505 us
  waiting for transfers between devices  189 us (37%)
  local copies, waits for them, and re-layouts  71.8 us (14%)
  starting transfers between devices  70.3 us (14%)
  blocking collectives  63.5 us (12%)
  Pallas kernels  40.6 us (8%)
  other arithmetic  27.9 us (5%)
  matrix products  25.4 us (5%)
  between operations  16.1 us (3%)
    ppermute x20, waiting for transfers between devices, swap(): return lax.ppermute(value, axis, [(i, i ^ bit) for i in range(size)])  52.9 us
    ppermute x3, waiting for transfers between devices, local(): lax.ppermute(own, 'ctx', [(i, (i + k) % ranks) for i in range(ranks)])  51.1 us
    all_to_all x12, waiting for transfers between devices, deal_out(): return lax.all_to_all(value, axis, split_axis=0, concat_axis=0, tiled=True)  49.4 us
    all_to_all x12, starting transfers between devices, deal_out(): return lax.all_to_all(value, axis, split_axis=0, concat_axis=0, tiled=True)  46.9 us
    psum x1, blocking collectives, local(): lax.psum((beta_part, taps_part, d_gain_one, d_gain_two, totals), ('shard'...  37.1 us
    unnamed x134, local copies, waits for them, and re-layouts  31.9 us
    dot_general x12, matrix products, dg(): lax.dot_general(left, right, (((cl,), (cr,)), ((), ())), preferred_elemen...  25.4 us
    pallas_call x1, Pallas kernels, attend_backward(): pl.pallas_call(backward_kernel, out_shape=(jax.ShapeDtypeStruct((rows, de...  24.6 us
  transfers between devices with their start and end apart: 43, of which 22 were waited for; matrix products, arithmetic and copies ran while one was open for 19% of the time, Pallas kernels for 8%

profile of v1, /device:TPU:0, one launch (start us, length us, event | category | flops | bytes accessed | tf_op | source)
XLA Modules:
  0.0 504.6 jit_solution(2191937232600104309)
XLA Ops:
  10.1 4.2 all-to-all-start.3
  17.2 4.4 all-to-all-done.3
  21.6 5.1 %all-to-all-start = ((bf16[4,208,512]{2,1,0:T(8,128)(2,1)}), bf16[4,208,512]{2,1,0:T(8,128)(2,1)S(1)}, u32[]{:S(2)}, u32[]{:S(2)}) async-start(bf16[4,208,512]{2,1,0:T(8,128)(2,1)} %pad.17), calls=%async_computation | async-start | bytes 1703936 | tf_op jit(solution)/shard_map/all_to_all | solution.py:450
  28.4 3.8 collective-permute-start.2
  33.4 24.4 %collective-permute-done.2 = bf16[96,1536]{1,0:T(8,128)(2,1)} collective-permute-done((bf16[96,1536]{1,0:T(8,128)(2,1)}, bf16[96,1536]{1,0:T(8,128)(2,1)}, u32[]{:S(2)}, u32[]{:S(2)}) %collective-permute-start.2) | collective-permute-done | bytes 294944 | tf_op jit(solution)/shard_map/ppermute | solution.py:482
  57.9 26.7 %collective-permute-done.1 = bf16[96,1536]{1,0:T(8,128)(2,1)} collective-permute-done((bf16[96,1536]{1,0:T(8,128)(2,1)}, bf16[96,1536]{1,0:T(8,128)(2,1)}, u32[]{:S(2)}, u32[]{:S(2)}) %collective-permute-start.1) | collective-permute-done | bytes 294944 | tf_op jit(solution)/shard_map/ppermute | solution.py:482
  84.6 2.3 pad_maximum_fusion
  100.4 4.4 all-to-all-start.2
  112.6 17.7 %collective-permute-done.4 = bf16[4,208,512]{2,1,0:T(8,128)(2,1)S(1)} collective-permute-done((bf16[4,208,512]{2,1,0:T(8,128)(2,1)S(1)}, bf16[4,208,512]{2,1,0:T(8,128)(2,1)S(1)}, u32[]{:S(2)}, u32[]{:S(2)}) %collective-permute-start.4) | collective-permute-done | bytes 852000 | tf_op jit(solution)/shard_map/ppermute | solution.py:424
  132.7 15.9 %attend_forward.1 = (bf16[768,128]{1,0:T(8,128)(2,1)}, bf16[768,1536]{1,0:T(8,128)(2,1)}, bf16[768,128]{1,0:T(8,128)(2,1)S(1)}, bf16[768,128]{1,0:T(8,128)(2,1)S...) custom-call(s32[1,8]{1,0:T(1,128)S(1)} %copy-done.17, ...), custom_call_target="tpu_custom_call" | custom-call | tf_op jit(solution)/shard_map/attend_forward/pallas_call | solution.py:374
  158.4 3.4 all-to-all-start.1
  162.5 6.6 %all-to-all-done.1 = bf16[4,192,128]{2,1,0:T(8,128)(2,1)S(1)} async-done(((bf16[4,192,128]{2,1,0:T(8,128)(2,1)}), bf16[4,192,128]{2,1,0:T(8,128)(2,1)S(1)}, u32[]{:S(2)}, u32[]{:S(2)}) %all-to-all-start.1) | async-done | bytes 196640 | tf_op jit(solution)/shard_map/all_to_all | solution.py:450
  169.1 3.5 all-to-all-start.4
  178.6 7.4 %collective-permute-done.14 = bf16[96,1536]{1,0:T(8,128)(2,1)S(1)} collective-permute-done((bf16[96,1536]{1,0:T(8,128)(2,1)S(1)}, bf16[96,1536]{1,0:T(8,128)(2,1)S(1)}, u32[]{:S(2)}, u32[]{:S(2)}) %collective-permute-start.14) | collective-permute-done | bytes 294944 | tf_op jit(solution)/shard_map/ppermute | solution.py:424
  186.1 2.6 collective-permute-done.6
  201.2 4.1 collective-permute-done.8
  208.3 3.5 fusion.34
  211.9 3.5 fusion.33
  215.4 24.4 %all-gather.11.cloned.1.call-done = bf16[1536,512]{1,0:T(8,128)(2,1)} async-done(((bf16[384,512]{1,0:T(8,128)(2,1)}), bf16[1536,512]{1,0:T(8,128)(2,1)}) %all-gather.11.cloned.1.call-update) | async-done | bytes 1572880 | tf_op jit(solution)/shard_map/all_gather | solution.py:502
  239.7 2.9 multiply_convert_fusion
  242.6 2.2 convolution_convert_fusion
  244.9 3.5 convolution_convert_fusion.1
  255.4 3.4 convolution_convert_fusion.2
  263.8 6.5 %collective-permute-done.11 = bf16[96,1536]{1,0:T(8,128)(2,1)S(1)} collective-permute-done((bf16[96,1536]{1,0:T(8,128)(2,1)S(1)}, bf16[96,1536]{1,0:T(8,128)(2,1)S(1)}, u32[]{:S(2)}, u32[]{:S(2)}) %collective-permute-start.11) | collective-permute-done | bytes 294944 | tf_op jit(solution)/shard_map/ppermute | solution.py:424
  271.9 4.2 collective-permute-done.17
  278.6 3.1 collective-permute-done.18
  286.5 3.7 collective-permute-done.19
  294.3 3.8 all-to-all-start.5
  298.6 13.3 %all-to-all-done.5 = bf16[4,192,128]{2,1,0:T(8,128)(2,1)S(1)} async-done(((bf16[4,192,128]{2,1,0:T(8,128)(2,1)}), bf16[4,192,128]{2,1,0:T(8,128)(2,1)S(1)}, u32[]{:S(2)}, u32[]{:S(2)}) %all-to-all-start.5) | async-done | bytes 196640 | tf_op jit(solution)/shard_map/all_to_all | solution.py:450
  312.6 24.6 %attend_backward.1 = (bf16[768,1536]{1,0:T(8,128)(2,1)}, bf16[1536,512]{1,0:T(8,128)(2,1)}, f32[1536,128]{1,0:T(8,128)}, f32[4,128]{1,0:T(4,128)}) custom-call(s32[1,8]{1,0:T(1,128)} %deal_ref.3, s32[1,16]{1,0:T(1,128)} %fusion.20.place_ref, s32[1,3]{1,0:T(1,128)} %len_ref.3, s32[1,1]{1,0:T(1,128)} %bitcast.21.live_ref, bf16[768,128]{1,0:T(8,128)(2,1)} %bitcast.145, ...), custom_call_target="tpu_custom_call" | custom-call | tf_op jit(solution)/shard_map/attend_backward/pallas_call | solution.py:388
  337.2 3.7 all-to-all-start.7
  341.4 7.9 %all_gather.22 = bf16[192,1536]{1,0:T(8,128)(2,1)} all-gather(bf16[48,1536]{1,0:T(8,128)(2,1)S(1)} %get-tuple-element.91), channel_id=1, replica_groups=mesh['shard'=2,'ctx'=4,'tp'=4] {'tp'}, dimensions={0}, use_global_device_ids=true | all-gather | bytes 737280 | tf_op jit(solution)/shard_map/all_gather | solution.py:593
  349.4 2.4 slice.126
  353.7 3.3 stack.55
  357.0 3.1 all-to-all-done.7
  360.1 3.5 all-to-all-start.11
  366.8 2.7 all-to-all-done.11
  369.5 3.5 all-to-all-start.10
  375.0 5.2 %all-to-all-done.10 = bf16[2,192,512]{2,1,0:T(8,128)(2,1)S(1)} async-done(((bf16[2,192,512]{2,1,0:T(8,128)(2,1)}), bf16[2,192,512]{2,1,0:T(8,128)(2,1)S(1)}, u32[]{:S(2)}, u32[]{:S(2)}) %all-to-all-start.10) | async-done | bytes 393248 | tf_op jit(solution)/shard_map/all_to_all | solution.py:450
  380.2 3.6 all-to-all-start.9
  388.3 2.5 all-to-all-done.9
  390.7 4.2 all-to-all-start.8
  399.6 11.6 %all-to-all-done.8 = bf16[4,192,512]{2,1,0:T(8,128)(2,1)} async-done(((bf16[4,192,512]{2,1,0:T(8,128)(2,1)}), bf16[4,192,512]{2,1,0:T(8,128)(2,1)}, u32[]{:S(2)}, u32[]{:S(2)}) %all-to-all-start.8) | async-done | bytes 786464 | tf_op jit(solution)/shard_map/all_to_all | solution.py:450
  411.3 4.1 all-to-all-start.6
  425.0 9.8 %reduce-scatter.5.cloned.1.call-done = bf16[192,384]{1,0:T(8,128)(2,1)} async-done(((bf16[1536,384]{1,0:T(8,128)(2,1)}), bf16[192,384]{1,0:T(8,128)(2,1)}) %reduce-scatter.5.cloned.1.call-update) | async-done | bytes 147472 | tf_op jit(solution)/shard_map/reduce_scatter | solution.py:573
  437.8 37.1 %all-reduce.4 = (f32[1536]{0:T(1024)S(1)}, f32[3,1536]{1,0:T(4,128)S(1)}, f32[4,384]{1,0:T(4,128)}, f32[1536]{0:T(1024)S(1)}, f32[5]{0:T(128)S(1)}) all-reduce(f32[1536]{0:T(1024)S(1)} %get-tuple-element.56, f32[3,1536]{1,0:T(4,128)S(1)} %copy-done.45, ...), channel_id=1, replica_groups=mesh['shard'=2,'ctx'=4,'tp'=4] {'shard','ctx'}, use_global_device_ids=true, to_apply=%region_6.8 | all-reduce | flops 9221 | bytes 73768 | tf_op jit(solution)/shard_map/psum | solution.py:608
  474.9 10.8 %all-reduce.5 = (f32[1536]{0:T(1024)}, f32[1536]{0:T(1024)}, f32[5]{0:T(128)S(1)}) all-reduce(f32[1536]{0:T(1024)S(1)} %get-tuple-element.66, f32[1536]{0:T(1024)S(1)} %get-tuple-element.69, f32[5]{0:T(128)S(1)} %get-tuple-element.70), channel_id=1, replica_groups=mesh['shard'=2,'ctx'=4,'tp'=4] {'tp'}, use_global_device_ids=true, to_apply=%region_7.9 | all-reduce | flops 3077 | bytes 24616 | tf_op jit(solution)/shard_map/psum | solution.py:611
  487.6 7.6 %all_gather.23 = bf16[192,1536]{1,0:T(8,128)(2,1)S(1)} all-gather(bf16[48,1536]{1,0:T(8,128)(2,1)S(1)} %fusion.9), channel_id=1, replica_groups=mesh['shard'=2,'ctx'=4,'tp'=4] {'tp'}, dimensions={0}, use_global_device_ids=true | all-gather | bytes 737280 | tf_op jit(solution)/shard_map/all_gather | solution.py:592
  (316 shorter events, 122.8 us)
Async XLA Ops:
  7.2 93.2 %copy-start = (bf16[4,384]{1,0:T(4,128)(2,1)S(1)}, bf16[4,384]{1,0:T(4,128)(2,1)}, u32[]{:S(2)}) copy-start(bf16[4,384]{1,0:T(4,128)(2,1)} %param.30) | copy-start | bytes 9220
  7.2 166.2 %all-gather.5.cloned.1.call-start = ((), (), s32[]{:S(2)}) async-start(), calls=%async_computation.16 | async-start | bytes 1327104 | tf_op jit(solution)/shard_map/all_gather | solution.py:504
  10.1 11.5 %all-to-all-start.3 = ((bf16[2,192,512]{2,1,0:T(8,128)(2,1)}), bf16[2,192,512]{2,1,0:T(8,128)(2,1)S(1)}, u32[]{:S(2)}, u32[]{:S(2)}) async-start(bf16[2,192,512]{2,1,0:T(8,128)(2,1)} %copy.100), calls=%async_computation.3 | async-start | bytes 786432 | tf_op jit(solution)/shard_map/all_to_all | solution.py:450
  21.6 78.8 %all-to-all-start = ((bf16[4,208,512]{2,1,0:T(8,128)(2,1)}), bf16[4,208,512]{2,1,0:T(8,128)(2,1)S(1)}, u32[]{:S(2)}, u32[]{:S(2)}) async-start(bf16[4,208,512]{2,1,0:T(8,128)(2,1)} %pad.17), calls=%async_computation | async-start | bytes 1703936 | tf_op jit(solution)/shard_map/all_to_all | solution.py:450
  26.7 181.6 %all-gather.9.cloned.1.call-start = ((), (), s32[]{:S(2)}) async-start(), calls=%async_computation.18 | async-start | bytes 1966080 | tf_op jit(solution)/shard_map/all_gather | solution.py:502
  28.4 29.4 %collective-permute-start.2 = (bf16[96,1536]{1,0:T(8,128)(2,1)}, bf16[96,1536]{1,0:T(8,128)(2,1)}, u32[]{:S(2)}, u32[]{:S(2)}) collective-permute-start(bf16[96,1536]{1,0:T(8,128)(2,1)} %get-tuple-element.79), channel_id=1, source_target_pairs={{0,12},{4,0},{8,4},{12,8},{1,13},{5,1},{9,5},{13,9},{2,14},{6,2},{... | collective-permute-start | bytes 884744 | tf_op jit(solution)/shard_map/ppermute | solution.py:482
  32.3 52.3 %collective-permute-start.1 = (bf16[96,1536]{1,0:T(8,128)(2,1)}, bf16[96,1536]{1,0:T(8,128)(2,1)}, u32[]{:S(2)}, u32[]{:S(2)}) collective-permute-start(bf16[96,1536]{1,0:T(8,128)(2,1)} %get-tuple-element.79), channel_id=1, source_target_pairs={{0,8},{4,12},{8,0},{12,4},{1,9},{5,13},{9,1},{13,5},{2,10},{6,14},... | collective-permute-start | bytes 884744 | tf_op jit(solution)/shard_map/ppermute | solution.py:482
  32.3 52.3 %collective-permute-start = (bf16[96,1536]{1,0:T(8,128)(2,1)}, bf16[96,1536]{1,0:T(8,128)(2,1)}, u32[]{:S(2)}, u32[]{:S(2)}) collective-permute-start(bf16[96,1536]{1,0:T(8,128)(2,1)} %get-tuple-element.79), channel_id=1, source_target_pairs={{0,4},{4,8},{8,12},{12,0},{1,5},{5,9},{9,13},{13,1},{2,6},{6,10},{... | collective-permute-start | bytes 884744 | tf_op jit(solution)/shard_map/ppermute | solution.py:482
  86.9 22.9 %collective-permute-start.3 = (bf16[384,1536]{1,0:T(8,128)(2,1)}, bf16[384,1536]{1,0:T(8,128)(2,1)}, u32[]{:S(2)}, u32[]{:S(2)}) collective-permute-start(bf16[384,1536]{1,0:T(8,128)(2,1)} %pad_maximum_fusion), channel_id=1, source_target_pairs={{0,1},{1,0},{2,3},{3,2},{4,5},{5,4},{6,7},{7,6},{8,9},{9,8},{10,11... | collective-permute-start | bytes 3538952 | tf_op jit(solution)/shard_map/ppermute | solution.py:424
  91.6 84.5 %collective-permute-start.13 = (bf16[48,1536]{1,0:T(8,128)(2,1)S(1)}, bf16[48,1536]{1,0:T(8,128)(2,1)S(1)}, u32[]{:S(2)}, u32[]{:S(2)}) collective-permute-start(bf16[48,1536]{1,0:T(8,128)(2,1)S(1)} %reshape.311), channel_id=1, source_target_pairs={{0,16},{16,0},{1,17},{17,1},{2,18},{18,2},{3,19},{19,3},{4,20},{20... | collective-permute-start | bytes 442376 | tf_op jit(solution)/shard_map/ppermute | solution.py:424
  100.3 32.4 %copy-start.16 = (bf16[4,128]{1,0:T(4,128)(2,1)}, bf16[4,128]{1,0:T(4,128)(2,1)S(1)}, u32[]{:S(2)}) copy-start(bf16[4,128]{1,0:T(4,128)(2,1)S(1)} %constant_dynamic-slice_fusion.1.taps_ref) | copy-start | bytes 3076
  100.4 58.0 %all-to-all-start.2 = ((bf16[2,192,512]{2,1,0:T(8,128)(2,1)}), bf16[2,192,512]{2,1,0:T(8,128)(2,1)}, u32[]{:S(2)}, u32[]{:S(2)}) async-start(bf16[2,192,512]{2,1,0:T(8,128)(2,1)} %copy.99), calls=%async_computation.2 | async-start | bytes 786432 | tf_op jit(solution)/shard_map/all_to_all | solution.py:450
  104.8 25.5 %collective-permute-start.4 = (bf16[4,208,512]{2,1,0:T(8,128)(2,1)S(1)}, bf16[4,208,512]{2,1,0:T(8,128)(2,1)S(1)}, u32[]{:S(2)}, u32[]{:S(2)}) collective-permute-start(bf16[4,208,512]{2,1,0:T(8,128)(2,1)S(1)} %all-to-all-done), channel_id=1, source_target_pairs={{0,16},{16,0},{1,17},{17,1},{2,18},{18,2},{3,19},{19,3},{4,20},{20... | collective-permute-start | bytes 2555912 | tf_op jit(solution)/shard_map/ppermute | solution.py:424
  158.4 10.7 %all-to-all-start.1 = ((bf16[4,192,128]{2,1,0:T(8,128)(2,1)}), bf16[4,192,128]{2,1,0:T(8,128)(2,1)S(1)}, u32[]{:S(2)}, u32[]{:S(2)}) async-start(bf16[4,192,128]{2,1,0:T(8,128)(2,1)} %bitcast.6), calls=%async_computation.1 | async-start | bytes 393216 | tf_op jit(solution)/shard_map/all_to_all | solution.py:450
  161.8 50.1 %all-gather.7.cloned.1.call-start = ((), (), s32[]{:S(2)}) async-start(), calls=%async_computation.17 | async-start | bytes 1966080 | tf_op jit(solution)/shard_map/all_gather | solution.py:502
  169.1 24.7 %all-to-all-start.4 = ((bf16[2,192,512]{2,1,0:T(8,128)(2,1)}), bf16[2,192,512]{2,1,0:T(8,128)(2,1)S(1)}, u32[]{:S(2)}, u32[]{:S(2)}) async-start(bf16[2,192,512]{2,1,0:T(8,128)(2,1)} %copy.101), calls=%async_computation.4 | async-start | bytes 786432 | tf_op jit(solution)/shard_map/all_to_all | solution.py:450
  172.6 67.2 %all-gather.11.cloned.1.call-start = ((), (), s32[]{:S(2)}) async-start(), calls=%async_computation.19 | async-start | bytes 1966080 | tf_op jit(solution)/shard_map/all_gather | solution.py:502
  175.3 2.3 collective-permute-start.5
  176.1 9.9 %collective-permute-start.14 = (bf16[96,1536]{1,0:T(8,128)(2,1)S(1)}, bf16[96,1536]{1,0:T(8,128)(2,1)S(1)}, u32[]{:S(2)}, u32[]{:S(2)}) collective-permute-start(bf16[96,1536]{1,0:T(8,128)(2,1)S(1)} %pad_maximum_fusion.5), channel_id=1, source_target_pairs={{0,2},{1,3},{2,0},{3,1},{4,6},{5,7},{6,4},{7,5},{8,10},{9,11},{10,... | collective-permute-start | bytes 884744 | tf_op jit(solution)/shard_map/ppermute | solution.py:424
  177.7 11.0 %collective-permute-start.6 = (bf16[48,1536]{1,0:T(8,128)(2,1)S(1)}, bf16[48,1536]{1,0:T(8,128)(2,1)S(1)}, u32[]{:S(2)}, u32[]{:S(2)}) collective-permute-start(bf16[48,1536]{1,0:T(8,128)(2,1)S(1)} %slice.209), channel_id=1, source_target_pairs={{0,2},{1,3},{2,0},{3,1},{4,6},{5,7},{6,4},{7,5},{8,10},{9,11},{10,... | collective-permute-start | bytes 442376 | tf_op jit(solution)/shard_map/ppermute | solution.py:424
  186.0 13.2 %collective-permute-start.15 = (bf16[192,1536]{1,0:T(8,128)(2,1)S(1)}, bf16[192,1536]{1,0:T(8,128)(2,1)}, u32[]{:S(2)}, u32[]{:S(2)}) collective-permute-start(bf16[192,1536]{1,0:T(8,128)(2,1)S(1)} %pad_maximum_fusion.2), channel_id=1, source_target_pairs={{0,1},{1,0},{2,3},{3,2},{4,5},{5,4},{6,7},{7,6},{8,9},{9,8},{10,11... | collective-permute-start | bytes 1769480 | tf_op jit(solution)/shard_map/ppermute | solution.py:424
  191.1 5.9 %collective-permute-start.7 = (bf16[48,1536]{1,0:T(8,128)(2,1)S(1)}, bf16[48,1536]{1,0:T(8,128)(2,1)S(1)}, u32[]{:S(2)}, u32[]{:S(2)}) collective-permute-start(bf16[48,1536]{1,0:T(8,128)(2,1)S(1)} %reshape.301), channel_id=1, source_target_pairs={{0,16},{16,0},{1,17},{17,1},{2,18},{18,2},{3,19},{19,3},{4,20},{20... | collective-permute-start | bytes 442376 | tf_op jit(solution)/shard_map/ppermute | solution.py:424
  194.5 165.6 %reduce-scatter.11.cloned.1.call-start = ((), (), s32[]{:S(2)}) async-start(), calls=%async_computation.23 | async-start | bytes 1966080 | tf_op jit(solution)/shard_map/reduce_scatter | solution.py:555
  197.0 8.3 %collective-permute-start.8 = (bf16[96,1536]{1,0:T(8,128)(2,1)S(1)}, bf16[96,1536]{1,0:T(8,128)(2,1)S(1)}, u32[]{:S(2)}, u32[]{:S(2)}) collective-permute-start(bf16[96,1536]{1,0:T(8,128)(2,1)S(1)} %pad_maximum_fusion.4), channel_id=1, source_target_pairs={{0,2},{1,3},{2,0},{3,1},{4,6},{5,7},{6,4},{7,5},{8,10},{9,11},{10,... | collective-permute-start | bytes 884744 | tf_op jit(solution)/shard_map/ppermute | solution.py:424
  205.3 2.1 collective-permute-start.9
  244.8 122.0 %reduce-scatter.9.cloned.1.call-start = ((), (), s32[]{:S(2)}) async-start(), calls=%async_computation.22 | async-start | bytes 1966080 | tf_op jit(solution)/shard_map/reduce_scatter | solution.py:555
  248.4 126.6 %reduce-scatter.7.cloned.1.call-start = ((), (), s32[]{:S(2)}) async-start(), calls=%async_computation.21 | async-start | bytes 1966080 | tf_op jit(solution)/shard_map/reduce_scatter | solution.py:555
  250.7 8.2 %collective-permute-start.10 = (bf16[192,1536]{1,0:T(8,128)(2,1)S(1)}, bf16[192,1536]{1,0:T(8,128)(2,1)}, u32[]{:S(2)}, u32[]{:S(2)}) collective-permute-start(bf16[192,1536]{1,0:T(8,128)(2,1)S(1)} %slice.203), channel_id=1, source_target_pairs={{0,1},{1,0},{2,3},{3,2},{4,5},{5,4},{6,7},{7,6},{8,9},{9,8},{10,11... | collective-permute-start | bytes 1769480 | tf_op jit(solution)/shard_map/ppermute | solution.py:424
  255.2 6.8 %collective-permute-start.16 = (bf16[192,1536]{1,0:T(8,128)(2,1)}, bf16[192,1536]{1,0:T(8,128)(2,1)}, u32[]{:S(2)}, u32[]{:S(2)}) collective-permute-start(bf16[192,1536]{1,0:T(8,128)(2,1)} %slice.202), channel_id=1, source_target_pairs={{0,1},{1,0},{2,3},{3,2},{4,5},{5,4},{6,7},{7,6},{8,9},{9,8},{10,11... | collective-permute-start | bytes 1769480 | tf_op jit(solution)/shard_map/ppermute | solution.py:424
  260.4 9.9 %collective-permute-start.11 = (bf16[96,1536]{1,0:T(8,128)(2,1)S(1)}, bf16[96,1536]{1,0:T(8,128)(2,1)S(1)}, u32[]{:S(2)}, u32[]{:S(2)}) collective-permute-start(bf16[96,1536]{1,0:T(8,128)(2,1)S(1)} %slice.205), channel_id=1, source_target_pairs={{0,2},{1,3},{2,0},{3,1},{4,6},{5,7},{6,4},{7,5},{8,10},{9,11},{10,... | collective-permute-start | bytes 884744 | tf_op jit(solution)/shard_map/ppermute | solution.py:424
  263.2 12.9 %collective-permute-start.17 = (bf16[96,1536]{1,0:T(8,128)(2,1)S(1)}, bf16[96,1536]{1,0:T(8,128)(2,1)S(1)}, u32[]{:S(2)}, u32[]{:S(2)}) collective-permute-start(bf16[96,1536]{1,0:T(8,128)(2,1)S(1)} %slice.204), channel_id=1, source_target_pairs={{0,2},{1,3},{2,0},{3,1},{4,6},{5,7},{6,4},{7,5},{8,10},{9,11},{10,... | collective-permute-start | bytes 884744 | tf_op jit(solution)/shard_map/ppermute | solution.py:424
  270.4 7.3 %collective-permute-start.12 = (bf16[48,1536]{1,0:T(8,128)(2,1)S(1)}, bf16[48,1536]{1,0:T(8,128)(2,1)S(1)}, u32[]{:S(2)}, u32[]{:S(2)}) collective-permute-start(bf16[48,1536]{1,0:T(8,128)(2,1)S(1)} %slice.208), channel_id=1, source_target_pairs={{0,16},{16,0},{1,17},{17,1},{2,18},{18,2},{3,19},{19,3},{4,20},{20... | collective-permute-start | bytes 442376 | tf_op jit(solution)/shard_map/ppermute | solution.py:424
  276.2 5.5 %collective-permute-start.18 = (bf16[48,1536]{1,0:T(8,128)(2,1)S(1)}, bf16[48,1536]{1,0:T(8,128)(2,1)S(1)}, u32[]{:S(2)}, u32[]{:S(2)}) collective-permute-start(bf16[48,1536]{1,0:T(8,128)(2,1)S(1)} %slice.207), channel_id=1, source_target_pairs={{0,16},{16,0},{1,17},{17,1},{2,18},{18,2},{3,19},{19,3},{4,20},{20... | collective-permute-start | bytes 442376 | tf_op jit(solution)/shard_map/ppermute | solution.py:424
  285.1 5.1 %collective-permute-start.19 = (bf16[48,1536]{1,0:T(8,128)(2,1)S(1)}, bf16[48,1536]{1,0:T(8,128)(2,1)S(1)}, u32[]{:S(2)}, u32[]{:S(2)}) collective-permute-start(bf16[48,1536]{1,0:T(8,128)(2,1)S(1)} %get-tuple-element.74), channel_id=1, source_target_pairs={{0,2},{1,3},{2,0},{3,1},{4,6},{5,7},{6,4},{7,5},{8,10},{9,11},{10,... | collective-permute-start | bytes 442376 | tf_op jit(solution)/shard_map/ppermute | solution.py:424
  290.3 1.6 collective-permute-start.20
  294.3 17.6 %all-to-all-start.5 = ((bf16[4,192,128]{2,1,0:T(8,128)(2,1)}), bf16[4,192,128]{2,1,0:T(8,128)(2,1)S(1)}, u32[]{:S(2)}, u32[]{:S(2)}) async-start(bf16[4,192,128]{2,1,0:T(8,128)(2,1)} %pad.19), calls=%async_computation.5 | async-start | bytes 393216 | tf_op jit(solution)/shard_map/all_to_all | solution.py:450
  337.2 22.9 %all-to-all-start.7 = ((bf16[2,768,512]{2,1,0:T(8,128)(2,1)}), bf16[2,768,512]{2,1,0:T(8,128)(2,1)S(1)}, u32[]{:S(2)}, u32[]{:S(2)}) async-start(bf16[2,768,512]{2,1,0:T(8,128)(2,1)} %bitcast.126), calls=%async_computation.7 | async-start | bytes 3145728 | tf_op jit(solution)/shard_map/all_to_all | solution.py:450
  351.8 32.1 %collective-permute-start.21 = (bf16[384,1536]{1,0:T(8,128)(2,1)}, bf16[384,1536]{1,0:T(8,128)(2,1)}, u32[]{:S(2)}, u32[]{:S(2)}) collective-permute-start(bf16[384,1536]{1,0:T(8,128)(2,1)} %slice.126), channel_id=1, source_target_pairs={{0,1},{1,0},{2,3},{3,2},{4,5},{5,4},{6,7},{7,6},{8,9},{9,8},{10,11... | collective-permute-start | bytes 3538952 | tf_op jit(solution)/shard_map/ppermute | solution.py:424
  360.1 9.3 %all-to-all-start.11 = ((bf16[2,192,512]{2,1,0:T(8,128)(2,1)}), bf16[2,192,512]{2,1,0:T(8,128)(2,1)S(1)}, u32[]{:S(2)}, u32[]{:S(2)}) async-start(bf16[2,192,512]{2,1,0:T(8,128)(2,1)} %bitcast.151), calls=%async_computation.15 | async-start | bytes 786432 | tf_op jit(solution)/shard_map/all_to_all | solution.py:450
  363.6 71.2 %reduce-scatter.5.cloned.1.call-start = ((), (), s32[]{:S(2)}) async-start(), calls=%async_computation.20 | async-start | bytes 1327104 | tf_op jit(solution)/shard_map/reduce_scatter | solution.py:573
  369.5 10.8 %all-to-all-start.10 = ((bf16[2,192,512]{2,1,0:T(8,128)(2,1)}), bf16[2,192,512]{2,1,0:T(8,128)(2,1)S(1)}, u32[]{:S(2)}, u32[]{:S(2)}) async-start(bf16[2,192,512]{2,1,0:T(8,128)(2,1)} %bitcast.150), calls=%async_computation.13 | async-start | bytes 786432 | tf_op jit(solution)/shard_map/all_to_all | solution.py:450
  380.2 10.5 %all-to-all-start.9 = ((bf16[2,192,512]{2,1,0:T(8,128)(2,1)}), bf16[2,192,512]{2,1,0:T(8,128)(2,1)S(1)}, u32[]{:S(2)}, u32[]{:S(2)}) async-start(bf16[2,192,512]{2,1,0:T(8,128)(2,1)} %bitcast.152), calls=%async_computation.11 | async-start | bytes 786432 | tf_op jit(solution)/shard_map/all_to_all | solution.py:450
  386.8 10.8 %collective-permute-start.22 = (bf16[192,1536]{1,0:T(8,128)(2,1)}, bf16[192,1536]{1,0:T(8,128)(2,1)}, u32[]{:S(2)}, u32[]{:S(2)}) collective-permute-start(bf16[192,1536]{1,0:T(8,128)(2,1)} %slice.201), channel_id=1, source_target_pairs={{0,2},{1,3},{2,0},{3,1},{4,6},{5,7},{6,4},{7,5},{8,10},{9,11},{10,... | collective-permute-start | bytes 1769480 | tf_op jit(solution)/shard_map/ppermute | solution.py:424
  390.7 20.5 %all-to-all-start.8 = ((bf16[4,192,512]{2,1,0:T(8,128)(2,1)}), bf16[4,192,512]{2,1,0:T(8,128)(2,1)}, u32[]{:S(2)}, u32[]{:S(2)}) async-start(bf16[4,192,512]{2,1,0:T(8,128)(2,1)} %bitcast.27), calls=%async_computation.8 | async-start | bytes 1572864 | tf_op jit(solution)/shard_map/all_to_all | solution.py:450
  411.3 25.2 %all-to-all-start.6 = ((bf16[4,48,1536]{2,1,0:T(8,128)(2,1)}), bf16[4,48,1536]{2,1,0:T(8,128)(2,1)}, u32[]{:S(2)}, u32[]{:S(2)}) async-start(bf16[4,48,1536]{2,1,0:T(8,128)(2,1)} %bitcast.125), calls=%async_computation.6 | async-start | bytes 1179648 | tf_op jit(solution)/shard_map/all_to_all | solution.py:450
  424.2 63.3 %copy-start.33 = (f32[48,1536]{1,0:T(8,128)S(1)}, f32[48,1536]{1,0:T(8,128)}, u32[]{:S(2)}) copy-start(f32[48,1536]{1,0:T(8,128)} %get-tuple-element.75) | copy-start | bytes 884740
  424.2 63.3 %copy-start.51 = (f32[48]{0:T(128)S(1)}, f32[48]{0:T(128)}, u32[]{:S(2)}) copy-start(f32[48]{0:T(128)} %get-tuple-element.92) | copy-start | bytes 580
  437.6 58.3 %copy-start.22 = (bf16[192,1536]{1,0:T(8,128)(2,1)S(1)}, bf16[192,1536]{1,0:T(8,128)(2,1)}, u32[]{:S(2)}) copy-start(bf16[192,1536]{1,0:T(8,128)(2,1)} %all_gather.22) | copy-start | bytes 1769476
  (54 other events, 231.9 us)
Sparse Core Ops, SparseCore 0:
  10.1 63.0 all-gather.4
  75.4 36.0 all-gather.8
  164.2 37.5 all-gather.6
  203.7 35.9 all-gather.10
  245.0 34.1 reduce-scatter.10
  281.3 37.4 reduce-scatter.8
  321.1 34.3 reduce-scatter.6
  367.8 66.8 reduce-scatter.4

commit v2 on v1

--- a/solution.py
+++ b/solution.py
@@ -77,28 +77,52 @@
     return row, col
 
 
-def forward_kernel(
-    deal_ref, found_ref, len_ref, x_ref, gain_ref, w_ref, wb_ref, taps_ref,
-    o_ref, h1_ref, q_ref, k_ref, v_ref, house_ref, raw_ref, logit_ref, prob_ref,
-    u_ref, kt_ref, tr_ref, tinv_ref, xq_ref, yk_ref, z_ref,
-    proj_ref, score_ref,
-):
-    rows = x_ref.shape[0]
+def forward_kernel(x_count, w_count, *refs):
+    deal_ref, spot_ref, slot_ref, len_ref = refs[:4]
+    x_refs, refs = refs[4:4 + x_count], refs[4 + x_count:]
+    gain_ref, refs = refs[0], refs[1:]
+    w_refs, refs = refs[:w_count], refs[w_count:]
+    taps_ref, o_ref, refs = refs[0], refs[1], refs[2:]
+    kept, refs = refs[:SAVED], refs[SAVED:]
+    held, (proj_ref, score_ref, sems) = refs[:SAVED], refs[SAVED:]
+    (
+        w_ref, wb_ref, h1_ref, q_ref, k_ref, v_ref, house_ref, raw_ref, logit_ref, prob_ref,
+        u_ref, kt_ref, tr_ref, tinv_ref, xq_ref, yk_ref, z_ref,
+    ) = held
+    piece, depth = x_refs[0].shape
     pieces = deal_ref.shape[1]
-    piece = rows // pieces
+    rows = pieces * piece
     chunks = rows // CHUNK
     width = o_ref.shape[1]
+    share = depth // w_count
     scale = width ** (-0.5)
     ends = seq_ends(len_ref)
     gain = gain_ref[...].astype(F32)
 
+    def keep(first, last):
+        for index in range(first, last):
+            pltpu.make_async_copy(held[index], kept[index], sems.at[index]).start()
+
+    pick = jnp.where(
+        (lax.broadcasted_iota(jnp.int32, (16, width), 0) == 0)
+        & (lax.broadcasted_iota(jnp.int32, (16, width), 1) == 0),
+        1.0,
+        0.0,
+    ).astype(BF)
+    for index, ref in enumerate(w_refs):
+        base = pl.multiple_of(slot_ref[0, index] * share, share)
+        w_ref[pl.ds(base, share), :] = ref[:share, :]
+        wb_ref[pl.ds(base, share), :] = dg(ref[share:, :share], pick, 0, 0).astype(BF)
+    for index, ref in enumerate(x_refs):
+        x = ref[...].astype(F32)
+        inv = lax.rsqrt(jnp.mean(x * x, axis=1, keepdims=True) + EPS)
+        base = pl.multiple_of(spot_ref[0, index] * piece, piece)
+        h1_ref[pl.ds(base, piece), :] = (x * inv * gain).astype(BF)
+    keep(0, 3)
+
     def project(step, carry):
         base = pl.multiple_of(step * piece, piece)
-        here = pl.multiple_of(found_ref[0, step] * piece, piece)
-        x = x_ref[pl.ds(here, piece), :].astype(F32)
-        inv = lax.rsqrt(jnp.mean(x * x, axis=1, keepdims=True) + EPS)
-        h1 = (x * inv * gain).astype(BF)
-        h1_ref[pl.ds(base, piece), :] = h1
+        h1 = h1_ref[pl.ds(base, piece), :]
         proj_ref[pl.ds(base, piece), :] = dg(h1, w_ref[...], 1, 0)
         logit_ref[pl.ds(base, piece), :] = dg(h1, wb_ref[...], 1, 0)
         return carry
@@ -118,6 +142,7 @@
         )
     unit = mixed * lax.rsqrt(jnp.sum(mixed * mixed, axis=1, keepdims=True) + EPS)
     house_ref[...] = unit.astype(BF)
+    keep(3, 9)
 
     row, col = tile_iota()
     strict = row > col
@@ -153,6 +178,7 @@
         proj_ref[s, :width] = query.astype(F32) - mm(xq, house)
         kt_ref[s, :] = key.astype(F32) - mm(yk, house, 0, 0)
         tr_ref[s, :] = eye - mm(house, zz, 0, 0)
+    keep(11, SAVED)
     offset = 0
     for n in range(chunks - 2, -1, -1):
         later = slice((n + 1) * CHUNK, rows)
@@ -163,12 +189,13 @@
         score_ref[later, spans[n]] = mm(carried, kt_ref[spans[n], :], 1, 1) * scale
         if n > 0:
             proj_ref[later, :width] = mm(carried, tr_ref[spans[n], :])
+    keep(10, 11)
     for m, s in enumerate(spans):
         reach = (m + 1) * CHUNK
         at_row = lax.broadcasted_iota(jnp.int32, (CHUNK, reach), 0) + m * CHUNK
         at_col = lax.broadcasted_iota(jnp.int32, (CHUNK, reach), 1)
-        keep = (at_row >= at_col) & (seg_at(at_row, ends) == seg_at(at_col, ends))
-        logits = jnp.where(keep, score_ref[s, :reach], NEG)
+        seen = (at_row >= at_col) & (seg_at(at_row, ends) == seg_at(at_col, ends))
+        logits = jnp.where(seen, score_ref[s, :reach], NEG)
         top = jnp.max(logits, axis=1, keepdims=True)
         grown = jnp.exp(logits - top)
         prob = grown / jnp.sum(grown, axis=1, keepdims=True)
@@ -181,16 +208,34 @@
         o_ref[pl.ds(given, piece), :] = proj_ref[pl.ds(base, piece), :width].astype(BF)
         return carry
 
+    keep(9, 10)
     lax.fori_loop(0, pieces, give, 0)
-
-
-def backward_kernel(
-    deal_ref, place_ref, len_ref, live_ref, do_ref, h1_ref, w_ref, wb_ref, taps_ref,
-    q_ref, k_ref, v_ref, house_ref, raw_ref, logit_ref, prob_ref,
-    u_ref, kt_ref, tr_ref, tinv_ref, xq_ref, yk_ref, z_ref,
-    dh1_ref, dw_ref, db_ref, dtaps_ref,
-    ds_ref, dout_ref, du_ref, dkt_ref, dtr_ref, dhouse_ref, dproj_ref,
-):
+    for index in range(SAVED):
+        pltpu.make_async_copy(held[index], kept[index], sems.at[index]).wait()
+
+
+def backward_kernel(*refs):
+    deal_ref, place_ref, len_ref, live_ref, do_ref, taps_ref = refs[:6]
+    kept, refs = refs[6:6 + SAVED], refs[6 + SAVED:]
+    (dh1_ref, dproj_ref, small_ref, dtaps_ref), refs = refs[:4], refs[4:]
+    held, refs = refs[:SAVED], refs[SAVED:]
+    ds_ref, dout_ref, du_ref, dkt_ref, dtr_ref, dhouse_ref, sems = refs
+    (
+        w_ref, wb_ref, h1_ref, q_ref, k_ref, v_ref, house_ref, raw_ref, logit_ref, prob_ref,
+        u_ref, kt_ref, tr_ref, tinv_ref, xq_ref, yk_ref, z_ref,
+    ) = held
+
+    def fetch(index):
+        return pltpu.make_async_copy(kept[index], held[index], sems.at[index])
+
+    needed = (5, 9), (10, 11, 12), (3, 4, 6, 8, 13, 14, 15, 16), (7,), (0, 1, 2)
+    for index in sum(needed, ()):
+        fetch(index).start()
+
+    def ready(stage):
+        for index in needed[stage]:
+            fetch(index).wait()
+
     rows = do_ref.shape[0]
     pieces = deal_ref.shape[1]
     piece = rows // pieces
@@ -210,6 +255,7 @@
         return carry
 
     lax.fori_loop(0, pieces, take, 0)
+    ready(0)
     for m, s in enumerate(spans):
         reach = (m + 1) * CHUNK
         prob = prob_ref[s, :reach]
@@ -225,6 +271,7 @@
     for n in range(chunks - 2, -1, -1):
         starts[n] = offset
         offset += rows - (n + 1) * CHUNK
+    ready(1)
     for n in range(chunks - 1):
         later = slice((n + 1) * CHUNK, rows)
         count = rows - (n + 1) * CHUNK
@@ -237,6 +284,7 @@
             dtr_ref[spans[n], :] = mm(carried, before, 0, 0)
             fresh = fresh + mm(before, tr_ref[spans[n], :], 1, 1)
         du_ref[later, :] = fresh
+    ready(2)
     for n, s in enumerate(spans):
         query, key, house = q_ref[s, :], k_ref[s, :], house_ref[s, :]
         strength = 2.0 * jax.nn.sigmoid(logit_ref[s, 0:1])
@@ -296,6 +344,7 @@
         dlogit = dstrength * 2.0 * gate * (1.0 - gate)
         lane = lax.broadcasted_iota(jnp.int32, (CHUNK, width), 1)
         dproj_ref[s, 4 * width:] = jnp.where(lane == 0, dlogit, 0.0).astype(BF)
+    ready(3)
     raw = raw_ref[...]
     taps = taps_ref[...].astype(F32)
     count = taps.shape[0]
@@ -322,91 +371,97 @@
         draw = draw + taps[shift:shift + 1, :] * pltpu.roll(later, rows - shift, 0)
     dproj_ref[:, 3 * width:4 * width] = draw.astype(BF)
 
-    def send(step, carry):
+    ready(4)
+
+    def send(step, total):
         base = pl.multiple_of(step * piece, piece)
         grads = dproj_ref[pl.ds(base, piece), :]
         dh1 = dg(grads[:, :4 * width], w_ref[...], 1, 1) + dg(grads[:, 4 * width:], wb_ref[...], 1, 1)
-        dh1 = (dh1 * live).astype(dh1_ref.dtype)
+        dh1 = dh1 * live
+        h1 = h1_ref[pl.ds(base, piece), :].astype(F32)
+        total = total + jnp.sum(dh1 * h1, axis=0, keepdims=True)
+        dh1 = dh1.astype(dh1_ref.dtype)
         for part in range(piece // small):
             there = place_ref[0, deal_ref[0, step] * (piece // small) + part]
             dh1_ref[pl.ds(pl.multiple_of(there * small, small), small), :] = dh1[
                 part * small:(part + 1) * small
             ]
-        return carry
-
-    lax.fori_loop(0, pieces, send, 0)
-    depth = h1_ref.shape[1]
-    block = 256
-
-    def weigh(step, carry):
-        base = pl.multiple_of(step * block, block)
-        got = dg(h1_ref[:, pl.ds(base, block)], dproj_ref[...], 0, 0) * live
-        dw_ref[pl.ds(base, block), :] = got[:, :4 * width].astype(dw_ref.dtype)
-        db_ref[pl.ds(base, block), :] = got[:, 4 * width:]
-        return carry
-
-    lax.fori_loop(0, depth // block, weigh, 0)
+        return total
+
+    small_ref[...] = jnp.zeros_like(small_ref)
+    small_ref[0:1, :] = lax.fori_loop(0, pieces, send, jnp.zeros((1, h1_ref.shape[1]), F32))
+    beta = dg(dproj_ref[:, 4 * width:], h1_ref[...], 0, 0)
+    small_ref[1:2, :] = beta[0:1, :] * live
+
+
+SAVED = 17
 
 
 def saved_shapes(rows, depth, width):
     chunks = rows // CHUNK
     carried = CHUNK * chunks * (chunks - 1) // 2
-
-    def of(shape, dtype):
-        return jax.ShapeDtypeStruct(shape, dtype)
-
-    tall = of((rows, width), F32)
-    slim = of((rows, width), BF)
+    slim = ((rows, width), BF)
+    tall = ((rows, width), F32)
     return (
-        of((rows, depth), BF), slim, slim, slim, slim, tall, tall, of((rows, rows), F32),
-        of((carried, width), F32), tall, tall, tall, tall, tall, tall,
+        ((depth, 4 * width), BF), ((depth, width), BF), ((rows, depth), BF), slim, slim, slim, slim,
+        tall, tall, ((rows, rows), F32), ((carried, width), F32), tall, tall, tall, tall, tall, tall,
     )
 
 
 VMEM = pl.BlockSpec(memory_space=pltpu.VMEM)
 SMEM = pl.BlockSpec(memory_space=pltpu.SMEM)
-
-
-def attend_forward(deal, found, lengths, x_all, gain, w_all, wb_all, taps):
-    rows, depth = x_all.shape
-    width = w_all.shape[1] // 4
+AWAY = pl.BlockSpec(memory_space=pl.ANY)
+LIMIT = pltpu.CompilerParams(vmem_limit_bytes=56 * 1024 * 1024)
+
+
+def attend_forward(deal, spot, slot, lengths, x_parts, gain, w_parts, taps):
+    piece, depth = x_parts[0].shape
+    rows = piece * deal.shape[1]
+    width = taps.shape[1]
     saved = saved_shapes(rows, depth, width)
     return pl.pallas_call(
-        forward_kernel,
-        out_shape=(jax.ShapeDtypeStruct((rows, width), BF),) + saved,
-        in_specs=[SMEM, SMEM, SMEM] + [VMEM] * 5,
-        out_specs=tuple([VMEM] * (1 + len(saved))),
-        scratch_shapes=[pltpu.VMEM((rows, 4 * width), F32), pltpu.VMEM((rows, rows), F32)],
-        compiler_params=pltpu.CompilerParams(vmem_limit_bytes=48 * 1024 * 1024),
+        functools.partial(forward_kernel, len(x_parts), len(w_parts)),
+        out_shape=(jax.ShapeDtypeStruct((rows, width), BF),)
+        + tuple(jax.ShapeDtypeStruct(*entry) for entry in saved),
+        in_specs=[SMEM] * 4 + [VMEM] * (len(x_parts) + len(w_parts) + 2),
+        out_specs=(VMEM,) + (AWAY,) * SAVED,
+        scratch_shapes=[pltpu.VMEM(*entry) for entry in saved]
+        + [
+            pltpu.VMEM((rows, 4 * width), F32),
+            pltpu.VMEM((rows, rows), F32),
+            pltpu.SemaphoreType.DMA((SAVED,)),
+        ],
+        compiler_params=LIMIT,
         name="attend_forward",
-    )(deal, found, lengths, x_all, gain, w_all, wb_all, taps)
-
-
-def attend_backward(deal, place, lengths, live, d_out, h1, w_all, wb_all, taps, saved):
+    )(deal, spot, slot, lengths, *x_parts, gain, *w_parts, taps)
+
+
+def attend_backward(deal, place, lengths, live, d_out, taps, depth, kept):
     rows, width = d_out.shape
-    depth = h1.shape[1]
+    saved = saved_shapes(rows, depth, width)
     return pl.pallas_call(
         backward_kernel,
         out_shape=(
             jax.ShapeDtypeStruct((rows, depth), BF),
-            jax.ShapeDtypeStruct((depth, 4 * width), BF),
-            jax.ShapeDtypeStruct((depth, width), F32),
+            jax.ShapeDtypeStruct((rows, 5 * width), BF),
+            jax.ShapeDtypeStruct((8, depth), F32),
             jax.ShapeDtypeStruct((taps.shape[0], width), F32),
         ),
-        in_specs=[SMEM, SMEM, SMEM, SMEM] + [VMEM] * (5 + len(saved)),
-        out_specs=(VMEM, VMEM, VMEM, VMEM),
-        scratch_shapes=[
+        in_specs=[SMEM] * 4 + [VMEM] * 2 + [AWAY] * SAVED,
+        out_specs=(VMEM,) * 4,
+        scratch_shapes=[pltpu.VMEM(*entry) for entry in saved]
+        + [
             pltpu.VMEM((rows, rows), F32),
             pltpu.VMEM((rows, width), BF),
             pltpu.VMEM((rows, width), F32),
             pltpu.VMEM((rows, width), F32),
             pltpu.VMEM((rows, width), F32),
             pltpu.VMEM((rows, width), F32),
-            pltpu.VMEM((rows, 5 * width), BF),
+            pltpu.SemaphoreType.DMA((SAVED,)),
         ],
-        compiler_params=pltpu.CompilerParams(vmem_limit_bytes=56 * 1024 * 1024),
+        compiler_params=LIMIT,
         name="attend_backward",
-    )(deal, place, lengths, live, d_out, h1, w_all, wb_all, taps, *saved)
+    )(deal, place, lengths, live, d_out, taps, *kept)
 
 
 def steps_of(axis, descending):
@@ -437,13 +492,48 @@
     return value
 
 
+def in_order(mine, other):
+    first = lax.axis_index("shard") == 0
+    return jnp.stack([jnp.where(first, mine, other), jnp.where(first, other, mine)])
+
+
 def over_shard(value):
-    size = lax.axis_size("shard")
-    if size == 2:
-        other = swap(value, "shard", 1)
-        mine = lax.axis_index("shard") == 0
-        return jnp.stack([jnp.where(mine, value, other), jnp.where(mine, other, value)])
+    if lax.axis_size("shard") == 2:
+        return in_order(value, swap(value, "shard", 1))
     return lax.all_gather(value, "shard", axis=0, tiled=False)
+
+
+def across_shard(parts):
+    if lax.axis_size("shard") == 2:
+        shard = lax.axis_index("shard")
+        mine = lax.dynamic_index_in_dim(parts, shard, axis=0, keepdims=False)
+        sent = lax.dynamic_index_in_dim(parts, 1 - shard, axis=0, keepdims=False)
+        return in_order(mine, swap(sent, "shard", 1))
+    return deal_out(parts, "shard")
+
+
+def sum_shard(parts):
+    if lax.axis_size("shard") == 2:
+        shard = lax.axis_index("shard")
+        mine = lax.dynamic_index_in_dim(parts, shard, axis=0, keepdims=False)
+        sent = lax.dynamic_index_in_dim(parts, 1 - shard, axis=0, keepdims=False)
+        return mine.astype(F32) + swap(sent, "shard", 1).astype(F32)
+    return jnp.sum(deal_out(parts, "shard").astype(F32), axis=0)
+
+
+def over_ctx(value):
+    ranks = lax.axis_size("ctx")
+    got = [value] + [
+        lax.ppermute(value, "ctx", [(i, (i + k) % ranks) for i in range(ranks)])
+        for k in range(1, ranks)
+    ]
+    return got
+
+
+def sum_over(value, steps):
+    for axis, bit in steps:
+        value = value + swap(value, axis, bit)
+    return value
 
 
 def deal_out(value, axis):
@@ -476,35 +566,53 @@
     live = (rank < heads).astype(jnp.int32).reshape(1, 1)
     head_at = jnp.minimum(rank, heads - 1)
 
-    half = lane % 2
-    own = lax.dynamic_slice_in_dim(tokens, half * piece, piece, axis=0)
-    near = [own] + [
-        lax.ppermute(own, "ctx", [(i, (i + k) % ranks) for i in range(ranks)])
-        for k in range(1, ranks)
-    ]
-    near = jnp.concatenate(near, axis=0)
-    x_all = jnp.concatenate([near, swap(near, "tp", 1)], axis=0)
-    owner = deal // 2
-    found = jnp.where(deal % 2 == half, 0, ranks) + (rank - owner) % ranks
-
     blocks = jnp.stack([w_query, w_key, w_value, w_house]).reshape(4, share, heads, width)
     blocks = blocks.transpose(2, 1, 0, 3).reshape(heads, share, 4 * width)
     beta_rows = jnp.pad(w_beta.T.reshape(heads, 1, share), ((0, 0), (0, 15), (0, 4 * width - share)))
     blocks = jnp.pad(jnp.concatenate([blocks, beta_rows], axis=1), ((0, spare), (0, 0), (0, 0)))
-    blocks = over_shard(deal_out(blocks, "ctx"))
-    w_all = blocks[:, :, :share].reshape(depth, 4 * width)
-    wb_all = jnp.pad(blocks[:, :, share, :share].reshape(depth, 1), ((0, 0), (0, width - 1)))
+    crossed, slots_of = [], []
+    for k in range(ranks):
+        block = lax.dynamic_index_in_dim(blocks, (rank + k) % ranks, axis=0, keepdims=False)
+        if k:
+            block = lax.ppermute(
+                block, "ctx",
+                [(i, (i + k) % ranks) for i in range(ranks) if (i + k) % ranks < heads],
+            )
+        crossed.append(block)
     taps = lax.dynamic_slice_in_dim(conv_taps, head_at * width, width, axis=1)
 
-    def fetch(weight):
-        parts = weight.reshape(share, shards, part).transpose(1, 0, 2)
-        rows = deal_out(parts, "shard").reshape(shards * share, part)
-        return lax.all_gather(rows, "ctx", axis=0, tiled=True)
-
-    wo_t = lax.all_gather(w_out.T, ("shard", "ctx"), axis=0, tiled=True)
-    wg_all = fetch(w_gate)
-    wu_all = fetch(w_up)
-    wd_all = fetch(w_down.T)
+    half = lane % 2
+    own = lax.dynamic_slice_in_dim(tokens, half * piece, piece, axis=0)
+    near = over_ctx(own)
+    owners = (rank - jnp.arange(ranks, dtype=jnp.int32)) % ranks
+    held = jnp.concatenate([2 * owners + half, 2 * owners + 1 - half])
+    labels = jnp.arange(2 * ranks, dtype=jnp.int32)
+    spot = jnp.sum(jnp.where(deal[0][None, :] == held[:, None], labels[None, :], 0), axis=1)[None]
+
+    def parted(weight):
+        return weight.reshape(share, shards, part).transpose(1, 0, 2)
+
+    wo_rows = over_shard(w_out.T)
+    hidden = jnp.concatenate([parted(w_gate), parted(w_up), parted(w_down.T)], axis=2)
+    hidden = across_shard(hidden).reshape(shards * share, 3 * part)
+    hidden, near, crossed = lax.optimization_barrier((hidden, near, crossed))
+    hidden = lax.all_gather(hidden, "ctx", axis=0, tiled=True)
+    wg_all, wu_all, wd_all = (hidden[:, i * part:(i + 1) * part] for i in range(3))
+    x_parts = list(near) + [swap(part_, "tp", 1) for part_ in near]
+    w_parts = []
+    for k, block in enumerate(crossed):
+        source = (rank - k) % ranks
+        if shards == 2:
+            w_parts += [block, swap(block, "shard", 1)]
+            slots_of += [shard * ranks + source, (1 - shard) * ranks + source]
+        else:
+            every = lax.all_gather(block, "shard", axis=0, tiled=False)
+            w_parts += [every[i] for i in range(shards)]
+            slots_of += [i * ranks + source for i in range(shards)]
+    slot = jnp.stack(slots_of)[None]
+    wo_near = jnp.stack(over_ctx(wo_rows))
+    wo_t = jnp.take(wo_near, (rank - jnp.arange(ranks)) % ranks, axis=0)
+    wo_t = wo_t.transpose(1, 0, 2, 3).reshape(depth, columns)
 
     def to_plane(value):
         value = value.reshape(-1, shards, ranks, share).transpose(0, 2, 1, 3)
@@ -520,8 +628,9 @@
     grad_own = my_rows(cotangent)
     grad_plane = spread_rows(to_plane(grad_own), plane_steps)
 
-    fwd = attend_forward(deal, found, lengths, x_all, attn_gain[None], w_all, wb_all, taps)
-    head_out, h1, saved = fwd[0], fwd[1], fwd[2:]
+    fwd = attend_forward(deal, spot, slot, lengths, x_parts, attn_gain[None], w_parts, taps)
+    head_out, saved = fwd[0], fwd[1:]
+    h1 = saved[2]
     slots = jnp.arange(lanes, dtype=jnp.int32)
     order = jnp.full_like(slots, lane)
     for index, (_, bit) in enumerate(tp_steps):
@@ -545,20 +654,21 @@
     d_act = dg(grad_plane, wd_all, 1, 0)
     d_gate = (d_act * up * sig * (1.0 + gate * (1.0 - sig))).astype(BF)
     d_up = (d_act * swish).astype(BF)
-    d_two = gather_rows(dg(d_gate, wg_all, 1, 1) + dg(d_up, wu_all, 1, 1), plane_steps)
+    d_two = dg(d_gate, wg_all, 1, 1) + dg(d_up, wu_all, 1, 1)
+    d_two = gather_rows(d_two, plane_steps[-1:])
+    down_grad = dg(grad_plane, act, 0, 0).astype(BF)
+    pair_grad = dg(h2, jnp.concatenate([d_gate, d_up], axis=1), 0, 0).astype(BF)
+    d_two, down_grad, pair_grad = lax.optimization_barrier((d_two, down_grad, pair_grad))
+    down_sum = lax.psum_scatter(down_grad, "ctx", scatter_dimension=0, tiled=True)
+    pair_sum = lax.psum_scatter(pair_grad, "ctx", scatter_dimension=0, tiled=True)
+    d_two = gather_rows(d_two, plane_steps[:-1])
     d_two = from_plane(d_two)
-    mlp = from_plane(gather_rows(dg(act, wd_all, 1, 1), plane_steps))
-    result = middle + mlp
-
-    def give_back(left, right):
-        grad = dg(left, right, 0, 0).astype(BF)
-        grad = lax.psum_scatter(grad, "ctx", scatter_dimension=0, tiled=True)
-        grad = deal_out(grad.reshape(shards, share, part), "shard")
-        return grad.transpose(1, 0, 2).reshape(share, shards * part).astype(F32)
-
-    d_wgate = give_back(h2, d_gate)
-    d_wup = give_back(h2, d_up)
-    d_wdown = give_back(grad_plane, act).T
+
+    def give_back(grad):
+        count = grad.shape[1] // part
+        grad = across_shard(grad.reshape(shards, share, count * part))
+        grad = grad.reshape(shards, share, count, part).transpose(2, 1, 0, 3)
+        return grad.reshape(count, share, shards * part).astype(F32)
 
     d_gain_two = jnp.sum(d_two * middle * inv_two, axis=0)
     d_middle = grad_own.astype(F32) + norm_back(middle, inv_two, gain_two, d_two)
@@ -569,48 +679,74 @@
         natural = natural + jnp.where(((slots ^ lane) & bit) != 0, 1 << index, 0)
     d_heads = jnp.take(d_heads, natural, axis=0).transpose(2, 0, 1, 3).reshape(heads, span, width)
     d_heads = deal_out(jnp.pad(d_heads, ((0, spare), (0, 0), (0, 0))), "ctx")
-    d_wout = dg(d_attn, o_rows, 0, 0).astype(BF)
-    d_wout = lax.psum_scatter(d_wout, ("shard", "ctx"), scatter_dimension=0, tiled=True)
-    d_wout = d_wout.astype(F32).T
-
     given = jnp.arange(group // small, dtype=jnp.int32)
     apart = (given % lanes) ^ lane
     turned = jnp.zeros_like(apart)
     for index, (_, bit) in enumerate(tp_steps):
         turned = turned + jnp.where((apart & bit) != 0, 1 << index, 0)
     place = (turned * ranks + given // lanes)[None]
-    d_one, d_w, d_b, d_taps = attend_backward(
-        deal, place, lengths, live, d_heads.reshape(group, width), h1, w_all, wb_all, taps, saved
-    )
-    d_one = gather_rows(d_one, tp_steps)
-    d_one = deal_out(d_one.astype(BF).reshape(ranks, small, depth), "ctx")
-    d_one = jnp.sum(d_one.astype(F32), axis=0)
+    d_one, d_proj, d_small, d_taps = attend_backward(
+        deal, place, lengths, live, d_heads.reshape(group, width), taps, depth, saved
+    )
     gain_one = attn_gain.astype(F32)
-    inv_one = lax.rsqrt(jnp.mean(x_own * x_own, axis=1, keepdims=True) + EPS)
-    d_gain_one = jnp.sum(d_one * x_own * inv_one, axis=0)
-    d_input = d_middle + norm_back(x_own, inv_one, gain_one, d_one)
-    d_tokens = lax.all_gather(d_input.astype(BF), "tp", axis=0, tiled=True)
-    output = lax.all_gather(result.astype(BF), "tp", axis=0, tiled=True)
-
-    d_w = deal_out(d_w.reshape(shards, ranks * share, 4 * width), "shard")
-    d_w = jnp.sum(d_w.astype(F32), axis=0).astype(BF)
-    d_w = deal_out(d_w.reshape(ranks, share, 4 * width), "ctx")[:heads].astype(F32)
-    d_w = d_w.reshape(heads, share, 4, width).transpose(2, 1, 0, 3).reshape(4, share, columns)
-
+    mine = (jnp.arange(heads) == rank).astype(F32)
+    taps_part = (mine[None, :, None] * d_taps[:, None]).reshape(conv_taps.shape)
+    taps_part = jnp.pad(taps_part, ((0, 0), (0, depth - columns)))
+    sums = jnp.concatenate(
+        [d_small[:1], d_gain_two[None], mine[:, None] * d_small[1][None], taps_part], axis=0
+    )
+    sum_steps = steps_of("ctx", False) + steps_of("shard", False)
+
+    d_one = gather_rows(d_one, tp_steps[-1:])
+    mlp = dg(act, wd_all, 1, 1)
+    mlp = gather_rows(mlp, plane_steps[-1:])
+    sums = sum_over(sums, sum_steps[:1])
+    d_one, mlp, sums, d_proj, d_attn = lax.optimization_barrier((d_one, mlp, sums, d_proj, d_attn))
+
+    d_one = gather_rows(d_one, tp_steps[:-1]).astype(BF).reshape(ranks, small, depth)
+    d_w = dg(h1, d_proj[:, :4 * width], 0, 0).astype(BF)
+    d_w = sum_shard(d_w.reshape(shards, ranks * share, 4 * width)).astype(BF)
+    d_wout = dg(d_attn, o_rows, 0, 0).astype(BF)
+    d_wout = sum_shard(d_wout.reshape(shards, ranks * share, columns)).astype(BF)
+    sums = sum_over(sums, sum_steps[1:2])
+    d_one, d_w, d_wout, mlp, sums = lax.optimization_barrier((d_one, d_w, d_wout, mlp, sums))
+
+    total = lax.dynamic_index_in_dim(d_one, rank, axis=0, keepdims=False).astype(F32)
+    for k in range(1, ranks):
+        sent = lax.dynamic_index_in_dim(d_one, (rank + k) % ranks, axis=0, keepdims=False)
+        got = lax.ppermute(sent, "ctx", [(i, (i + k) % ranks) for i in range(ranks)])
+        total = total + got.astype(F32)
+    d_one = total
+    mlp = from_plane(gather_rows(mlp, plane_steps[:-1]))
+    result = middle + mlp
     mask = my_rows(valid_mask).astype(F32)
     totals = jnp.stack(
         [jnp.sum(mask * jnp.sum(b * b, axis=1)) for b in (x_own, attn, mlp, result)]
         + [jnp.sum(mask)]
     )
-    mine = (jnp.arange(heads) == rank).astype(F32)
-    beta_part = mine[:, None] * d_b[:, 0][None]
-    taps_part = mine[:, None, None] * d_taps[None]
-    beta_sum, taps_sum, one_sum, two_sum, totals = lax.psum(
-        (beta_part, taps_part, d_gain_one, d_gain_two, totals), ("shard", "ctx")
-    )
-    one_sum, two_sum, totals = lax.psum((one_sum, two_sum, totals), "tp")
+    sums = sum_over(sums, sum_steps[2:])
+    d_one, result, sums, d_w, d_wout, totals, down_sum, pair_sum = lax.optimization_barrier(
+        (d_one, result, sums, d_w, d_wout, totals, down_sum, pair_sum)
+    )
+
+    inv_one = lax.rsqrt(jnp.mean(x_own * x_own, axis=1, keepdims=True) + EPS)
+    d_input = d_middle + norm_back(x_own, inv_one, gain_one, d_one)
+    ends = jnp.stack([d_input.astype(BF), result.astype(BF)], axis=1)
+    ends = spread_rows(ends, tp_steps).reshape(lanes, small, 2, depth)
+    ends = jnp.take(ends, natural, axis=0).reshape(span, 2, depth)
+    d_tokens, output = ends[:, 0], ends[:, 1]
+    d_w = deal_out(d_w.reshape(ranks, share, 4 * width), "ctx")[:heads].astype(F32)
+    d_w = d_w.reshape(heads, share, 4, width).transpose(2, 1, 0, 3).reshape(4, share, columns)
+    d_wout = deal_out(d_wout.reshape(ranks, share, columns), "ctx")
+    d_wout = jnp.sum(d_wout.astype(F32), axis=0).T
+    d_wdown = give_back(down_sum)[0].T
+    d_wgate, d_wup = give_back(pair_sum)
+    one_two = sum_over(sums[:2], tp_steps)
+    totals = sum_over(totals[None], sum_steps + tp_steps)[0]
+    one_sum, two_sum = one_two[0] / gain_one, one_two[1]
+    beta_sum, taps_sum = sums[2:2 + heads], sums[2 + heads:]
     d_beta = lax.dynamic_slice_in_dim(beta_sum, (shard * ranks + rank) * share, share, axis=1).T
-    d_conv = taps_sum.transpose(1, 0, 2).reshape(conv_taps.shape)
+    d_conv = taps_sum[:, :columns]
     rms_stats = jnp.sqrt(totals[:4] / (jnp.maximum(totals[4], 1.0) * depth))
     return (
         output, d_tokens, one_sum, d_w[0], d_w[1], d_w[2], d_w[3], d_beta, d_conv,

time: 511 us -> 430 us (0.84)
  blocking collectives: 63.5 us -> 0 us
  local copies, waits for them, and re-layouts: 71.8 us -> 49.4 us
  waiting for transfers between devices: 189 us -> 196 us
  starting transfers between devices: 70.3 us -> 76.4 us
    ppermute x20 -> x44, waiting for transfers between devices: 52.9 us -> 105 us  [swap(): return lax.ppermute(value, axis, [(i, i ^ bit) for i in range(size)])]
    psum x2 -> x0, blocking collectives: 47.9 us -> none  [the longest x1 37.1 us: local(): lax.psum((beta_part, taps_part, d_gain_one, d_gain_two, totals), ('shard'...]
    all_to_all x12 -> x4, starting transfers between devices: 46.9 us -> 16.1 us  [deal_out(): return lax.all_to_all(value, axis, split_axis=0, concat_axis=0, tiled=True)]
    ppermute x20 -> x44, starting transfers between devices: 17.9 us -> 42.8 us  [swap(): return lax.ppermute(value, axis, [(i, i ^ bit) for i in range(size)])]
    all_gather x4 -> x1, waiting for transfers between devices: 24.4 us -> 0.02 us  [local(): hidden = lax.all_gather(hidden, 'ctx', axis=0, tiled=True)]
    all_to_all x12 -> x4, waiting for transfers between devices: 49.4 us -> 29.6 us  [deal_out(): return lax.all_to_all(value, axis, split_axis=0, concat_axis=0, tiled=True)]
    unnamed x134 -> x112, local copies, waits for them, and re-layouts: 31.9 us -> 13.6 us
    all_gather x2 -> x0, blocking collectives: 15.5 us -> none  [the longest x1 7.95 us: local(): output = lax.all_gather(result.astype(BF), 'tp', axis=0, tiled=True)]
  transfers between devices with their start and end apart: 43 -> 63, of which waited for: 22 -> 34; matrix products, arithmetic and copies ran while one was open for 19% -> 17% of each run, Pallas kernels for 8% -> 9%
where the time goes in v2:
time: 430 us; the launch traced here: 421 us
  waiting for transfers between devices  196 us (46%)
  starting transfers between devices  76.4 us (18%)
  local copies, waits for them, and re-layouts  49.4 us (11%)
  Pallas kernels  37.7 us (9%)
  other arithmetic  24.9 us (6%)
  matrix products  20.7 us (5%)
  between operations  16.2 us (4%)
    ppermute x44, waiting for transfers between devices, swap(): return lax.ppermute(value, axis, [(i, i ^ bit) for i in range(size)])  105 us
    ppermute x44, starting transfers between devices, swap(): return lax.ppermute(value, axis, [(i, i ^ bit) for i in range(size)])  42.8 us
    ppermute x6, waiting for transfers between devices, over_ctx(): lax.ppermute(value, 'ctx', [(i, (i + k) % ranks) for i in range(ranks)])  29.7 us
    all_to_all x4, waiting for transfers between devices, deal_out(): return lax.all_to_all(value, axis, split_axis=0, concat_axis=0, tiled=True)  29.6 us
    ppermute x3, waiting for transfers between devices, local(): lax.ppermute(block, 'ctx', [(i, (i + k) % ranks) for i in range(ranks) if...  25.9 us
    dot_general x12, matrix products, dg(): lax.dot_general(left, right, (((cl,), (cr,)), ((), ())), preferred_elemen...  20.7 us
    pallas_call x1, Pallas kernels, attend_backward(): pl.pallas_call(backward_kernel, out_shape=(jax.ShapeDtypeStruct((rows, de...  20.3 us
    pallas_call x1, Pallas kernels, attend_forward(): pl.pallas_call(functools.partial(forward_kernel, len(x_parts), len(w_part...  17.4 us
  transfers between devices with their start and end apart: 63, of which 34 were waited for; matrix products, arithmetic and copies ran while one was open for 17% of the time, Pallas kernels for 9%

profile of v2, /device:TPU:0, one launch (start us, length us, event | category | flops | bytes accessed | tf_op | source)
XLA Modules:
  0.0 421.2 jit_solution(6345122461682222434)
XLA Ops:
  11.3 2.4 constant_dynamic-slice_fusion.4
  13.9 3.0 collective-permute-start
  18.6 2.6 collective-permute-start.2
  24.6 2.6 collective-permute-start.4
  27.2 3.2 collective-permute-done
  30.3 4.7 %collective-permute-start.5 = (bf16[208,512]{1,0:T(8,128)(2,1)S(1)}, bf16[208,512]{1,0:T(8,128)(2,1)S(1)}, u32[]{:S(2)}, u32[]{:S(2)}) collective-permute-start(bf16[208,512]{1,0:T(8,128)(2,1)S(1)} %get-tuple-element.155), channel_id=1, source_target_pairs={{0,8},{8,0},{12,4},{1,9},{9,1},{13,5},{2,10},{10,2},{14,6},{3,11},... | collective-permute-start | bytes 638984 | tf_op jit(solution)/shard_map/ppermute | solution.py:577
  36.3 9.9 %collective-permute-done.4.refs_15_ = bf16[208,512]{1,0:T(8,128)(2,1)S(1)} collective-permute-done((bf16[208,512]{1,0:T(8,128)(2,1)S(1)}, bf16[208,512]{1,0:T(8,128)(2,1)S(1)}, u32[]{:S(2)}, u32[]{:S(2)}) %collective-permute-start.4) | collective-permute-done | bytes 213024 | tf_op jit(solution)/shard_map/ppermute | solution.py:577
  48.6 11.6 %collective-permute-done.5.refs_17_ = bf16[208,512]{1,0:T(8,128)(2,1)S(1)} collective-permute-done((bf16[208,512]{1,0:T(8,128)(2,1)S(1)}, bf16[208,512]{1,0:T(8,128)(2,1)S(1)}, u32[]{:S(2)}, u32[]{:S(2)}) %collective-permute-start.5) | collective-permute-done | bytes 213024 | tf_op jit(solution)/shard_map/ppermute | solution.py:577
  60.2 4.4 %collective-permute-done.6.refs_19_ = bf16[208,512]{1,0:T(8,128)(2,1)S(1)} collective-permute-done((bf16[208,512]{1,0:T(8,128)(2,1)S(1)}, bf16[208,512]{1,0:T(8,128)(2,1)S(1)}, u32[]{:S(2)}, u32[]{:S(2)}) %collective-permute-start.6) | collective-permute-done | bytes 213024 | tf_op jit(solution)/shard_map/ppermute | solution.py:577
  72.9 2.7 collective-permute-done.11.refs_14_
  77.1 3.1 collective-permute-done.12.refs_16_
  80.2 4.6 %collective-permute-done.13.refs_18_ = bf16[208,512]{1,0:T(8,128)(2,1)S(1)} collective-permute-done((bf16[208,512]{1,0:T(8,128)(2,1)S(1)}, bf16[208,512]{1,0:T(8,128)(2,1)S(1)}, u32[]{:S(2)}, u32[]{:S(2)}) %collective-permute-start.13) | collective-permute-done | bytes 213024 | tf_op jit(solution)/shard_map/ppermute | solution.py:479
  84.8 4.0 collective-permute-done.14.refs_20_
  93.4 17.4 %attend_forward.1 = (bf16[768,128]{1,0:T(8,128)(2,1)}, bf16[1536,512]{1,0:T(8,128)(2,1)}, bf16[1536,128]{1,0:T(8,128)(2,1)}, bf16[768,1536]{1,0:T(8,128)(2,1)}, ...) custom-call(s32[1,8]{1,0:T(1,128)} %refs_0_.3, ...), custom_call_target="tpu_custom_call" | custom-call | tf_op jit(solution)/shard_map/attend_forward/pallas_call | solution.py:422
  110.8 4.6 %all-to-all-start = ((bf16[4,192,128]{2,1,0:T(8,128)(2,1)}), bf16[4,192,128]{2,1,0:T(8,128)(2,1)S(1)}, u32[]{:S(2)}, u32[]{:S(2)}) async-start(bf16[4,192,128]{2,1,0:T(8,128)(2,1)} %bitcast.269), calls=%async_computation | async-start | bytes 393216 | tf_op jit(solution)/shard_map/all_to_all | solution.py:540
  115.6 29.7 %collective-permute-done.17 = bf16[2,192,384]{2,1,0:T(8,128)(2,1)S(1)} collective-permute-done((bf16[2,192,384]{2,1,0:T(8,128)(2,1)S(1)}, bf16[2,192,384]{2,1,0:T(8,128)(2,1)S(1)}, u32[]{:S(2)}, u32[]{:S(2)}) %collective-permute-start.17) | collective-permute-done | bytes 294944 | tf_op jit(solution)/shard_map/ppermute | solution.py:527
  146.6 5.8 %all-to-all-done = bf16[4,192,128]{2,1,0:T(8,128)(2,1)S(1)} async-done(((bf16[4,192,128]{2,1,0:T(8,128)(2,1)}), bf16[4,192,128]{2,1,0:T(8,128)(2,1)S(1)}, u32[]{:S(2)}, u32[]{:S(2)}) %all-to-all-start) | async-done | bytes 196640 | tf_op jit(solution)/shard_map/all_to_all | solution.py:540
  157.1 7.4 %collective-permute-done.22 = bf16[96,1536]{1,0:T(8,128)(2,1)S(1)} collective-permute-done((bf16[96,1536]{1,0:T(8,128)(2,1)S(1)}, bf16[96,1536]{1,0:T(8,128)(2,1)S(1)}, u32[]{:S(2)}, u32[]{:S(2)}) %collective-permute-start.22) | collective-permute-done | bytes 294944 | tf_op jit(solution)/shard_map/ppermute | solution.py:479
  164.7 2.6 collective-permute-done.20
  171.2 3.5 collective-permute-done.24
  177.9 4.9 %collective-permute-done.25 = bf16[96,1536]{1,0:T(8,128)(2,1)S(1)} collective-permute-done((bf16[96,1536]{1,0:T(8,128)(2,1)S(1)}, bf16[96,1536]{1,0:T(8,128)(2,1)S(1)}, u32[]{:S(2)}, u32[]{:S(2)}) %collective-permute-start.25) | collective-permute-done | bytes 294944 | tf_op jit(solution)/shard_map/ppermute | solution.py:479
  185.0 2.6 fusion.3
  193.3 2.2 convolution_convert_fusion.2
  195.5 5.0 %convolution_convert_fusion = bf16[1536,1024]{1,0:T(8,128)(2,1)} fusion(bf16[384,1536]{1,0:T(8,128)(2,1)} %copy-done.43, bf16[384,512]{1,0:T(8,128)(2,1)} %copy-done.21, bf16[384,512]{1,0:T(8,128)(2,1)} %copy-done.20), kind=kOutput, calls=%fused_computation.4 | convolution fusion | flops 1211105280 | bytes 5111808 | tf_op jit(solution)/shard_map/dot_general | solution.py:18
  204.4 7.5 %collective-permute-done.28 = bf16[96,1536]{1,0:T(8,128)(2,1)S(1)} collective-permute-done((bf16[96,1536]{1,0:T(8,128)(2,1)S(1)}, bf16[96,1536]{1,0:T(8,128)(2,1)S(1)}, u32[]{:S(2)}, u32[]{:S(2)}) %collective-permute-start.28) | collective-permute-done | bytes 294944 | tf_op jit(solution)/shard_map/ppermute | solution.py:479
  213.5 3.7 collective-permute-done.29
  220.8 3.6 collective-permute-done.30
  225.2 2.4 fusion.8
  229.5 2.5 convolution_convert_fusion.4
  236.2 3.8 all-to-all-start.1
  240.0 2.2 slice_add_fusion
  242.3 8.2 %all-to-all-done.1 = bf16[4,192,128]{2,1,0:T(8,128)(2,1)S(1)} async-done(((bf16[4,192,128]{2,1,0:T(8,128)(2,1)}), bf16[4,192,128]{2,1,0:T(8,128)(2,1)S(1)}, u32[]{:S(2)}, u32[]{:S(2)}) %all-to-all-start.1) | async-done | bytes 196640 | tf_op jit(solution)/shard_map/all_to_all | solution.py:540
  251.1 20.3 %attend_backward.1 = (bf16[768,1536]{1,0:T(8,128)(2,1)}, bf16[768,640]{1,0:T(8,128)(2,1)}, f32[8,1536]{1,0:T(8,128)}, f32[4,128]{1,0:T(4,128)}) custom-call(s32[1,8]{1,0:T(1,128)} %refs_0_.3, s32[1,16]{1,0:T(1,128)} %fusion.43.refs_1_, s32[1,3]{1,0:T(1,128)} %refs_2_.1, s32[1,1]{1,0:T(1,128)} %bitcast.41.refs_3_, bf16[768,128]{1,0:T(8,128)(2,1)} %bitcast.255, ...), custom_call_target="tpu_custom_call" | custom-call | tf_op jit(solution)/shard_map/attend_backward/pallas_call | solution.py:442
  275.8 8.7 %collective-permute-done.34 = f32[9,1536]{1,0:T(8,128)S(1)} collective-permute-done((f32[9,1536]{1,0:T(8,128)S(1)}, f32[9,1536]{1,0:T(8,128)S(1)}, u32[]{:S(2)}, u32[]{:S(2)}) %collective-permute-start.34) | collective-permute-done | bytes 55328 | tf_op jit(solution)/shard_map/ppermute | solution.py:479
  285.0 3.7 collective-permute-start.35
  293.1 9.6 %collective-permute-done.38 = f32[9,1536]{1,0:T(8,128)S(1)} collective-permute-done((f32[9,1536]{1,0:T(8,128)S(1)}, f32[9,1536]{1,0:T(8,128)S(1)}, u32[]{:S(2)}, u32[]{:S(2)}) %collective-permute-start.38) | collective-permute-done | bytes 55328 | tf_op jit(solution)/shard_map/ppermute | solution.py:479
  302.7 3.0 collective-permute-done.37
  306.8 14.1 %collective-permute-done.36 = bf16[768,512]{1,0:T(8,128)(2,1)S(1)} collective-permute-done((bf16[768,512]{1,0:T(8,128)(2,1)S(1)}, bf16[768,512]{1,0:T(8,128)(2,1)S(1)}, u32[]{:S(2)}, u32[]{:S(2)}) %collective-permute-start.36) | collective-permute-done | bytes 786464 | tf_op jit(solution)/shard_map/ppermute | solution.py:479
  325.1 2.2 collective-permute-done.44
  327.3 2.3 collective-permute-done.42
  330.4 5.4 %collective-permute-done.40 = bf16[48,1536]{1,0:T(8,128)(2,1)S(1)} collective-permute-done((bf16[48,1536]{1,0:T(8,128)(2,1)S(1)}, bf16[48,1536]{1,0:T(8,128)(2,1)S(1)}, u32[]{:S(2)}, u32[]{:S(2)}) %collective-permute-start.40) | collective-permute-done | bytes 147488 | tf_op jit(solution)/shard_map/ppermute | solution.py:717
  338.0 3.3 stack.150
  344.4 3.8 all-to-all-start.3
  353.1 4.5 %collective-permute-done.51 = f32[1,5]{1,0:T(1,128)S(1)} collective-permute-done((f32[1,5]{1,0:T(1,128)S(1)}, f32[1,5]{1,0:T(1,128)S(1)}, u32[]{:S(2)}, u32[]{:S(2)}) %collective-permute-start.51) | collective-permute-done | bytes 52 | tf_op jit(solution)/shard_map/ppermute | solution.py:479
  357.6 4.4 %collective-permute-start.52 = (f32[1,5]{1,0:T(1,128)S(1)}, f32[1,5]{1,0:T(1,128)S(1)}, u32[]{:S(2)}, u32[]{:S(2)}) collective-permute-start(f32[1,5]{1,0:T(1,128)S(1)} %bitcast_add_fusion), channel_id=1, source_target_pairs={{0,8},{4,12},{8,0},{12,4},{1,9},{5,13},{9,1},{13,5},{2,10},{6,14},... | collective-permute-start | bytes 68 | tf_op jit(solution)/shard_map/ppermute | solution.py:479
  368.7 2.2 collective-permute-done.54
  384.7 4.0 all-to-all-start.2
  393.6 15.6 %all-to-all-done.2 = bf16[4,192,512]{2,1,0:T(8,128)(2,1)S(1)} async-done(((bf16[4,192,512]{2,1,0:T(8,128)(2,1)}), bf16[4,192,512]{2,1,0:T(8,128)(2,1)S(1)}, u32[]{:S(2)}, u32[]{:S(2)}) %all-to-all-start.2) | async-done | bytes 786464 | tf_op jit(solution)/shard_map/all_to_all | solution.py:540
  (373 shorter events, 119.6 us)
Async XLA Ops:
  7.2 177.8 %all-gather.2.cloned.1.call-start = ((), (), s32[]{:S(2)}) async-start(), calls=%async_computation.6 | async-start | bytes 5898240 | tf_op jit(solution)/shard_map/all_gather | solution.py:599
  13.9 16.4 %collective-permute-start = (bf16[192,1536]{1,0:T(8,128)(2,1)S(1)}, bf16[192,1536]{1,0:T(8,128)(2,1)}, u32[]{:S(2)}, u32[]{:S(2)}) collective-permute-start(bf16[192,1536]{1,0:T(8,128)(2,1)S(1)} %bitcast.256), channel_id=1, source_target_pairs={{0,16},{16,0},{1,17},{17,1},{2,18},{18,2},{3,19},{19,3},{4,20},{20... | collective-permute-start | bytes 1769480 | tf_op jit(solution)/shard_map/ppermute | solution.py:479
  16.9 47.6 %collective-permute-start.1 = (bf16[96,1536]{1,0:T(8,128)(2,1)S(1)}, bf16[96,1536]{1,0:T(8,128)(2,1)}, u32[]{:S(2)}, u32[]{:S(2)}) collective-permute-start(bf16[96,1536]{1,0:T(8,128)(2,1)S(1)} %constant_dynamic-slice_fusion.2.refs_4_), channel_id=1, source_target_pairs={{0,4},{4,8},{8,12},{12,0},{1,5},{5,9},{9,13},{13,1},{2,6},{6,10},{... | collective-permute-start | bytes 884744 | tf_op jit(solution)/shard_map/ppermute | solution.py:527
  18.6 46.0 %collective-permute-start.2 = (bf16[96,1536]{1,0:T(8,128)(2,1)S(1)}, bf16[96,1536]{1,0:T(8,128)(2,1)}, u32[]{:S(2)}, u32[]{:S(2)}) collective-permute-start(bf16[96,1536]{1,0:T(8,128)(2,1)S(1)} %constant_dynamic-slice_fusion.2.refs_4_), channel_id=1, source_target_pairs={{0,8},{4,12},{8,0},{12,4},{1,9},{5,13},{9,1},{13,5},{2,10},{6,14},... | collective-permute-start | bytes 884744 | tf_op jit(solution)/shard_map/ppermute | solution.py:527
  21.2 43.4 %collective-permute-start.3 = (bf16[96,1536]{1,0:T(8,128)(2,1)S(1)}, bf16[96,1536]{1,0:T(8,128)(2,1)}, u32[]{:S(2)}, u32[]{:S(2)}) collective-permute-start(bf16[96,1536]{1,0:T(8,128)(2,1)S(1)} %constant_dynamic-slice_fusion.2.refs_4_), channel_id=1, source_target_pairs={{0,12},{4,0},{8,4},{12,8},{1,13},{5,1},{9,5},{13,9},{2,14},{6,2},{... | collective-permute-start | bytes 884744 | tf_op jit(solution)/shard_map/ppermute | solution.py:527
  24.6 21.6 %collective-permute-start.4 = (bf16[208,512]{1,0:T(8,128)(2,1)S(1)}, bf16[208,512]{1,0:T(8,128)(2,1)S(1)}, u32[]{:S(2)}, u32[]{:S(2)}) collective-permute-start(bf16[208,512]{1,0:T(8,128)(2,1)S(1)} %get-tuple-element.154), channel_id=1, source_target_pairs={{0,4},{4,8},{12,0},{1,5},{5,9},{13,1},{2,6},{6,10},{14,2},{3,7},{7... | collective-permute-start | bytes 638984 | tf_op jit(solution)/shard_map/ppermute | solution.py:577
  30.3 29.8 %collective-permute-start.5 = (bf16[208,512]{1,0:T(8,128)(2,1)S(1)}, bf16[208,512]{1,0:T(8,128)(2,1)S(1)}, u32[]{:S(2)}, u32[]{:S(2)}) collective-permute-start(bf16[208,512]{1,0:T(8,128)(2,1)S(1)} %get-tuple-element.155), channel_id=1, source_target_pairs={{0,8},{8,0},{12,4},{1,9},{9,1},{13,5},{2,10},{10,2},{14,6},{3,11},... | collective-permute-start | bytes 638984 | tf_op jit(solution)/shard_map/ppermute | solution.py:577
  46.1 18.5 %collective-permute-start.6 = (bf16[208,512]{1,0:T(8,128)(2,1)S(1)}, bf16[208,512]{1,0:T(8,128)(2,1)S(1)}, u32[]{:S(2)}, u32[]{:S(2)}) collective-permute-start(bf16[208,512]{1,0:T(8,128)(2,1)S(1)} %get-tuple-element.153), channel_id=1, source_target_pairs={{4,0},{8,4},{12,8},{5,1},{9,5},{13,9},{6,2},{10,6},{14,10},{7,3},{... | collective-permute-start | bytes 638984 | tf_op jit(solution)/shard_map/ppermute | solution.py:577
  64.6 7.4 %collective-permute-start.15 = (bf16[192,384]{1,0:T(8,128)(2,1)S(1)}, bf16[192,384]{1,0:T(8,128)(2,1)S(1)}, u32[]{:S(2)}, u32[]{:S(2)}) collective-permute-start(bf16[192,384]{1,0:T(8,128)(2,1)S(1)} %bitcast.270), channel_id=1, source_target_pairs={{0,16},{16,0},{1,17},{17,1},{2,18},{18,2},{3,19},{19,3},{4,20},{20... | collective-permute-start | bytes 442376 | tf_op jit(solution)/shard_map/ppermute | solution.py:479
  67.4 8.2 %collective-permute-start.11 = (bf16[208,512]{1,0:T(8,128)(2,1)S(1)}, bf16[208,512]{1,0:T(8,128)(2,1)S(1)}, u32[]{:S(2)}, u32[]{:S(2)}) collective-permute-start(bf16[208,512]{1,0:T(8,128)(2,1)S(1)} %get-tuple-element.72.refs_13_), channel_id=1, source_target_pairs={{0,16},{16,0},{1,17},{17,1},{2,18},{18,2},{3,19},{19,3},{4,20},{20... | collective-permute-start | bytes 638984 | tf_op jit(solution)/shard_map/ppermute | solution.py:479
  70.3 19.5 %collective-permute-start.7 = (bf16[96,1536]{1,0:T(8,128)(2,1)S(1)}, bf16[96,1536]{1,0:T(8,128)(2,1)S(1)}, u32[]{:S(2)}, u32[]{:S(2)}) collective-permute-start(bf16[96,1536]{1,0:T(8,128)(2,1)S(1)} %constant_dynamic-slice_fusion.2.refs_4_), channel_id=1, source_target_pairs={{0,1},{1,0},{2,3},{3,2},{4,5},{5,4},{6,7},{7,6},{8,9},{9,8},{10,11... | collective-permute-start | bytes 884744 | tf_op jit(solution)/shard_map/ppermute | solution.py:479
  70.4 19.4 %collective-permute-start.8 = (bf16[96,1536]{1,0:T(8,128)(2,1)}, bf16[96,1536]{1,0:T(8,128)(2,1)S(1)}, u32[]{:S(2)}, u32[]{:S(2)}) collective-permute-start(bf16[96,1536]{1,0:T(8,128)(2,1)} %collective-permute-done.1.refs_5_), channel_id=1, source_target_pairs={{0,1},{1,0},{2,3},{3,2},{4,5},{5,4},{6,7},{7,6},{8,9},{9,8},{10,11... | collective-permute-start | bytes 884744 | tf_op jit(solution)/shard_map/ppermute | solution.py:479
  70.9 9.3 %collective-permute-start.12 = (bf16[208,512]{1,0:T(8,128)(2,1)S(1)}, bf16[208,512]{1,0:T(8,128)(2,1)S(1)}, u32[]{:S(2)}, u32[]{:S(2)}) collective-permute-start(bf16[208,512]{1,0:T(8,128)(2,1)S(1)} %collective-permute-done.4.refs_15_), channel_id=1, source_target_pairs={{0,16},{16,0},{1,17},{17,1},{2,18},{18,2},{3,19},{19,3},{4,20},{20... | collective-permute-start | bytes 638984 | tf_op jit(solution)/shard_map/ppermute | solution.py:479
  72.0 12.8 %collective-permute-start.13 = (bf16[208,512]{1,0:T(8,128)(2,1)S(1)}, bf16[208,512]{1,0:T(8,128)(2,1)S(1)}, u32[]{:S(2)}, u32[]{:S(2)}) collective-permute-start(bf16[208,512]{1,0:T(8,128)(2,1)S(1)} %collective-permute-done.5.refs_17_), channel_id=1, source_target_pairs={{0,16},{16,0},{1,17},{17,1},{2,18},{18,2},{3,19},{19,3},{4,20},{20... | collective-permute-start | bytes 638984 | tf_op jit(solution)/shard_map/ppermute | solution.py:479
  75.7 13.1 %collective-permute-start.14 = (bf16[208,512]{1,0:T(8,128)(2,1)S(1)}, bf16[208,512]{1,0:T(8,128)(2,1)S(1)}, u32[]{:S(2)}, u32[]{:S(2)}) collective-permute-start(bf16[208,512]{1,0:T(8,128)(2,1)S(1)} %collective-permute-done.6.refs_19_), channel_id=1, source_target_pairs={{0,16},{16,0},{1,17},{17,1},{2,18},{18,2},{3,19},{19,3},{4,20},{20... | collective-permute-start | bytes 638984 | tf_op jit(solution)/shard_map/ppermute | solution.py:479
  80.2 35.4 %collective-permute-start.18 = (bf16[2,192,384]{2,1,0:T(8,128)(2,1)S(1)}, bf16[2,192,384]{2,1,0:T(8,128)(2,1)S(1)}, u32[]{:S(2)}, u32[]{:S(2)}) collective-permute-start(bf16[2,192,384]{2,1,0:T(8,128)(2,1)S(1)} %get-tuple-element.164), channel_id=1, source_target_pairs={{0,12},{4,0},{8,4},{12,8},{1,13},{5,1},{9,5},{13,9},{2,14},{6,2},{... | collective-permute-start | bytes 884744 | tf_op jit(solution)/shard_map/ppermute | solution.py:527
  84.8 60.5 %collective-permute-start.17 = (bf16[2,192,384]{2,1,0:T(8,128)(2,1)S(1)}, bf16[2,192,384]{2,1,0:T(8,128)(2,1)S(1)}, u32[]{:S(2)}, u32[]{:S(2)}) collective-permute-start(bf16[2,192,384]{2,1,0:T(8,128)(2,1)S(1)} %get-tuple-element.164), channel_id=1, source_target_pairs={{0,8},{4,12},{8,0},{12,4},{1,9},{5,13},{9,1},{13,5},{2,10},{6,14},... | collective-permute-start | bytes 884744 | tf_op jit(solution)/shard_map/ppermute | solution.py:527
  88.7 56.5 %collective-permute-start.16 = (bf16[2,192,384]{2,1,0:T(8,128)(2,1)S(1)}, bf16[2,192,384]{2,1,0:T(8,128)(2,1)S(1)}, u32[]{:S(2)}, u32[]{:S(2)}) collective-permute-start(bf16[2,192,384]{2,1,0:T(8,128)(2,1)S(1)} %get-tuple-element.164), channel_id=1, source_target_pairs={{0,4},{4,8},{8,12},{12,0},{1,5},{5,9},{9,13},{13,1},{2,6},{6,10},{... | collective-permute-start | bytes 884744 | tf_op jit(solution)/shard_map/ppermute | solution.py:527
  91.6 63.0 %collective-permute-start.21 = (bf16[48,1536]{1,0:T(8,128)(2,1)S(1)}, bf16[48,1536]{1,0:T(8,128)(2,1)S(1)}, u32[]{:S(2)}, u32[]{:S(2)}) collective-permute-start(bf16[48,1536]{1,0:T(8,128)(2,1)S(1)} %reshape.428), channel_id=1, source_target_pairs={{0,16},{16,0},{1,17},{17,1},{2,18},{18,2},{3,19},{19,3},{4,20},{20... | collective-permute-start | bytes 442376 | tf_op jit(solution)/shard_map/ppermute | solution.py:479
  110.8 41.6 %all-to-all-start = ((bf16[4,192,128]{2,1,0:T(8,128)(2,1)}), bf16[4,192,128]{2,1,0:T(8,128)(2,1)S(1)}, u32[]{:S(2)}, u32[]{:S(2)}) async-start(bf16[4,192,128]{2,1,0:T(8,128)(2,1)} %bitcast.269), calls=%async_computation | async-start | bytes 393216 | tf_op jit(solution)/shard_map/all_to_all | solution.py:540
  115.4 225.9 %reduce-scatter.3.cloned.1.call-start = ((), (), s32[]{:S(2)}) async-start(), calls=%async_computation.7 | async-start | bytes 1966080 | tf_op jit(solution)/shard_map/reduce_scatter | solution.py:662
  154.7 9.9 %collective-permute-start.22 = (bf16[96,1536]{1,0:T(8,128)(2,1)S(1)}, bf16[96,1536]{1,0:T(8,128)(2,1)S(1)}, u32[]{:S(2)}, u32[]{:S(2)}) collective-permute-start(bf16[96,1536]{1,0:T(8,128)(2,1)S(1)} %pad_maximum_fusion.9), channel_id=1, source_target_pairs={{0,2},{1,3},{2,0},{3,1},{4,6},{5,7},{6,4},{7,5},{8,10},{9,11},{10,... | collective-permute-start | bytes 884744 | tf_op jit(solution)/shard_map/ppermute | solution.py:479
  156.3 11.0 %collective-permute-start.20 = (bf16[48,1536]{1,0:T(8,128)(2,1)S(1)}, bf16[48,1536]{1,0:T(8,128)(2,1)S(1)}, u32[]{:S(2)}, u32[]{:S(2)}) collective-permute-start(bf16[48,1536]{1,0:T(8,128)(2,1)S(1)} %slice.272), channel_id=1, source_target_pairs={{0,2},{1,3},{2,0},{3,1},{4,6},{5,7},{6,4},{7,5},{8,10},{9,11},{10,... | collective-permute-start | bytes 442376 | tf_op jit(solution)/shard_map/ppermute | solution.py:479
  164.6 12.5 %collective-permute-start.23 = (bf16[192,1536]{1,0:T(8,128)(2,1)S(1)}, bf16[192,1536]{1,0:T(8,128)(2,1)S(1)}, u32[]{:S(2)}, u32[]{:S(2)}) collective-permute-start(bf16[192,1536]{1,0:T(8,128)(2,1)S(1)} %pad_maximum_fusion.4), channel_id=1, source_target_pairs={{0,1},{1,0},{2,3},{3,2},{4,5},{5,4},{6,7},{7,6},{8,9},{9,8},{10,11... | collective-permute-start | bytes 1769480 | tf_op jit(solution)/shard_map/ppermute | solution.py:479
  174.8 8.0 %collective-permute-start.25 = (bf16[96,1536]{1,0:T(8,128)(2,1)S(1)}, bf16[96,1536]{1,0:T(8,128)(2,1)S(1)}, u32[]{:S(2)}, u32[]{:S(2)}) collective-permute-start(bf16[96,1536]{1,0:T(8,128)(2,1)S(1)} %pad_maximum_fusion.10), channel_id=1, source_target_pairs={{0,2},{1,3},{2,0},{3,1},{4,6},{5,7},{6,4},{7,5},{8,10},{9,11},{10,... | collective-permute-start | bytes 884744 | tf_op jit(solution)/shard_map/ppermute | solution.py:479
  192.1 8.4 %collective-permute-start.27 = (bf16[192,1536]{1,0:T(8,128)(2,1)S(1)}, bf16[192,1536]{1,0:T(8,128)(2,1)}, u32[]{:S(2)}, u32[]{:S(2)}) collective-permute-start(bf16[192,1536]{1,0:T(8,128)(2,1)S(1)} %slice.266), channel_id=1, source_target_pairs={{0,1},{1,0},{2,3},{3,2},{4,5},{5,4},{6,7},{7,6},{8,9},{9,8},{10,11... | collective-permute-start | bytes 1769480 | tf_op jit(solution)/shard_map/ppermute | solution.py:479
  202.8 9.1 %collective-permute-start.28 = (bf16[96,1536]{1,0:T(8,128)(2,1)S(1)}, bf16[96,1536]{1,0:T(8,128)(2,1)S(1)}, u32[]{:S(2)}, u32[]{:S(2)}) collective-permute-start(bf16[96,1536]{1,0:T(8,128)(2,1)S(1)} %slice.268), channel_id=1, source_target_pairs={{0,2},{1,3},{2,0},{3,1},{4,6},{5,7},{6,4},{7,5},{8,10},{9,11},{10,... | collective-permute-start | bytes 884744 | tf_op jit(solution)/shard_map/ppermute | solution.py:479
  204.3 137.0 %reduce-scatter.5.cloned.1.call-start = ((), (), s32[]{:S(2)}) async-start(), calls=%async_computation.8 | async-start | bytes 3932160 | tf_op jit(solution)/shard_map/reduce_scatter | solution.py:663
  228.5 11.6 %collective-permute-start.33 = (bf16[192,1536]{1,0:T(8,128)(2,1)}, bf16[192,1536]{1,0:T(8,128)(2,1)}, u32[]{:S(2)}, u32[]{:S(2)}) collective-permute-start(bf16[192,1536]{1,0:T(8,128)(2,1)} %slice.265), channel_id=1, source_target_pairs={{0,1},{1,0},{2,3},{3,2},{4,5},{5,4},{6,7},{7,6},{8,9},{9,8},{10,11... | collective-permute-start | bytes 1769480 | tf_op jit(solution)/shard_map/ppermute | solution.py:479
  236.2 14.2 %all-to-all-start.1 = ((bf16[4,192,128]{2,1,0:T(8,128)(2,1)}), bf16[4,192,128]{2,1,0:T(8,128)(2,1)S(1)}, u32[]{:S(2)}, u32[]{:S(2)}) async-start(bf16[4,192,128]{2,1,0:T(8,128)(2,1)} %pad.18), calls=%async_computation.1 | async-start | bytes 393216 | tf_op jit(solution)/shard_map/all_to_all | solution.py:540
  272.9 11.6 %collective-permute-start.32 = (bf16[384,1536]{1,0:T(8,128)(2,1)S(1)}, bf16[384,1536]{1,0:T(8,128)(2,1)S(1)}, u32[]{:S(2)}, u32[]{:S(2)}) collective-permute-start(bf16[384,1536]{1,0:T(8,128)(2,1)S(1)} %slice.157), channel_id=1, source_target_pairs={{0,1},{1,0},{2,3},{3,2},{4,5},{5,4},{6,7},{7,6},{8,9},{9,8},{10,11... | collective-permute-start | bytes 3538952 | tf_op jit(solution)/shard_map/ppermute | solution.py:479
  274.7 9.8 %collective-permute-start.34 = (f32[9,1536]{1,0:T(8,128)S(1)}, f32[9,1536]{1,0:T(8,128)S(1)}, u32[]{:S(2)}, u32[]{:S(2)}) collective-permute-start(f32[9,1536]{1,0:T(8,128)S(1)} %select_maximum_fusion), channel_id=1, source_target_pairs={{0,4},{4,0},{8,12},{12,8},{1,5},{5,1},{9,13},{13,9},{2,6},{6,2},{1... | collective-permute-start | bytes 165896 | tf_op jit(solution)/shard_map/ppermute | solution.py:479
  285.0 21.7 %collective-permute-start.35 = (bf16[192,1536]{1,0:T(8,128)(2,1)S(1)}, bf16[192,1536]{1,0:T(8,128)(2,1)S(1)}, u32[]{:S(2)}, u32[]{:S(2)}) collective-permute-start(bf16[192,1536]{1,0:T(8,128)(2,1)S(1)} %slice.264), channel_id=1, source_target_pairs={{0,2},{1,3},{2,0},{3,1},{4,6},{5,7},{6,4},{7,5},{8,10},{9,11},{10,... | collective-permute-start | bytes 1769480 | tf_op jit(solution)/shard_map/ppermute | solution.py:479
  289.4 16.3 %collective-permute-start.37 = (bf16[768,384]{1,0:T(8,128)(2,1)S(1)}, bf16[768,384]{1,0:T(8,128)(2,1)S(1)}, u32[]{:S(2)}, u32[]{:S(2)}) collective-permute-start(bf16[768,384]{1,0:T(8,128)(2,1)S(1)} %dynamic-slice_bitcast_fusion.1), channel_id=1, source_target_pairs={{0,16},{16,0},{1,17},{17,1},{2,18},{18,2},{3,19},{19,3},{4,20},{20... | collective-permute-start | bytes 1769480 | tf_op jit(solution)/shard_map/ppermute | solution.py:479
  291.0 30.0 %collective-permute-start.36 = (bf16[768,512]{1,0:T(8,128)(2,1)S(1)}, bf16[768,512]{1,0:T(8,128)(2,1)S(1)}, u32[]{:S(2)}, u32[]{:S(2)}) collective-permute-start(bf16[768,512]{1,0:T(8,128)(2,1)S(1)} %dynamic-slice_bitcast_fusion), channel_id=1, source_target_pairs={{0,16},{16,0},{1,17},{17,1},{2,18},{18,2},{3,19},{19,3},{4,20},{20... | collective-permute-start | bytes 2359304 | tf_op jit(solution)/shard_map/ppermute | solution.py:479
  293.1 9.6 %collective-permute-start.38 = (f32[9,1536]{1,0:T(8,128)S(1)}, f32[9,1536]{1,0:T(8,128)S(1)}, u32[]{:S(2)}, u32[]{:S(2)}) collective-permute-start(f32[9,1536]{1,0:T(8,128)S(1)} %fusion.57), channel_id=1, source_target_pairs={{0,8},{4,12},{8,0},{12,4},{1,9},{5,13},{9,1},{13,5},{2,10},{6,14},... | collective-permute-start | bytes 165896 | tf_op jit(solution)/shard_map/ppermute | solution.py:479
  322.1 7.5 %collective-permute-start.42 = (bf16[96,1536]{1,0:T(8,128)(2,1)S(1)}, bf16[96,1536]{1,0:T(8,128)(2,1)S(1)}, u32[]{:S(2)}, u32[]{:S(2)}) collective-permute-start(bf16[96,1536]{1,0:T(8,128)(2,1)S(1)} %slice.267), channel_id=1, source_target_pairs={{0,2},{1,3},{2,0},{3,1},{4,6},{5,7},{6,4},{7,5},{8,10},{9,11},{10,... | collective-permute-start | bytes 884744 | tf_op jit(solution)/shard_map/ppermute | solution.py:479
  323.0 7.4 %collective-permute-start.41 = (bf16[48,1536]{1,0:T(8,128)(2,1)S(1)}, bf16[48,1536]{1,0:T(8,128)(2,1)S(1)}, u32[]{:S(2)}, u32[]{:S(2)}) collective-permute-start(bf16[48,1536]{1,0:T(8,128)(2,1)S(1)} %get-tuple-element.161), channel_id=1, source_target_pairs={{0,12},{4,0},{8,4},{12,8},{1,13},{5,1},{9,5},{13,9},{2,14},{6,2},{... | collective-permute-start | bytes 442376 | tf_op jit(solution)/shard_map/ppermute | solution.py:717
  323.8 11.9 %collective-permute-start.40 = (bf16[48,1536]{1,0:T(8,128)(2,1)S(1)}, bf16[48,1536]{1,0:T(8,128)(2,1)S(1)}, u32[]{:S(2)}, u32[]{:S(2)}) collective-permute-start(bf16[48,1536]{1,0:T(8,128)(2,1)S(1)} %get-tuple-element.162), channel_id=1, source_target_pairs={{0,8},{4,12},{8,0},{12,4},{1,9},{5,13},{9,1},{13,5},{2,10},{6,14},... | collective-permute-start | bytes 442376 | tf_op jit(solution)/shard_map/ppermute | solution.py:717
  323.8 11.9 %collective-permute-start.39 = (bf16[48,1536]{1,0:T(8,128)(2,1)S(1)}, bf16[48,1536]{1,0:T(8,128)(2,1)S(1)}, u32[]{:S(2)}, u32[]{:S(2)}) collective-permute-start(bf16[48,1536]{1,0:T(8,128)(2,1)S(1)} %get-tuple-element.160), channel_id=1, source_target_pairs={{0,4},{4,8},{8,12},{12,0},{1,5},{5,9},{9,13},{13,1},{2,6},{6,10},{... | collective-permute-start | bytes 442376 | tf_op jit(solution)/shard_map/ppermute | solution.py:717
  342.3 35.1 %collective-permute-start.45 = (bf16[48,2,1536]{2,0,1:T(8,128)(2,1)S(1)}, bf16[48,2,1536]{2,0,1:T(8,128)(2,1)S(1)}, u32[]{:S(2)}, u32[]{:S(2)}) collective-permute-start(bf16[48,2,1536]{2,0,1:T(8,128)(2,1)S(1)} %pad_maximum_fusion.12), channel_id=1, source_target_pairs={{0,2},{1,3},{2,0},{3,1},{4,6},{5,7},{6,4},{7,5},{8,10},{9,11},{10,... | collective-permute-start | bytes 884744 | tf_op jit(solution)/shard_map/ppermute | solution.py:479
  343.9 29.3 %collective-permute-start.47 = (f32[2,1536]{1,0:T(2,128)S(1)}, f32[2,1536]{1,0:T(2,128)S(1)}, u32[]{:S(2)}, u32[]{:S(2)}) collective-permute-start(f32[2,1536]{1,0:T(2,128)S(1)} %slice.171), channel_id=1, source_target_pairs={{0,2},{1,3},{2,0},{3,1},{4,6},{5,7},{6,4},{7,5},{8,10},{9,11},{10,... | collective-permute-start | bytes 36872 | tf_op jit(solution)/shard_map/ppermute | solution.py:479
  344.4 40.3 %all-to-all-start.3 = ((bf16[4,192,384]{2,1,0:T(8,128)(2,1)}), bf16[4,192,384]{2,1,0:T(8,128)(2,1)S(1)}, u32[]{:S(2)}, u32[]{:S(2)}) async-start(bf16[4,192,384]{2,1,0:T(8,128)(2,1)} %bitcast.74), calls=%async_computation.5 | async-start | bytes 1179648 | tf_op jit(solution)/shard_map/all_to_all | solution.py:540
  348.2 30.3 %collective-permute-start.49 = (bf16[192,1024]{1,0:T(8,128)(2,1)S(1)}, bf16[192,1024]{1,0:T(8,128)(2,1)S(1)}, u32[]{:S(2)}, u32[]{:S(2)}) collective-permute-start(bf16[192,1024]{1,0:T(8,128)(2,1)S(1)} %dynamic-slice_bitcast_fusion.2), channel_id=1, source_target_pairs={{0,16},{16,0},{1,17},{17,1},{2,18},{18,2},{3,19},{19,3},{4,20},{20... | collective-permute-start | bytes 1179656 | tf_op jit(solution)/shard_map/ppermute | solution.py:479
  349.7 26.0 %collective-permute-start.50 = (bf16[192,512]{1,0:T(8,128)(2,1)S(1)}, bf16[192,512]{1,0:T(8,128)(2,1)S(1)}, u32[]{:S(2)}, u32[]{:S(2)}) collective-permute-start(bf16[192,512]{1,0:T(8,128)(2,1)S(1)} %dynamic-slice_bitcast_fusion.3), channel_id=1, source_target_pairs={{0,16},{16,0},{1,17},{17,1},{2,18},{18,2},{3,19},{19,3},{4,20},{20... | collective-permute-start | bytes 589832 | tf_op jit(solution)/shard_map/ppermute | solution.py:479
  350.4 7.2 %collective-permute-start.51 = (f32[1,5]{1,0:T(1,128)S(1)}, f32[1,5]{1,0:T(1,128)S(1)}, u32[]{:S(2)}, u32[]{:S(2)}) collective-permute-start(f32[1,5]{1,0:T(1,128)S(1)} %bitcast.275), channel_id=1, source_target_pairs={{0,4},{4,0},{8,12},{12,8},{1,5},{5,1},{9,13},{13,9},{2,6},{6,2},{1... | collective-permute-start | bytes 68 | tf_op jit(solution)/shard_map/ppermute | solution.py:479
  378.3 10.3 %collective-permute-start.46 = (bf16[96,2,1536]{2,0,1:T(8,128)(2,1)}, bf16[96,2,1536]{2,0,1:T(8,128)(2,1)}, u32[]{:S(2)}, u32[]{:S(2)}) collective-permute-start(bf16[96,2,1536]{2,0,1:T(8,128)(2,1)} %pad_maximum_fusion.7), channel_id=1, source_target_pairs={{0,1},{1,0},{2,3},{3,2},{4,5},{5,4},{6,7},{7,6},{8,9},{9,8},{10,11... | collective-permute-start | bytes 1769480 | tf_op jit(solution)/shard_map/ppermute | solution.py:479
  384.7 24.5 %all-to-all-start.2 = ((bf16[4,192,512]{2,1,0:T(8,128)(2,1)}), bf16[4,192,512]{2,1,0:T(8,128)(2,1)S(1)}, u32[]{:S(2)}, u32[]{:S(2)}) async-start(bf16[4,192,512]{2,1,0:T(8,128)(2,1)} %bitcast.71), calls=%async_computation.4 | async-start | bytes 1572864 | tf_op jit(solution)/shard_map/all_to_all | solution.py:540
  (64 other events, 510.3 us)
Sparse Core Ops, SparseCore 0:
  64.8 116.4 all-gather.1
  204.4 32.4 reduce-scatter.2
  239.2 63.2 reduce-scatter.4
